TPU v7x, 256 devices: a whole 4x4x8 slice. The times are simulated.
256 devices in a mesh: gx: 16 (over x, y), gy: 16 (over z, core).
Axes of the slice: x: 4, y: 4, z: 8, core: 2. Of those that a mesh axis runs over, the one named last changes fastest.
Arguments:
- source: float32 [256, 256, 128], P('gx', 'gy'), may hold values from -12 to 12
- dielectric: float32 [256, 256, 128], P('gx', 'gy'), may hold values from 0.2 to 4
- screening: float32 [256, 256, 128], P('gx', 'gy'), may hold values from 0.05 to 2
Outputs:
- solution: float32 [256, 256, 128], P('gx', 'gy')
All inputs are finite; a program needn't handle non-finite values.
Results may differ from a plain program's by a relative error of at most 0.0001.
Values sent between devices are 32-bit elements; how exact they have to be, the bound alone decides.
No kernel may reach another device: no remote copies, remote signals or barrier semaphores. Data moves between devices by JAX's collectives and lax.ppermute only.
A program may use at most 128 MiB of HBM per device.

v0:
```python
import jax
import jax.numpy as jnp
from jax import lax
from jax.sharding import PartitionSpec as P

LEVELS = 5
SWEEPS = 3
COARSE = 6


OMEGA = 0.8


def with_halo(cells, sides, width):
    for axis, dim in sides:
        count = lax.axis_size(axis)
        ends = count - 1
        head = lax.slice_in_dim(cells, 0, width, axis=dim)
        tail = lax.slice_in_dim(cells, cells.shape[dim] - width, cells.shape[dim], axis=dim)
        cells = jnp.concatenate(
            [
                lax.ppermute(tail, axis, [(i, (i + 1) % count) for i in range(ends)]),
                cells,
                lax.ppermute(head, axis, [((i + 1) % count, i) for i in range(ends)]),
            ],
            axis=dim,
        )
    return cells


def grid_rims(values):
    return with_halo(values, (("gx", 0), ("gy", 1)), 1)


def face_weights(padded, screening):
    centre = padded[1:-1, 1:-1]
    low_x = 0.5 * (padded[:-2, 1:-1] + centre)
    high_x = 0.5 * (padded[2:, 1:-1] + centre)
    low_y = 0.5 * (padded[1:-1, :-2] + centre)
    high_y = 0.5 * (padded[1:-1, 2:] + centre)
    z_padded = jnp.pad(centre, ((0, 0), (0, 0), (1, 1)))
    low_z = 0.5 * (z_padded[:, :, :-2] + centre)
    high_z = 0.5 * (z_padded[:, :, 2:] + centre)
    return jnp.stack([low_x, high_x, low_y, high_y, low_z, high_z, screening])


def diagonal(stencil):
    return stencil[0] + stencil[1] + stencil[2] + stencil[3] + stencil[4] + stencil[5] + stencil[6]


def operate(values, stencil, padder):
    padded = padder(values)
    z_padded = jnp.pad(values, ((0, 0), (0, 0), (1, 1)))
    beside = stencil[0] * padded[:-2, 1:-1] + stencil[1] * padded[2:, 1:-1]
    beside = beside + stencil[2] * padded[1:-1, :-2] + stencil[3] * padded[1:-1, 2:]
    beside = beside + stencil[4] * z_padded[:, :, :-2] + stencil[5] * z_padded[:, :, 2:]
    return diagonal(stencil) * values - beside


def jacobi_step(values, right_side, stencil, padder):
    return values + OMEGA * (right_side - operate(values, stencil, padder)) / diagonal(stencil)


def first_sweep(right_side, stencil):
    return OMEGA * right_side / diagonal(stencil)


def restrict(values):
    count_x, count_y, count_z = values.shape
    return values.reshape(count_x // 2, 2, count_y // 2, 2, count_z // 2, 2).sum(axis=(1, 3, 5))


def coarsen(stencil):
    count_c, count_x, count_y, count_z = stencil.shape
    blocks = stencil.reshape(count_c, count_x // 2, 2, count_y // 2, 2, count_z // 2, 2)
    low_x = blocks[0][:, 0].sum(axis=(2, 4))
    high_x = blocks[1][:, 1].sum(axis=(2, 4))
    low_y = blocks[2][:, :, :, 0].sum(axis=(1, 4))
    high_y = blocks[3][:, :, :, 1].sum(axis=(1, 4))
    low_z = blocks[4][:, :, :, :, :, 0].sum(axis=(1, 3))
    high_z = blocks[5][:, :, :, :, :, 1].sum(axis=(1, 3))
    screen = blocks[6].sum(axis=(1, 3, 5))
    return jnp.stack([low_x, high_x, low_y, high_y, low_z, high_z, screen])


def prolong(values):
    count_x, count_y, count_z = values.shape
    spread_out = jnp.broadcast_to(
        values[:, None, :, None, :, None], (count_x, 2, count_y, 2, count_z, 2)
    )
    return spread_out.reshape(2 * count_x, 2 * count_y, 2 * count_z)


def plain_down(right_side, stencil, padder):
    values = first_sweep(right_side, stencil)
    for _ in range(SWEEPS - 1):
        values = jacobi_step(values, right_side, stencil, padder)
    residual = right_side - operate(values, stencil, padder)
    return (values, residual)


def plain_up(values, right_side, stencil, padder):
    for _ in range(SWEEPS):
        values = jacobi_step(values, right_side, stencil, padder)
    return values


def descend(right_side, stencil, padder, count):
    stored = []
    for _ in range(count):
        widened = None
        values, residual = plain_down(right_side, stencil, padder)
        stored.append((values, right_side, stencil, widened))
        right_side = restrict(residual)
        stencil = coarsen(stencil)
    return (right_side, stencil, stored)


def bottom(right_side, stencil, padder):
    values = first_sweep(right_side, stencil)
    for _ in range(COARSE - 1):
        values = jacobi_step(values, right_side, stencil, padder)
    return values


def ascend(values, stored, padder):
    for fine_values, right_side, stencil, widened in reversed(stored):
        values = fine_values + prolong(values)
        values = plain_up(values, right_side, stencil, padder)
    return values


def local(source, dielectric, screening):
    padded = with_halo(dielectric, (("gx", 0), ("gy", 1)), 1)
    stencil = face_weights(padded, screening)
    coarse_side, coarse_stencil, stored = descend(source, stencil, grid_rims, LEVELS - 1)
    values = bottom(coarse_side, coarse_stencil, grid_rims)
    return ascend(values, stored, grid_rims)


def solution(mesh):
    placed = (P("gx", "gy", None), P("gx", "gy", None), P("gx", "gy", None))
    return jax.shard_map(
        local, mesh=mesh, in_specs=placed, out_specs=P("gx", "gy", None), check_vma=False
    )
```

profile of v0, /device:TPU:32, one launch (start us, length us, event | category | flops | bytes accessed | tf_op | source)
XLA Modules:
  0.0 645.1 jit_solution(9431521219959831834)
XLA Ops:
  15.5 10.5 %squeeze.112 = f32[8,2,8,2,64,2]{5,4,3,2,1,0:T(8,128)} reshape(f32[16,16,128]{2,1,0:T(8,128)} %param.5) | data formatting | bytes 262144 | tf_op jit(solution)/shard_map/squeeze | solution.py:82
  36.7 9.7 %squeeze.110 = f32[8,2,8,2,64,2]{5,4,3,2,1,0:T(8,128)} reshape(f32[16,16,128]{2,1,0:T(8,128)S(1)} %get-tuple-element.12) | data formatting | bytes 262144 | tf_op jit(solution)/shard_map/squeeze | solution.py:80
  46.4 9.8 %squeeze.111 = f32[8,2,8,2,64,2]{5,4,3,2,1,0:T(8,128)} reshape(f32[16,16,128]{2,1,0:T(8,128)S(1)} %get-tuple-element.13) | data formatting | bytes 262144 | tf_op jit(solution)/shard_map/squeeze | solution.py:81
  56.1 9.7 %squeeze.108 = f32[8,2,8,2,64,2]{5,4,3,2,1,0:T(8,128)} reshape(f32[16,16,128]{2,1,0:T(8,128)S(1)} %get-tuple-element.10) | data formatting | bytes 262144 | tf_op jit(solution)/shard_map/squeeze | solution.py:78
  65.8 9.8 %squeeze.109 = f32[8,2,8,2,64,2]{5,4,3,2,1,0:T(8,128)} reshape(f32[16,16,128]{2,1,0:T(8,128)S(1)} %get-tuple-element.11) | data formatting | bytes 262144 | tf_op jit(solution)/shard_map/squeeze | solution.py:79
  75.6 7.7 %slice_reduce_fusion = (f32[8,8,64]{2,1,0:T(8,128)S(1)}, f32[8,8,64]{2,1,0:T(8,128)S(1)}) fusion(f32[8,2,8,2,64,2]{5,4,3,2,1,0:T(8,128)} %squeeze.111, f32[8,2,8,2,64,2]{5,4,3,2,1,0:T(8,128)} %squeeze.110), kind=kLoop, calls=%fused_computation | loop fusion | flops 24576 | bytes 163840 | tf_op jit(solution)/shard_map/reduce_sum | solution.py:81
  87.3 9.7 %squeeze.106 = f32[8,2,8,2,64,2]{5,4,3,2,1,0:T(8,128)} reshape(f32[16,16,128]{2,1,0:T(8,128)S(1)} %get-tuple-element.9) | data formatting | bytes 262144 | tf_op jit(solution)/shard_map/squeeze | solution.py:76
  97.0 9.8 %squeeze.107 = f32[8,2,8,2,64,2]{5,4,3,2,1,0:T(8,128)} reshape(f32[16,16,128]{2,1,0:T(8,128)S(1)} %get-tuple-element.8) | data formatting | bytes 262144 | tf_op jit(solution)/shard_map/squeeze | solution.py:77
  112.4 4.6 slice_reduce_fusion.4
  118.3 4.8 collective-permute-start.8
  153.0 9.8 %reshape.240 = f32[8,2,8,2,64,2]{5,4,3,2,1,0:T(8,128)} reshape(f32[16,16,128]{2,1,0:T(8,128)S(1)} %fusion.26) | data formatting | bytes 262144 | tf_op jit(solution)/shard_map/reshape | solution.py:70
  166.8 6.0 collective-permute-start.16
  205.6 4.1 collective-permute-start.24
  224.6 4.1 collective-permute-start.28
  283.4 4.1 collective-permute-done.41
  336.6 4.1 collective-permute-done.53
  354.2 4.1 collective-permute-done.57
  389.5 4.1 collective-permute-done.65
  407.1 4.1 collective-permute-done.69
  424.9 4.2 collective-permute-done.73
  442.5 4.2 collective-permute-done.77
  460.2 4.2 collective-permute-done.81
  478.1 4.2 collective-permute-done.85
  495.8 4.2 collective-permute-done.89
  513.5 4.2 collective-permute-done.93
  532.1 4.2 collective-permute-done.97
  549.8 4.2 collective-permute-done.101
  567.6 4.2 collective-permute-done.105
  583.9 6.9 %reshape.245 = f32[16,16,128]{2,1,0:T(8,128)S(1)} reshape(f32[8,2,8,2,64,2]{5,4,3,2,1,0:T(8,128)} %broadcast_in_dim.36) | data formatting | bytes 262144 | tf_op jit(solution)/shard_map/reshape | solution.py:91
  596.2 4.2 collective-permute-done.109
  614.1 4.2 collective-permute-done.113
  632.0 4.2 collective-permute-done.117
  (395 shorter events, 455.6 us)
Async XLA Ops:
  9.8 21.7 %collective-permute-start.2 = (f32[18,1,128]{2,1,0:T(1,128)S(1)}, f32[18,1,128]{2,1,0:T(1,128)S(1)}, u32[]{:S(2)}, u32[]{:S(2)}) collective-permute-start(f32[18,1,128]{2,1,0:T(1,128)S(1)} %get-tuple-element.27), channel_id=1, source_target_pairs={{0,1},{1,2},{2,3},{3,4},{4,5},{5,6},{6,7},{7,8},{8,9},{9,10},{10,1... | collective-permute-start | bytes 27656 | tf_op jit(solution)/shard_map/ppermute | solution.py:22
  11.7 19.8 %collective-permute-start.3 = (f32[18,1,128]{2,1,0:T(1,128)S(1)}, f32[18,1,128]{2,1,0:T(1,128)S(1)}, u32[]{:S(2)}, u32[]{:S(2)}) collective-permute-start(f32[18,1,128]{2,1,0:T(1,128)S(1)} %get-tuple-element.26), channel_id=1, source_target_pairs={{1,0},{2,1},{3,2},{4,3},{5,4},{6,5},{7,6},{8,7},{9,8},{10,9},{11,1... | collective-permute-start | bytes 27656 | tf_op jit(solution)/shard_map/ppermute | solution.py:24
  31.7 75.1 %collective-permute-start.4 = (f32[1,16,128]{2,1,0:T(8,128)S(1)}, f32[1,16,128]{2,1,0:T(8,128)S(1)}, u32[]{:S(2)}, u32[]{:S(2)}) collective-permute-start(f32[1,16,128]{2,1,0:T(8,128)S(1)} %get-tuple-element.39), channel_id=1, source_target_pairs={{0,16},{16,32},{32,48},{48,64},{64,80},{80,96},{96,112},{112,128},... | collective-permute-start | bytes 24584 | tf_op jit(solution)/shard_map/ppermute | solution.py:22
  35.2 71.6 %collective-permute-start.5 = (f32[1,16,128]{2,1,0:T(8,128)S(1)}, f32[1,16,128]{2,1,0:T(8,128)S(1)}, u32[]{:S(2)}, u32[]{:S(2)}) collective-permute-start(f32[1,16,128]{2,1,0:T(8,128)S(1)} %get-tuple-element.40), channel_id=1, source_target_pairs={{16,0},{32,16},{48,32},{64,48},{80,64},{96,80},{112,96},{128,112},... | collective-permute-start | bytes 24584 | tf_op jit(solution)/shard_map/ppermute | solution.py:24
  106.8 11.3 %collective-permute-start.6 = (f32[18,1,128]{2,1,0:T(1,128)S(1)}, f32[18,1,128]{2,1,0:T(1,128)S(1)}, u32[]{:S(2)}, u32[]{:S(2)}) collective-permute-start(f32[18,1,128]{2,1,0:T(1,128)S(1)} %get-tuple-element.24), channel_id=1, source_target_pairs={{0,1},{1,2},{2,3},{3,4},{4,5},{5,6},{6,7},{7,8},{8,9},{9,10},{10,1... | collective-permute-start | bytes 27656 | tf_op jit(solution)/shard_map/ppermute | solution.py:22
  108.7 9.4 %collective-permute-start.7 = (f32[18,1,128]{2,1,0:T(1,128)S(1)}, f32[18,1,128]{2,1,0:T(1,128)S(1)}, u32[]{:S(2)}, u32[]{:S(2)}) collective-permute-start(f32[18,1,128]{2,1,0:T(1,128)S(1)} %get-tuple-element.25), channel_id=1, source_target_pairs={{1,0},{2,1},{3,2},{4,3},{5,4},{6,5},{7,6},{8,7},{9,8},{10,9},{11,1... | collective-permute-start | bytes 27656 | tf_op jit(solution)/shard_map/ppermute | solution.py:24
  118.3 7.6 %collective-permute-start.8 = (f32[1,16,128]{2,1,0:T(8,128)S(1)}, f32[1,16,128]{2,1,0:T(8,128)S(1)}, u32[]{:S(2)}, u32[]{:S(2)}) collective-permute-start(f32[1,16,128]{2,1,0:T(8,128)S(1)} %get-tuple-element.37), channel_id=1, source_target_pairs={{0,16},{16,32},{32,48},{48,64},{64,80},{80,96},{96,112},{112,128},... | collective-permute-start | bytes 24584 | tf_op jit(solution)/shard_map/ppermute | solution.py:22
  123.1 6.1 collective-permute-start.9
  129.2 6.8 %collective-permute-start.10 = (f32[18,1,128]{2,1,0:T(1,128)S(1)}, f32[18,1,128]{2,1,0:T(1,128)S(1)}, u32[]{:S(2)}, u32[]{:S(2)}) collective-permute-start(f32[18,1,128]{2,1,0:T(1,128)S(1)} %get-tuple-element.22), channel_id=1, source_target_pairs={{0,1},{1,2},{2,3},{3,4},{4,5},{5,6},{6,7},{7,8},{8,9},{9,10},{10,1... | collective-permute-start | bytes 27656 | tf_op jit(solution)/shard_map/ppermute | solution.py:22
  136.3 6.5 %collective-permute-start.12 = (f32[1,16,128]{2,1,0:T(8,128)S(1)}, f32[1,16,128]{2,1,0:T(8,128)S(1)}, u32[]{:S(2)}, u32[]{:S(2)}) collective-permute-start(f32[1,16,128]{2,1,0:T(8,128)S(1)} %get-tuple-element.35), channel_id=1, source_target_pairs={{0,16},{16,32},{32,48},{48,64},{64,80},{80,96},{96,112},{112,128},... | collective-permute-start | bytes 24584 | tf_op jit(solution)/shard_map/ppermute | solution.py:22
  140.2 5.7 collective-permute-start.13
  145.9 6.8 %collective-permute-start.14 = (f32[18,1,128]{2,1,0:T(1,128)S(1)}, f32[18,1,128]{2,1,0:T(1,128)S(1)}, u32[]{:S(2)}, u32[]{:S(2)}) collective-permute-start(f32[18,1,128]{2,1,0:T(1,128)S(1)} %get-tuple-element.20), channel_id=1, source_target_pairs={{0,1},{1,2},{2,3},{3,4},{4,5},{5,6},{6,7},{7,8},{8,9},{9,10},{10,1... | collective-permute-start | bytes 27656 | tf_op jit(solution)/shard_map/ppermute | solution.py:22
  166.8 8.6 %collective-permute-start.16 = (f32[1,8,64]{2,1,0:T(8,128)S(1)}, f32[1,8,64]{2,1,0:T(8,128)S(1)}, u32[]{:S(2)}, u32[]{:S(2)}) collective-permute-start(f32[1,8,64]{2,1,0:T(8,128)S(1)} %get-tuple-element.65), channel_id=1, source_target_pairs={{0,16},{16,32},{32,48},{48,64},{64,80},{80,96},{96,112},{112,128},... | collective-permute-start | bytes 6152 | tf_op jit(solution)/shard_map/ppermute | solution.py:22
  178.3 5.9 collective-permute-start.18
  181.1 6.6 %collective-permute-start.19 = (f32[10,1,64]{2,1,0:T(1,128)S(1)}, f32[10,1,64]{2,1,0:T(1,128)S(1)}, u32[]{:S(2)}, u32[]{:S(2)}) collective-permute-start(f32[10,1,64]{2,1,0:T(1,128)S(1)} %get-tuple-element.54), channel_id=1, source_target_pairs={{1,0},{2,1},{3,2},{4,3},{5,4},{6,5},{7,6},{8,7},{9,8},{10,9},{11,1... | collective-permute-start | bytes 7688 | tf_op jit(solution)/shard_map/ppermute | solution.py:24
  187.8 5.6 collective-permute-start.20
  197.3 5.8 collective-permute-start.22
  205.6 5.6 collective-permute-start.24
  215.2 5.8 collective-permute-start.26
  224.6 5.6 collective-permute-start.28
  234.2 5.8 collective-permute-start.30
  242.4 5.6 collective-permute-start.32
  251.9 5.8 collective-permute-start.34
  269.6 5.7 collective-permute-start.38
  287.5 5.8 collective-permute-start.42
  305.2 5.9 collective-permute-start.46
  322.9 6.0 collective-permute-start.50
  366.5 5.6 collective-permute-start.60
  429.0 5.6 collective-permute-start.74
  446.7 5.6 collective-permute-start.78
  536.3 5.6 collective-permute-start.98
  600.4 5.6 collective-permute-start.110
  (93 other events, 544.1 us)
where the time goes:
time: 658 us; the launch traced here: 645 us
  starting transfers between devices  329 us (50%)
  waiting for transfers between devices  180 us (27%)
  local copies, waits for them, and re-layouts  106 us (16%)
  other arithmetic  29.4 us (4%)
    ppermute x60, starting transfers between devices, with_halo(): lax.ppermute(tail, axis, [(i, (i + 1) % count) for i in range(ends)])  212 us
    ppermute x60, waiting for transfers between devices, with_halo(): lax.ppermute(head, axis, [((i + 1) % count, i) for i in range(ends)])  179 us
    ppermute x60, starting transfers between devices, with_halo(): lax.ppermute(head, axis, [((i + 1) % count, i) for i in range(ends)])  117 us
  transfers between devices with their start and end apart: 120, of which 57 were waited for; matrix products, arithmetic and copies ran while one was open for 15% of the time, Pallas kernels for 0%

commit v1 on v0

v1 whole, which is shorter than its diff:
```python
import jax
import jax.numpy as jnp
from jax import lax
from jax.experimental import pallas as pl
from jax.experimental.pallas import tpu as pltpu
from jax.sharding import PartitionSpec as P

OMEGA = 0.8
F32 = jnp.float32
LANES = 128


def roll(values, shift, dim):
    return pltpu.roll(values, shift % values.shape[dim], dim)


def lane_of(values):
    return lax.broadcasted_iota(jnp.int32, values.shape, values.ndim - 1)


def row_of(values):
    return lax.broadcasted_iota(jnp.int32, values.shape, values.ndim - 2)


def bit_of(values, bit):
    return ((lane_of(values) >> bit) & 1) == 1


def pair(values, bit):
    step, dim = 1 << bit, values.ndim - 1
    other = jnp.where(bit_of(values, bit), roll(values, step, dim), roll(values, -step, dim))
    return values + other


def keep(values, bit, want):
    step, dim = 1 << bit, values.ndim - 1
    if want:
        return jnp.where(bit_of(values, bit), values, roll(values, -step, dim))
    return jnp.where(bit_of(values, bit), roll(values, step, dim), values)


def spread(values, which, bits):
    for bit in range(bits):
        values = keep(values, bit, (which >> bit) & 1)
    return values


def relax_factor(diag):
    good = diag > 0.0
    return jnp.where(good, OMEGA / jnp.where(good, diag, 1.0), 0.0)


def loop(first, last, step, body):
    count = (last - first + 1) // step
    assert count * step == last - first + 1

    def run(index, carry):
        body(first + index * step)
        return carry

    lax.fori_loop(0, count, run, 0)


def beside(vals, faces, plane, count, level):
    fx, fy, fz = faces
    shift = 1 << level
    v = vals[pl.ds(plane, count)]
    y_face, z_face = fy[pl.ds(plane, count)], fz[pl.ds(plane, count)]
    total = fx[pl.ds(plane, count)] * vals[pl.ds(plane - 1, count)]
    total = total + fx[pl.ds(plane + 1, count)] * vals[pl.ds(plane + 1, count)]
    total = total + y_face * roll(v, 1, 1) + roll(y_face * v, -1, 1)
    total = total + z_face * roll(v, shift, 2) + roll(z_face * v, -shift, 2)
    return v, total


def sweep(out, vals, side, faces, weight, first, last, step, level):
    def body(plane):
        v, total = beside(vals, faces, plane, step, level)
        here = pl.ds(plane, step)
        out[here] = (1.0 - OMEGA) * v + weight[here] * (side[here] + total)

    loop(first, last, step, body)


def remains(out, vals, side, faces, diag, first, last, step, level):
    def body(plane):
        v, total = beside(vals, faces, plane, step, level)
        here = pl.ds(plane, step)
        out[here] = side[here] - diag[here] * v + total

    loop(first, last, step, body)


def block_sum(ref, plane, start, count):
    even, odd = pl.ds(start, count, stride=2), pl.ds(start + 1, count, stride=2)
    low = ref[plane, even, :] + ref[plane, odd, :]
    return low + (ref[plane + 1, even, :] + ref[plane + 1, odd, :])


def coarse_stencil(faces, diag, plane, start, count, level):
    fx, fy, fz = faces
    even, odd = pl.ds(start, count, stride=2), pl.ds(start + 1, count, stride=2)
    x_low = fx[plane, even, :] + fx[plane, odd, :]
    x_mid = fx[plane + 1, even, :] + fx[plane + 1, odd, :]
    y_low = fy[plane, even, :] + fy[plane + 1, even, :]
    y_mid = fy[plane, odd, :] + fy[plane + 1, odd, :]
    z_sum = block_sum(fz, plane, start, count)
    d_sum = block_sum(diag, plane, start, count)
    d_new = pair(d_sum - 2.0 * (x_mid + y_mid), level) - 2.0 * keep(z_sum, level, 1)
    return pair(x_low, level), pair(y_low, level), keep(z_sum, level, 0), d_new


def call(body, outs, scratch, limit, flops, *args):
    nbytes = sum(4 * a.size for a in args) + sum(4 * o.size for o in outs)
    return pl.pallas_call(
        body,
        out_shape=outs,
        in_specs=[pl.BlockSpec(memory_space=pltpu.VMEM)] * len(args),
        out_specs=[pl.BlockSpec(memory_space=pltpu.VMEM)] * len(outs),
        scratch_shapes=scratch,
        compiler_params=pltpu.CompilerParams(vmem_limit_bytes=limit << 20),
        cost_estimate=pl.CostEstimate(flops=flops, bytes_accessed=nbytes, transcendentals=0),
    )(*args)


def array(*shape):
    return jax.ShapeDtypeStruct(shape, F32)


def strips_kernel(eps, src, scr, xl, xr, up, down):
    at = 0
    for own, start, wide in ((eps, 0, 10), (src, 10, 9), (scr, 19, 9)):
        for part, low, count in ((xl, start, wide), (own, 0, 16), (xr, start, wide)):
            up[at : at + count] = part[low : low + count, 8:16]
            down[at : at + count] = part[low : low + count, 0:8]
            for k in range(count):
                tile, row = 104 + (at + k) // 4, 2 * ((at + k) % 4)
                up[tile, row : row + 2] = part[low + k, 6:8]
                down[tile, row : row + 2] = part[low + k, 8:10]
            at += count


def down_kernel(
    eps, src, scr, xl, xr, yl, yr,
    u0_out, fx0_out, fy0_out, fz0_out, w0_out, r0_out,
    fx1, fy1, fz1, w1, l1_own, l2_own, up, down,
    e, b, s, fx, fy, fz, w, d, ua, ub, b1, d1, va, vb,
):
    at = 0
    for ref, own, start, wide in ((e, eps, 0, 10), (b, src, 10, 9), (s, scr, 19, 9)):
        first = 10 - wide
        planes = 16 + 2 * wide
        ref[first:10, 16:32] = xl[start : start + wide]
        ref[10:26, 16:32] = own[...]
        ref[26 : 26 + wide, 16:32] = xr[start : start + wide]
        ref[first : first + planes, 8:16] = yl[at : at + planes]
        ref[first : first + planes, 32:40] = yr[at : at + planes]
        for k in range(planes):
            tile, row = 104 + (at + k) // 4, 2 * ((at + k) % 4)
            below, above = yl[tile], yr[tile]
            rows = row_of(below)
            ref[first + k, 0:8] = jnp.where(
                rows < 2, roll(above, -row, 0), jnp.where(rows >= 6, roll(below, 6 - row, 0), 0.0)
            )
        at += planes

    def stencil(plane):
        cells = e[pl.ds(plane - 1, 4)]
        centre = cells[1:3]
        x_face = 0.5 * (cells[0:3] + cells[1:4])
        y_face = 0.5 * (centre + roll(centre, 1, 1))
        lanes = lane_of(centre)
        z_face = jnp.where(lanes == 0, 0.0, 0.5 * (centre + roll(centre, 1, 2)))
        ends = jnp.where((lanes == 0) | (lanes == LANES - 1), 0.5 * centre, 0.0)
        here = pl.ds(plane, 2)
        screen = s[here]
        diag = x_face[0:2] + x_face[1:3] + y_face + roll(y_face, -1, 1)
        diag = diag + z_face + roll(z_face, -1, 2) + screen + ends
        diag = jnp.where(screen > 0.0, diag, 0.0)
        weight = relax_factor(diag)
        fx[pl.ds(plane, 3)] = x_face
        fy[here] = y_face
        fz[here] = z_face
        d[here] = diag
        w[here] = weight
        ua[here] = weight * b[here]

    loop(1, 34, 2, stencil)
    faces = (fx, fy, fz)
    sweep(ub, ua, b, faces, w, 2, 33, 2, 0)
    sweep(ua, ub, b, faces, w, 3, 32, 2, 0)
    remains(ub, ua, b, faces, d, 4, 31, 2, 0)
    u0_out[...] = ua[10:26, 16:32]

    def keep_window(plane):
        for out, ref in ((fx0_out, fx), (fy0_out, fy), (fz0_out, fz), (w0_out, w), (r0_out, ub)):
            out[plane, 8:24] = ref[plane + 7, 16:32]
            high, low = ref[plane + 7, 32:40], ref[plane + 7, 8:16]
            out[plane, 0:8] = jnp.where(row_of(high) < 4, high, low)

    loop(0, 21, 1, keep_window)

    def to_level1(plane):
        x_face, y_face, z_face, diag = coarse_stencil(faces, d, 2 * plane, 0, 20, 0)
        fx1[plane, 0:20] = x_face
        fy1[plane, 0:20] = y_face
        fz1[plane, 0:20] = z_face
        fy1[plane, 20:21] = y_face[0:1]
        d1[plane, 0:20] = diag
        w1[plane, 0:20] = relax_factor(diag)

    for ref in (fx1, fy1, fz1, w1, d1, b1):
        ref[:, 16:24] = jnp.zeros((18, 8, LANES), F32)
    loop(1, 16, 1, to_level1)
    even, odd = pl.ds(0, 20, stride=2), pl.ds(1, 20, stride=2)
    fx1[17, 0:20] = pair(fx[34, even, :] + fx[34, odd, :], 0)

    def side1(plane):
        side = pair(block_sum(ub, 2 * plane, 0, 20), 0)
        b1[plane, 0:20] = side
        va[plane, 0:20] = w1[plane, 0:20] * side

    loop(2, 15, 1, side1)
    va[:, 20:24] = jnp.zeros((18, 4, LANES), F32)
    faces1 = (fx1, fy1, fz1)
    sweep(vb, va, b1, faces1, w1, 3, 14, 4, 1)
    sweep(va, vb, b1, faces1, w1, 4, 13, 2, 1)
    remains(vb, va, b1, faces1, d1, 5, 12, 4, 1)

    own = jnp.where(bit_of(va[5:13, 8:16], 0), va[5:13, 8:16], vb[5:13, 8:16])
    l1_own[...] = own
    l2_own[2] = jnp.zeros((8, LANES), F32)
    packed = jnp.zeros((4, LANES), F32)
    quarter = lane_of(packed) & 3
    for k in range(4):
        parts = coarse_stencil(faces1, d1, 5 + 2 * k, 8, 4, 1)
        stack = parts[3]
        for q in range(3):
            stack = jnp.where(quarter == q, parts[q], stack)
        l2_own[k // 2, 4 * (k % 2) : 4 * (k % 2) + 4] = stack
        packed = jnp.where(quarter == k, pair(block_sum(vb, 5 + 2 * k, 8, 4), 1), packed)
    l2_own[2, 0:4] = packed
    up[0:3] = l2_own[...]
    down[0:3] = l2_own[...]
    for t in range(4):
        first, second = l1_own[2 * t], l1_own[2 * t + 1]
        low = row_of(first) < 4
        up[3 + t] = jnp.where(low, roll(first, -4, 0), second)
        down[3 + t] = jnp.where(low, first, roll(second, 4, 0))


def window_kernel(l2_own, l1_own, a1u, a1d, a2u, a2d, main, up, down, l1_ext):
    low = lax.broadcasted_iota(jnp.int32, (8, LANES), 0) < 4
    for k in range(5):
        t, turn = k // 2, 4 * (k % 2)
        main[3 * k] = jnp.where(low, roll(a2u[t], -turn, 0), roll(a1u[t], 4 - turn, 0))
        main[3 * k + 1] = jnp.where(low, roll(l2_own[t], -turn, 0), roll(a1d[t], 4 - turn, 0))
        main[3 * k + 2] = jnp.where(low, roll(a2d[t], -turn, 0), 0.0)
    for k in range(8):
        t, turn = 3 + k // 2, 4 * (k % 2)
        l1_ext[2 * k] = jnp.where(low, roll(a1d[t], -turn, 0), roll(a1u[t], 4 - turn, 0))
        l1_ext[2 * k + 1] = l1_own[k]
    up[0:15] = main[...]
    down[0:15] = main[...]
    up[15:23] = l1_ext[8:16]
    down[15:23] = l1_ext[0:8]


def level2_kernel(
    main, c1u, c1d, c2u, c2d,
    fx, fy, fz, w, r, u, payload,
    d, b, ua, ub, coarse,
):
    for group, part in enumerate((c2u, c1u, main, c1d, c2d)):
        sides = jnp.concatenate([part[12], part[13], part[14]], axis=0)
        for k in range(4):
            plane = 4 * group + k
            tiles = jnp.concatenate([part[3 * k], part[3 * k + 1], part[3 * k + 2]], axis=0)
            fx[plane] = spread(tiles, 0, 2)
            fy[plane] = spread(tiles, 1, 2)
            fz[plane] = spread(tiles, 2, 2)
            diag = spread(tiles, 3, 2)
            side = spread(sides, k, 2)
            weight = relax_factor(diag)
            d[plane] = diag
            b[plane] = side
            w[plane] = weight
            ua[plane] = weight * side
    faces = (fx, fy, fz)
    sweep(ub, ua, b, faces, w, 1, 18, 3, 2)
    sweep(u, ub, b, faces, w, 2, 17, 4, 2)
    remains(r, u, b, faces, d, 3, 16, 2, 2)

    gx, gy = lax.axis_index("gx"), lax.axis_index("gy")
    x_odd, y_odd = lax.rem(gx, 2), lax.rem(gy, 2)
    for plane in range(2, 8):
        parts = coarse_stencil(faces, d, 2 * plane, 0, 8, 2)
        side = pair(block_sum(r, 2 * plane, 0, 8), 2)
        rows = row_of(side)
        x_face = jnp.where(2 * gx + plane - 4 == 0, 0.0, parts[0])
        y_face = jnp.where(2 * gy + rows - 4 == 0, 0.0, parts[1])
        for index, values in enumerate((x_face, y_face, parts[2], parts[3], side)):
            coarse[index, plane] = jnp.where(y_odd == 1, roll(values, -2, 0), roll(values, -4, 0))
    x_start = 4 - 2 * x_odd
    rows = lax.broadcasted_iota(jnp.int32, (8, LANES), 0)
    slot = lax.broadcasted_iota(jnp.int32, (8, LANES), 1) & 7
    for index in range(5):
        for lead in range(2):
            total = jnp.where(slot == 2 * rows, coarse[index, x_start + lead], 0.0)
            total = total + jnp.where(slot == 2 * rows + 1, coarse[index, x_start + 2 + lead], 0.0)
            line = jnp.sum(total, axis=0, keepdims=True)
            payload[pl.ds(2 * index + lead, 64, stride=10), :] = jnp.broadcast_to(line, (64, LANES))


def level3_beside(v0, v1, faces):
    (x0, x1), (y0, y1), (z0, z1) = faces
    x_bit = bit_of(v0, 0)
    quarter = (lane_of(v0) >> 1) & 3
    from_low = jnp.where(x_bit, roll(v1, 1, 1), roll(roll(v1, -1, 1), 8, 0))
    product = x0 * v0
    from_high = jnp.where(x_bit, roll(roll(product, 1, 1), -8, 0), roll(product, -1, 1))
    totals = [x0 * from_low + x1 * v1, x1 * v0 + from_high]
    for lead, (v, y_face, z_face) in enumerate(((v0, y0, z0), (v1, y1, z1))):
        low = jnp.where(quarter == 0, roll(roll(v, -6, 1), 1, 0), roll(v, 2, 1))
        product = y_face * v
        high = jnp.where(quarter == 3, roll(roll(product, 6, 1), -1, 0), roll(product, -2, 1))
        totals[lead] = totals[lead] + y_face * low + high
        totals[lead] = totals[lead] + z_face * roll(v, 8, 1) + roll(z_face * v, -8, 1)
    return totals


def level4_beside(v, x_face, y_face, z_face):
    x_bit, y_bit = bit_of(v, 0), bit_of(v, 2)
    low = jnp.where(x_bit, roll(v, 1, 1), roll(roll(v, -1, 1), 8, 0))
    product = x_face * v
    high = jnp.where(x_bit, roll(roll(product, 1, 1), -8, 0), roll(product, -1, 1))
    total = x_face * low + high
    low = jnp.where(y_bit, roll(v, 4, 1), roll(roll(v, -4, 1), 1, 0))
    product = y_face * v
    high = jnp.where(y_bit, roll(roll(product, 4, 1), -1, 0), roll(product, -4, 1))
    total = total + y_face * low + high
    return total + z_face * roll(v, 16, 1) + roll(z_face * v, -16, 1)


def coarse_levels(got):
    lines = [[got[pl.ds(2 * index + lead, 64, stride=10), :] for lead in range(2)] for index in range(5)]
    faces, diag, side = lines[0:3], lines[3], lines[4]
    weight = [relax_factor(d) for d in diag]

    def sweep3(v, side):
        total = level3_beside(v[0], v[1], faces)
        return [(1.0 - OMEGA) * v[k] + weight[k] * (side[k] + total[k]) for k in range(2)]

    u = [weight[k] * side[k] for k in range(2)]
    u = sweep3(u, side)
    u = sweep3(u, side)
    total = level3_beside(u[0], u[1], faces)
    r = [side[k] - diag[k] * u[k] + total[k] for k in range(2)]

    (x0, x1), (y0, y1), (z0, z1) = faces
    y_sum, z_sum = pair(y0 + y1, 3), pair(z0 + z1, 1)
    x4, y4, z4 = pair(pair(x0, 1), 3), keep(y_sum, 1, 0), keep(z_sum, 3, 0)
    inner = pair(pair(x1, 1), 3) + keep(y_sum, 1, 1) + keep(z_sum, 3, 1)
    w4 = relax_factor(pair(pair(diag[0] + diag[1], 1), 3) - 2.0 * inner)
    b4 = pair(pair(r[0] + r[1], 1), 3)
    v = w4 * b4
    for _ in range(5):
        v = (1.0 - OMEGA) * v + w4 * (b4 + level4_beside(v, x4, y4, z4))

    c = [v, v]
    for _ in range(3):
        c = sweep3(c, r)
    return [u[k] + c[k] for k in range(2)]


def up_kernel(
    got, u0, fx0, fy0, fz0, w0, r0,
    fx1, fy1, fz1, w1, l1_ext, c1u, c1d,
    fx2, fy2, fz2, w2, r2, u2,
    out,
    u3, e3, ea2, eb2, r1, u1, ea1, eb1, ea0, eb0,
):
    gx, gy = lax.axis_index("gx"), lax.axis_index("gy")
    x_odd, y_odd = lax.rem(gx, 2), lax.rem(gy, 2)
    solved = coarse_levels(got)
    for lead in range(2):
        u3[lead, 16:80] = solved[lead]
    corner = 16 + 8 * (lax.div(gx, 2) - 1) + lax.div(gy, 2) - 1
    for lead in range(2):
        for a in range(3):
            three = u3[lead, pl.ds(corner + 8 * a, 8), :]
            for q in range(8):
                values = spread(three, q, 3)
                e3[4 * a + 2 * (q % 2) + lead, pl.ds(q // 2, 3, stride=4), :] = values[0:3]

    def start2(plane):
        values = e3[2 * x_odd + plane]
        values = jnp.where(y_odd == 1, roll(values, -2, 0), values)[0:12]
        for k in range(2):
            ea2[2 * plane + k, pl.ds(0, 12, stride=2), :] = values
            ea2[2 * plane + k, pl.ds(1, 12, stride=2), :] = values

    loop(1, 8, 1, start2)

    def inside(values, weight, first, last, step):
        def body(plane):
            here = pl.ds(plane, step)
            values[here] = jnp.where(weight[here] > 0.0, values[here], 0.0)

        loop(first, last, step, body)

    inside(ea2, w2, 2, 17, 4)
    faces = (fx2, fy2, fz2)
    sweep(eb2, ea2, r2, faces, w2, 3, 16, 2, 2)
    sweep(ea2, eb2, r2, faces, w2, 4, 15, 4, 2)
    sweep(eb2, ea2, r2, faces, w2, 5, 14, 2, 2)

    for part, first, tile, count in ((c1u, 1, 15, 4), (l1_ext, 5, 0, 8), (c1d, 13, 15, 4)):
        for k in range(count):
            sides, own = part[tile + 2 * k], part[tile + 2 * k + 1]
            for ref, which in ((r1, 0), (u1, 1)):
                edge = keep(sides, 0, which)
                ref[first + k, 0:8] = edge
                ref[first + k, 8:16] = keep(own, 0, which)
                ref[first + k, 16:24] = edge

    def start1(plane):
        values = (u2[plane] + eb2[plane])[5:15]
        return values

    for plane in range(5, 15):
        values = start1(plane)
        for k in range(2):
            target = 5 + 2 * (plane - 8) + k
            if 0 <= target < 18:
                ea1[target, pl.ds(2, 10, stride=2), :] = values
                ea1[target, pl.ds(3, 10, stride=2), :] = values
    inside(ea1, w1, 1, 16, 4)
    faces = (fx1, fy1, fz1)
    for plane in (0, 17):
        ea1[plane] = jnp.where(edge_inside(gx, plane), ea1[plane], 0.0)
    sweep(eb1, ea1, r1, faces, w1, 1, 16, 4, 1)
    sweep(ea1, eb1, r1, faces, w1, 2, 15, 2, 1)
    sweep(eb1, ea1, r1, faces, w1, 3, 14, 4, 1)

    for plane in range(3, 15):
        values = u1[plane] + eb1[plane]
        for k in range(2):
            target = 3 + 2 * (plane - 5) + k
            if 0 <= target < 22:
                for parity in range(2):
                    ea0[target, pl.ds(4 + parity, 10, stride=2), :] = values[6:16]
                    ea0[target, pl.ds(parity, 2, stride=2), :] = values[16:18]
    inside(ea0, w0, 0, 21, 2)
    faces = (fx0, fy0, fz0)
    sweep(eb0, ea0, r0, faces, w0, 1, 20, 2, 0)
    sweep(ea0, eb0, r0, faces, w0, 2, 19, 2, 0)

    def last(plane):
        v, total = beside(ea0, faces, plane, 2, 0)
        here = pl.ds(plane, 2)
        values = (1.0 - OMEGA) * v + w0[here] * (r0[here] + total)
        out[pl.ds(plane - 3, 2)] = u0[pl.ds(plane - 3, 2)] + values[:, 8:24]

    loop(3, 18, 2, last)


def edge_inside(gx, plane):
    where = 8 * gx + plane - 5
    return (where >= 0) & (where < 8 * lax.axis_size("gx"))


def shifted(values, axis, step):
    count = lax.axis_size(axis)
    pairs = [(k, k + step) for k in range(count) if 0 <= k + step < count]
    return lax.ppermute(values, axis, pairs)


def local(source, dielectric, screening):
    fields = (dielectric, source, screening)
    last = jnp.concatenate([dielectric[6:], source[7:], screening[7:]], axis=0)
    first = jnp.concatenate([dielectric[:10], source[:9], screening[:9]], axis=0)
    xl, xr = shifted(last, "gx", 1), shifted(first, "gx", -1)
    up, down = call(strips_kernel, [array(130, 8, LANES)] * 2, [], 16, 10_000, *fields, xl, xr)
    yl, yr = shifted(up, "gy", 1), shifted(down, "gy", -1)

    big, mid = pltpu.VMEM((36, 40, LANES), F32), pltpu.VMEM((18, 24, LANES), F32)
    outs = [array(16, 16, LANES)] + [array(22, 24, LANES)] * 5 + [array(18, 24, LANES)] * 4
    outs += [array(8, 8, LANES), array(3, 8, LANES), array(7, 8, LANES), array(7, 8, LANES)]
    made = call(down_kernel, outs, [big] * 10 + [mid] * 4, 24, 10_000_000, *fields, xl, xr, yl, yr)
    fine, level1, (l1_own, l2_own, up, down) = made[0:6], made[6:10], made[10:14]

    a1u, a1d = shifted(up, "gy", 1), shifted(down, "gy", -1)
    a2u, a2d = shifted(l2_own, "gy", 2), shifted(l2_own, "gy", -2)
    outs = [array(15, 8, LANES), array(23, 8, LANES), array(23, 8, LANES), array(16, 8, LANES)]
    main, up, down, l1_ext = call(window_kernel, outs, [], 16, 10_000, l2_own, l1_own, a1u, a1d, a2u, a2d)
    c1u, c1d = shifted(up, "gx", 1), shifted(down, "gx", -1)
    c2u, c2d = shifted(main, "gx", 2), shifted(main, "gx", -2)

    two = pltpu.VMEM((20, 24, LANES), F32)
    outs = [array(20, 24, LANES)] * 6 + [array(640, LANES)]
    scratch = [two] * 4 + [pltpu.VMEM((5, 10, 8, LANES), F32)]
    *level2, payload = call(level2_kernel, outs, scratch, 16, 5_000_000, main, c1u, c1d, c2u, c2d)

    n_x, n_y = lax.axis_size("gx"), lax.axis_size("gy")
    groups = [
        [(2 * a + p) * n_y + 2 * b + q for a in range(n_x // 2) for b in range(n_y // 2)]
        for p in range(2)
        for q in range(2)
    ]
    got = lax.all_to_all(payload, ("gx", "gy"), 0, 0, tiled=True, axis_index_groups=groups)

    scratch = [pltpu.VMEM((2, 96, LANES), F32), pltpu.VMEM((12, 16, LANES), F32)]
    scratch += [two] * 2 + [mid] * 4 + [pltpu.VMEM((22, 24, LANES), F32)] * 2
    (result,) = call(
        up_kernel, [array(16, 16, LANES)], scratch, 24, 10_000_000,
        got, *fine, *level1, l1_ext, c1u, c1d, *level2,
    )
    return result


def solution(mesh):
    spec = P("gx", "gy", None)
    return jax.shard_map(local, mesh=mesh, in_specs=(spec,) * 3, out_specs=spec, check_vma=False)
```

time: 658 us -> 126 us (0.19); the launches traced: 645 us -> 125 us
  starting transfers between devices: 329 us -> 36.1 us
  waiting for transfers between devices: 180 us -> 17.9 us
  local copies, waits for them, and re-layouts: 106 us -> 8.08 us
  blocking collectives: 0 us -> 38.1 us
  other arithmetic: 29.4 us -> 0.04 us
  Pallas kernels: 0 us -> 24.4 us
    ppermute x120 -> x12, starting transfers between devices: 329 us -> 36.1 us  [shifted(): return lax.ppermute(values, axis, pairs)]
    ppermute x120 -> x12, waiting for transfers between devices: 180 us -> 17.9 us  [shifted(): return lax.ppermute(values, axis, pairs)]
    squeeze x27 -> x0, local copies, waits for them, and re-layouts: 77.6 us -> none  [the longest x3 11.7 us: coarsen(): screen = blocks[6].sum(axis=(1, 3, 5))]
    all_to_all x0 -> x1, blocking collectives: none -> 38.1 us  [local(): lax.all_to_all(payload, ('gx', 'gy'), 0, 0, tiled=True, axis_index_groups...]
    reduce_sum x33 -> x0, other arithmetic: 25.4 us -> none  [the longest x4 8.54 us: coarsen(): high_z = blocks[5][:, :, :, :, :, 1].sum(axis=(1, 3))]
    pallas_call x0 -> x5, Pallas kernels: none -> 24.4 us  [call(): pl.pallas_call(body, out_shape=outs, in_specs=[pl.BlockSpec(memory_space=...]
    reshape x6 -> x0, local copies, waits for them, and re-layouts: 18.6 us -> none  [the longest x3 11 us: restrict(): values.reshape(count_x // 2, 2, count_y // 2, 2, count_z // 2, 2)]
  transfers between devices with their start and end apart: 120 -> 12, of which waited for: 57 -> 7; matrix products, arithmetic and copies ran while one was open for 15% -> 0% of each run, Pallas kernels for 0% -> 0%
where the time goes in v1:
time: 126 us; the launch traced here: 125 us
  blocking collectives  38.1 us (30%)
  starting transfers between devices  36.1 us (29%)
  Pallas kernels  24.4 us (19%)
  waiting for transfers between devices  17.9 us (14%)
  local copies, waits for them, and re-layouts  8.08 us (6%)
    all_to_all x1, blocking collectives, local(): lax.all_to_all(payload, ('gx', 'gy'), 0, 0, tiled=True, axis_index_groups...  38.1 us
    ppermute x12, starting transfers between devices, shifted(): return lax.ppermute(values, axis, pairs)  36.1 us
    pallas_call x5, Pallas kernels, call(): pl.pallas_call(body, out_shape=outs, in_specs=[pl.BlockSpec(memory_space=...  24.4 us
    ppermute x12, waiting for transfers between devices, shifted(): return lax.ppermute(values, axis, pairs)  17.9 us
    unnamed x22, local copies, waits for them, and re-layouts  5.15 us
  transfers between devices with their start and end apart: 12, of which 7 were waited for; matrix products, arithmetic and copies ran while one was open for 0% of the time, Pallas kernels for 0%

profile of v1, /device:TPU:32, one launch (start us, length us, event | category | flops | bytes accessed | tf_op | source)
XLA Modules:
  0.0 124.9 jit_solution(16432745989569992979)
XLA Ops:
  0.0 1.0 fusion
  1.1 3.5 %collective-permute-start = (f32[28,16,128]{2,1,0:T(8,128)S(1)}, f32[28,16,128]{2,1,0:T(8,128)S(1)}, u32[]{:S(2)}, u32[]{:S(2)}) collective-permute-start(f32[28,16,128]{2,1,0:T(8,128)S(1)} %pad_maximum_fusion), channel_id=1, source_target_pairs={{0,16},{16,32},{32,48},{48,64},{64,80},{80,96},{96,112},{112,128},... | collective-permute-start | bytes 688136 | tf_op jit(solution)/shard_map/ppermute | solution.py:476
  4.6 1.4 %collective-permute-start.1 = (f32[28,16,128]{2,1,0:T(8,128)S(1)}, f32[28,16,128]{2,1,0:T(8,128)S(1)}, u32[]{:S(2)}, u32[]{:S(2)}) collective-permute-start(f32[28,16,128]{2,1,0:T(8,128)S(1)} %pad_maximum_fusion.1), channel_id=1, source_target_pairs={{16,0},{32,16},{48,32},{64,48},{80,64},{96,80},{112,96},{128,112},... | collective-permute-start | bytes 688136 | tf_op jit(solution)/shard_map/ppermute | solution.py:476
  6.1 3.4 %collective-permute-done.xl = f32[28,16,128]{2,1,0:T(8,128)S(1)} collective-permute-done((f32[28,16,128]{2,1,0:T(8,128)S(1)}, f32[28,16,128]{2,1,0:T(8,128)S(1)}, u32[]{:S(2)}, u32[]{:S(2)}) %collective-permute-start) | collective-permute-done | bytes 229408 | tf_op jit(solution)/shard_map/ppermute | solution.py:476
  9.4 4.3 %collective-permute-done.1.xr = f32[28,16,128]{2,1,0:T(8,128)S(1)} collective-permute-done((f32[28,16,128]{2,1,0:T(8,128)S(1)}, f32[28,16,128]{2,1,0:T(8,128)S(1)}, u32[]{:S(2)}, u32[]{:S(2)}) %collective-permute-start.1) | collective-permute-done | bytes 229408 | tf_op jit(solution)/shard_map/ppermute | solution.py:476
  13.9 1.9 %collective-permute-start.2 = (f32[130,8,128]{2,1,0:T(8,128)S(1)}, f32[130,8,128]{2,1,0:T(8,128)S(1)}, u32[]{:S(2)}, u32[]{:S(2)}) collective-permute-start(f32[130,8,128]{2,1,0:T(8,128)S(1)} %get-tuple-element.32), channel_id=1, source_target_pairs={{0,1},{1,2},{2,3},{3,4},{4,5},{5,6},{6,7},{7,8},{8,9},{9,10},{10,1... | collective-permute-start | bytes 1597448 | tf_op jit(solution)/shard_map/ppermute | solution.py:476
  15.8 3.6 %collective-permute-start.3 = (f32[130,8,128]{2,1,0:T(8,128)S(1)}, f32[130,8,128]{2,1,0:T(8,128)S(1)}, u32[]{:S(2)}, u32[]{:S(2)}) collective-permute-start(f32[130,8,128]{2,1,0:T(8,128)S(1)} %get-tuple-element.33), channel_id=1, source_target_pairs={{1,0},{2,1},{3,2},{4,3},{5,4},{6,5},{7,6},{8,7},{9,8},{10,9},{11,1... | collective-permute-start | bytes 1597448 | tf_op jit(solution)/shard_map/ppermute | solution.py:476
  19.4 5.0 %collective-permute-done.2.yl = f32[130,8,128]{2,1,0:T(8,128)S(1)} collective-permute-done((f32[130,8,128]{2,1,0:T(8,128)S(1)}, f32[130,8,128]{2,1,0:T(8,128)S(1)}, u32[]{:S(2)}, u32[]{:S(2)}) %collective-permute-start.2) | collective-permute-done | bytes 532512 | tf_op jit(solution)/shard_map/ppermute | solution.py:476
  24.4 1.8 %collective-permute-done.3.yr = f32[130,8,128]{2,1,0:T(8,128)S(1)} collective-permute-done((f32[130,8,128]{2,1,0:T(8,128)S(1)}, f32[130,8,128]{2,1,0:T(8,128)S(1)}, u32[]{:S(2)}, u32[]{:S(2)}) %collective-permute-start.3) | collective-permute-done | bytes 532512 | tf_op jit(solution)/shard_map/ppermute | solution.py:476
  26.2 11.1 %shard_map.38 = (f32[16,16,128]{2,1,0:T(8,128)S(1)}, f32[22,24,128]{2,1,0:T(8,128)S(1)}, f32[22,24,128]{2,1,0:T(8,128)S(1)}, f32[22,24,128]{2,1,0:T(8,128)S(1)},...) custom-call(f32[16,16,128]{2,1,0:T(8,128)S(1)} %copy-done, ...), custom_call_target="tpu_custom_call" | custom-call | flops 10000000 | bytes 4386816 | tf_op jit(solution)/shard_map/pallas_call | solution.py:115
  37.3 0.7 copy-done.7
  38.0 0.7 copy-done.9
  38.7 4.1 %collective-permute-start.4 = (f32[7,8,128]{2,1,0:T(8,128)S(1)}, f32[7,8,128]{2,1,0:T(8,128)S(1)}, u32[]{:S(2)}, u32[]{:S(2)}) collective-permute-start(f32[7,8,128]{2,1,0:T(8,128)S(1)} %get-tuple-element.36), channel_id=1, source_target_pairs={{0,1},{1,2},{2,3},{3,4},{4,5},{5,6},{6,7},{7,8},{8,9},{9,10},{10,1... | collective-permute-start | bytes 86024 | tf_op jit(solution)/shard_map/ppermute | solution.py:476
  42.8 1.9 %collective-permute-start.5 = (f32[7,8,128]{2,1,0:T(8,128)S(1)}, f32[7,8,128]{2,1,0:T(8,128)S(1)}, u32[]{:S(2)}, u32[]{:S(2)}) collective-permute-start(f32[7,8,128]{2,1,0:T(8,128)S(1)} %get-tuple-element.37), channel_id=1, source_target_pairs={{1,0},{2,1},{3,2},{4,3},{5,4},{6,5},{7,6},{8,7},{9,8},{10,9},{11,1... | collective-permute-start | bytes 86024 | tf_op jit(solution)/shard_map/ppermute | solution.py:476
  44.7 1.9 %collective-permute-start.7 = (f32[3,8,128]{2,1,0:T(8,128)S(1)}, f32[3,8,128]{2,1,0:T(8,128)S(1)}, u32[]{:S(2)}, u32[]{:S(2)}) collective-permute-start(f32[3,8,128]{2,1,0:T(8,128)S(1)} %get-tuple-element.34.l2_own), channel_id=1, source_target_pairs={{2,0},{3,1},{4,2},{5,3},{6,4},{7,5},{8,6},{9,7},{10,8},{11,9},{12,... | collective-permute-start | bytes 36872 | tf_op jit(solution)/shard_map/ppermute | solution.py:476
  46.7 3.9 %collective-permute-start.6 = (f32[3,8,128]{2,1,0:T(8,128)S(1)}, f32[3,8,128]{2,1,0:T(8,128)S(1)}, u32[]{:S(2)}, u32[]{:S(2)}) collective-permute-start(f32[3,8,128]{2,1,0:T(8,128)S(1)} %get-tuple-element.34.l2_own), channel_id=1, source_target_pairs={{0,2},{1,3},{2,4},{3,5},{4,6},{5,7},{6,8},{7,9},{8,10},{9,11},{10,... | collective-permute-start | bytes 36872 | tf_op jit(solution)/shard_map/ppermute | solution.py:476
  50.6 1.6 %collective-permute-done.6.a2u = f32[3,8,128]{2,1,0:T(8,128)S(1)} collective-permute-done((f32[3,8,128]{2,1,0:T(8,128)S(1)}, f32[3,8,128]{2,1,0:T(8,128)S(1)}, u32[]{:S(2)}, u32[]{:S(2)}) %collective-permute-start.6) | collective-permute-done | bytes 12320 | tf_op jit(solution)/shard_map/ppermute | solution.py:476
  52.3 3.5 %collective-permute-start.8 = (f32[23,8,128]{2,1,0:T(8,128)S(1)}, f32[23,8,128]{2,1,0:T(8,128)S(1)}, u32[]{:S(2)}, u32[]{:S(2)}) collective-permute-start(f32[23,8,128]{2,1,0:T(8,128)S(1)} %get-tuple-element.39), channel_id=1, source_target_pairs={{0,16},{16,32},{32,48},{48,64},{64,80},{80,96},{96,112},{112,128},... | collective-permute-start | bytes 282632 | tf_op jit(solution)/shard_map/ppermute | solution.py:476
  55.8 1.3 %collective-permute-start.9 = (f32[23,8,128]{2,1,0:T(8,128)S(1)}, f32[23,8,128]{2,1,0:T(8,128)S(1)}, u32[]{:S(2)}, u32[]{:S(2)}) collective-permute-start(f32[23,8,128]{2,1,0:T(8,128)S(1)} %get-tuple-element.40), channel_id=1, source_target_pairs={{16,0},{32,16},{48,32},{64,48},{80,64},{96,80},{112,96},{128,112},... | collective-permute-start | bytes 282632 | tf_op jit(solution)/shard_map/ppermute | solution.py:476
  57.1 1.3 %collective-permute-start.11 = (f32[15,8,128]{2,1,0:T(8,128)S(1)}, f32[15,8,128]{2,1,0:T(8,128)S(1)}, u32[]{:S(2)}, u32[]{:S(2)}) collective-permute-start(f32[15,8,128]{2,1,0:T(8,128)S(1)} %get-tuple-element.38.main), channel_id=1, source_target_pairs={{32,0},{48,16},{64,32},{80,48},{96,64},{112,80},{128,96},{144,112}... | collective-permute-start | bytes 184328 | tf_op jit(solution)/shard_map/ppermute | solution.py:476
  58.4 7.7 %collective-permute-start.10 = (f32[15,8,128]{2,1,0:T(8,128)S(1)}, f32[15,8,128]{2,1,0:T(8,128)S(1)}, u32[]{:S(2)}, u32[]{:S(2)}) collective-permute-start(f32[15,8,128]{2,1,0:T(8,128)S(1)} %get-tuple-element.38.main), channel_id=1, source_target_pairs={{0,32},{16,48},{32,64},{48,80},{64,96},{80,112},{96,128},{112,144}... | collective-permute-start | bytes 184328 | tf_op jit(solution)/shard_map/ppermute | solution.py:476
  66.1 0.3 collective-permute-done.11.c2d
  66.4 1.6 %collective-permute-done.10.c2u = f32[15,8,128]{2,1,0:T(8,128)S(1)} collective-permute-done((f32[15,8,128]{2,1,0:T(8,128)S(1)}, f32[15,8,128]{2,1,0:T(8,128)S(1)}, u32[]{:S(2)}, u32[]{:S(2)}) %collective-permute-start.10) | collective-permute-done | bytes 61472 | tf_op jit(solution)/shard_map/ppermute | solution.py:476
  68.0 4.5 %shard_map.40 = (f32[20,24,128]{2,1,0:T(8,128)S(1)}, f32[20,24,128]{2,1,0:T(8,128)S(1)}, f32[20,24,128]{2,1,0:T(8,128)S(1)}, f32[20,24,128]{2,1,0:T(8,128)S(1)},...) custom-call(f32[15,8,128]{2,1,0:T(8,128)S(1)} %get-tuple-element.38.main, ...), custom_call_target="tpu_custom_call" | custom-call | flops 5000000 | bytes 2174976 | tf_op jit(solution)/shard_map/pallas_call | solution.py:115
  72.5 0.8 all_to_all.7
  73.4 38.1 %all_to_all.11 = f32[64,10,128]{2,1,0:T(8,128)} all-to-all(f32[64,10,128]{2,1,0:T(8,128)} %all_to_all.7), channel_id=1, replica_groups={{0,2,4,6,8,10,12,14,32,34,36,38,40,42,44,46,64,66,68,70,72,74,76,78,96,..., dimensions={0} | all-to-all | bytes 655360 | tf_op jit(solution)/shard_map/all_to_all | solution.py:511
  111.5 1.1 all_to_all.9.got
  112.6 0.9 copy-done.4
  113.5 0.9 copy-done.6
  114.5 0.9 copy-done.8
  115.4 0.9 copy-done.10
  116.3 8.6 %shard_map.41 = f32[16,16,128]{2,1,0:T(8,128)} custom-call(f32[640,128]{1,0:T(8,128)S(1)} %all_to_all.9.got, f32[16,16,128]{2,1,0:T(8,128)S(1)} %get-tuple-element.42.u0, f32[22,24,128]{2,1,0:T(8,128)S(1)} %get-tuple-element.43.fx0, f32[22,24,128]{2,1,0:T(8,128)S(1)} %get-tuple-element.44.fy0, f32[22,24,128]{2,1,0:T(8,128)S(1)} %get-tuple-element.45.fz0, ...), custom_call_target="tpu_custom_call" | custom-call | flops 10000000 | bytes 4554752 | tf_op jit(solution)/shard_map/pallas_call | solution.py:115
  (26 shorter events, 0.3 us)
Async XLA Ops:
  0.0 1.0 copy-start.2
  0.0 1.0 copy-start.1
  1.1 8.3 %collective-permute-start = (f32[28,16,128]{2,1,0:T(8,128)S(1)}, f32[28,16,128]{2,1,0:T(8,128)S(1)}, u32[]{:S(2)}, u32[]{:S(2)}) collective-permute-start(f32[28,16,128]{2,1,0:T(8,128)S(1)} %pad_maximum_fusion), channel_id=1, source_target_pairs={{0,16},{16,32},{32,48},{48,64},{64,80},{80,96},{96,112},{112,128},... | collective-permute-start | bytes 688136 | tf_op jit(solution)/shard_map/ppermute | solution.py:476
  4.6 9.1 %copy-start = (f32[16,16,128]{2,1,0:T(8,128)S(1)}, f32[16,16,128]{2,1,0:T(8,128)}, u32[]{:S(2)}) copy-start(f32[16,16,128]{2,1,0:T(8,128)} %eps.3) | copy-start | bytes 393220
  4.6 9.1 %collective-permute-start.1 = (f32[28,16,128]{2,1,0:T(8,128)S(1)}, f32[28,16,128]{2,1,0:T(8,128)S(1)}, u32[]{:S(2)}, u32[]{:S(2)}) collective-permute-start(f32[28,16,128]{2,1,0:T(8,128)S(1)} %pad_maximum_fusion.1), channel_id=1, source_target_pairs={{16,0},{32,16},{48,32},{64,48},{80,64},{96,80},{112,96},{128,112},... | collective-permute-start | bytes 688136 | tf_op jit(solution)/shard_map/ppermute | solution.py:476
  13.9 10.6 %collective-permute-start.2 = (f32[130,8,128]{2,1,0:T(8,128)S(1)}, f32[130,8,128]{2,1,0:T(8,128)S(1)}, u32[]{:S(2)}, u32[]{:S(2)}) collective-permute-start(f32[130,8,128]{2,1,0:T(8,128)S(1)} %get-tuple-element.32), channel_id=1, source_target_pairs={{0,1},{1,2},{2,3},{3,4},{4,5},{5,6},{6,7},{7,8},{8,9},{9,10},{10,1... | collective-permute-start | bytes 1597448 | tf_op jit(solution)/shard_map/ppermute | solution.py:476
  15.8 10.4 %collective-permute-start.3 = (f32[130,8,128]{2,1,0:T(8,128)S(1)}, f32[130,8,128]{2,1,0:T(8,128)S(1)}, u32[]{:S(2)}, u32[]{:S(2)}) collective-permute-start(f32[130,8,128]{2,1,0:T(8,128)S(1)} %get-tuple-element.33), channel_id=1, source_target_pairs={{1,0},{2,1},{3,2},{4,3},{5,4},{6,5},{7,6},{8,7},{9,8},{10,9},{11,1... | collective-permute-start | bytes 1597448 | tf_op jit(solution)/shard_map/ppermute | solution.py:476
  37.3 0.7 copy-start.7
  38.0 0.7 copy-start.9
  38.7 33.8 %copy-start.3 = (f32[18,24,128]{2,1,0:T(8,128)}, f32[18,24,128]{2,1,0:T(8,128)S(1)}, u32[]{:S(2)}) copy-start(f32[18,24,128]{2,1,0:T(8,128)S(1)} %get-tuple-element.48.fx1) | copy-start | bytes 663556
  38.7 33.8 %copy-start.5 = (f32[18,24,128]{2,1,0:T(8,128)}, f32[18,24,128]{2,1,0:T(8,128)S(1)}, u32[]{:S(2)}) copy-start(f32[18,24,128]{2,1,0:T(8,128)S(1)} %get-tuple-element.49.fy1) | copy-start | bytes 663556
  38.7 13.5 %collective-permute-start.4 = (f32[7,8,128]{2,1,0:T(8,128)S(1)}, f32[7,8,128]{2,1,0:T(8,128)S(1)}, u32[]{:S(2)}, u32[]{:S(2)}) collective-permute-start(f32[7,8,128]{2,1,0:T(8,128)S(1)} %get-tuple-element.36), channel_id=1, source_target_pairs={{0,1},{1,2},{2,3},{3,4},{4,5},{5,6},{6,7},{7,8},{8,9},{9,10},{10,1... | collective-permute-start | bytes 86024 | tf_op jit(solution)/shard_map/ppermute | solution.py:476
  42.8 9.5 %collective-permute-start.5 = (f32[7,8,128]{2,1,0:T(8,128)S(1)}, f32[7,8,128]{2,1,0:T(8,128)S(1)}, u32[]{:S(2)}, u32[]{:S(2)}) collective-permute-start(f32[7,8,128]{2,1,0:T(8,128)S(1)} %get-tuple-element.37), channel_id=1, source_target_pairs={{1,0},{2,1},{3,2},{4,3},{5,4},{6,5},{7,6},{8,7},{9,8},{10,9},{11,1... | collective-permute-start | bytes 86024 | tf_op jit(solution)/shard_map/ppermute | solution.py:476
  44.7 5.9 %collective-permute-start.7 = (f32[3,8,128]{2,1,0:T(8,128)S(1)}, f32[3,8,128]{2,1,0:T(8,128)S(1)}, u32[]{:S(2)}, u32[]{:S(2)}) collective-permute-start(f32[3,8,128]{2,1,0:T(8,128)S(1)} %get-tuple-element.34.l2_own), channel_id=1, source_target_pairs={{2,0},{3,1},{4,2},{5,3},{6,4},{7,5},{8,6},{9,7},{10,8},{11,9},{12,... | collective-permute-start | bytes 36872 | tf_op jit(solution)/shard_map/ppermute | solution.py:476
  46.7 5.6 %collective-permute-start.6 = (f32[3,8,128]{2,1,0:T(8,128)S(1)}, f32[3,8,128]{2,1,0:T(8,128)S(1)}, u32[]{:S(2)}, u32[]{:S(2)}) collective-permute-start(f32[3,8,128]{2,1,0:T(8,128)S(1)} %get-tuple-element.34.l2_own), channel_id=1, source_target_pairs={{0,2},{1,3},{2,4},{3,5},{4,6},{5,7},{6,8},{7,9},{8,10},{9,11},{10,... | collective-permute-start | bytes 36872 | tf_op jit(solution)/shard_map/ppermute | solution.py:476
  52.3 15.7 %collective-permute-start.8 = (f32[23,8,128]{2,1,0:T(8,128)S(1)}, f32[23,8,128]{2,1,0:T(8,128)S(1)}, u32[]{:S(2)}, u32[]{:S(2)}) collective-permute-start(f32[23,8,128]{2,1,0:T(8,128)S(1)} %get-tuple-element.39), channel_id=1, source_target_pairs={{0,16},{16,32},{32,48},{48,64},{64,80},{80,96},{96,112},{112,128},... | collective-permute-start | bytes 282632 | tf_op jit(solution)/shard_map/ppermute | solution.py:476
  55.8 12.2 %collective-permute-start.9 = (f32[23,8,128]{2,1,0:T(8,128)S(1)}, f32[23,8,128]{2,1,0:T(8,128)S(1)}, u32[]{:S(2)}, u32[]{:S(2)}) collective-permute-start(f32[23,8,128]{2,1,0:T(8,128)S(1)} %get-tuple-element.40), channel_id=1, source_target_pairs={{16,0},{32,16},{48,32},{64,48},{80,64},{96,80},{112,96},{128,112},... | collective-permute-start | bytes 282632 | tf_op jit(solution)/shard_map/ppermute | solution.py:476
  57.1 9.3 %collective-permute-start.11 = (f32[15,8,128]{2,1,0:T(8,128)S(1)}, f32[15,8,128]{2,1,0:T(8,128)S(1)}, u32[]{:S(2)}, u32[]{:S(2)}) collective-permute-start(f32[15,8,128]{2,1,0:T(8,128)S(1)} %get-tuple-element.38.main), channel_id=1, source_target_pairs={{32,0},{48,16},{64,32},{80,48},{96,64},{112,80},{128,96},{144,112}... | collective-permute-start | bytes 184328 | tf_op jit(solution)/shard_map/ppermute | solution.py:476
  58.4 9.6 %collective-permute-start.10 = (f32[15,8,128]{2,1,0:T(8,128)S(1)}, f32[15,8,128]{2,1,0:T(8,128)S(1)}, u32[]{:S(2)}, u32[]{:S(2)}) collective-permute-start(f32[15,8,128]{2,1,0:T(8,128)S(1)} %get-tuple-element.38.main), channel_id=1, source_target_pairs={{0,32},{16,48},{32,64},{48,80},{64,96},{80,112},{96,128},{112,144}... | collective-permute-start | bytes 184328 | tf_op jit(solution)/shard_map/ppermute | solution.py:476
  112.6 0.9 copy-start.4
  113.5 0.9 copy-start.6
  114.5 0.9 copy-start.8
  115.4 0.9 copy-start.10

commit v2 on v1

--- a/solution.py
+++ b/solution.py
@@ -50,15 +50,22 @@
     return jnp.where(good, OMEGA / jnp.where(good, diag, 1.0), 0.0)
 
 
-def loop(first, last, step, body):
+def loop(first, last, step, body, unroll=4):
     count = (last - first + 1) // step
     assert count * step == last - first + 1
+    trips = count // unroll
 
     def run(index, carry):
-        body(first + index * step)
+        for k in range(unroll):
+            body(first + (index * unroll + k) * step)
         return carry
 
-    lax.fori_loop(0, count, run, 0)
+    if trips > 1:
+        lax.fori_loop(0, trips, run, 0)
+    else:
+        trips = 0
+    for k in range(trips * unroll, count):
+        body(first + k * step)
 
 
 def beside(vals, faces, plane, count, level):
@@ -73,22 +80,22 @@
     return v, total
 
 
-def sweep(out, vals, side, faces, weight, first, last, step, level):
+def sweep(out, vals, side, faces, weight, first, last, step, level, unroll=4):
     def body(plane):
         v, total = beside(vals, faces, plane, step, level)
         here = pl.ds(plane, step)
         out[here] = (1.0 - OMEGA) * v + weight[here] * (side[here] + total)
 
-    loop(first, last, step, body)
-
-
-def remains(out, vals, side, faces, diag, first, last, step, level):
+    loop(first, last, step, body, unroll)
+
+
+def remains(out, vals, side, faces, diag, first, last, step, level, unroll=4):
     def body(plane):
         v, total = beside(vals, faces, plane, step, level)
         here = pl.ds(plane, step)
         out[here] = side[here] - diag[here] * v + total
 
-    loop(first, last, step, body)
+    loop(first, last, step, body, unroll)
 
 
 def block_sum(ref, plane, start, count):
@@ -110,12 +117,12 @@
     return pair(x_low, level), pair(y_low, level), keep(z_sum, level, 0), d_new
 
 
-def call(body, outs, scratch, limit, flops, *args):
+def call(body, outs, scratch, limit, flops, *args, space=pltpu.VMEM):
     nbytes = sum(4 * a.size for a in args) + sum(4 * o.size for o in outs)
     return pl.pallas_call(
         body,
         out_shape=outs,
-        in_specs=[pl.BlockSpec(memory_space=pltpu.VMEM)] * len(args),
+        in_specs=[pl.BlockSpec(memory_space=space)] * len(args),
         out_specs=[pl.BlockSpec(memory_space=pltpu.VMEM)] * len(outs),
         scratch_shapes=scratch,
         compiler_params=pltpu.CompilerParams(vmem_limit_bytes=limit << 20),
@@ -127,41 +134,73 @@
     return jax.ShapeDtypeStruct(shape, F32)
 
 
-def strips_kernel(eps, src, scr, xl, xr, up, down):
-    at = 0
+def x_strips_kernel(eps, src, scr, first, second, sems):
+    even = is_even("gx", 1).astype(jnp.int32)
+    copies = []
     for own, start, wide in ((eps, 0, 10), (src, 10, 9), (scr, 19, 9)):
-        for part, low, count in ((xl, start, wide), (own, 0, 16), (xr, start, wide)):
-            up[at : at + count] = part[low : low + count, 8:16]
-            down[at : at + count] = part[low : low + count, 0:8]
-            for k in range(count):
-                tile, row = 104 + (at + k) // 4, 2 * ((at + k) % 4)
-                up[tile, row : row + 2] = part[low + k, 6:8]
-                down[tile, row : row + 2] = part[low + k, 8:10]
-            at += count
+        for out, low in ((first, (16 - wide) * even), (second, (16 - wide) * (1 - even))):
+            source, target = own.at[pl.ds(low, wide)], out.at[pl.ds(start, wide)]
+            copies.append(pltpu.make_async_copy(source, target, sems.at[len(copies)]))
+    for copy in copies:
+        copy.start()
+    for copy in copies:
+        copy.wait()
+
+
+def y_strips_kernel(eps, src, scr, xa, xb, first, second):
+    x_even = is_even("gx", 1)
+    y_even = is_even("gy", 1)
+
+    def fill(up, down, xl, xr):
+        at = 0
+        for own, start, wide in ((eps, 0, 10), (src, 10, 9), (scr, 19, 9)):
+            for part, low, count in ((xl, start, wide), (own, 0, 16), (xr, start, wide)):
+                up[at : at + count] = part[low : low + count, 8:16]
+                down[at : at + count] = part[low : low + count, 0:8]
+                for k in range(count):
+                    tile, row = 104 + (at + k) // 4, 2 * ((at + k) % 4)
+                    up[tile, row : row + 2] = part[low + k, 6:8]
+                    down[tile, row : row + 2] = part[low + k, 8:10]
+                at += count
+
+    for x_want, (xl, xr) in ((True, (xb, xa)), (False, (xa, xb))):
+        for y_want, (up, down) in ((True, (first, second)), (False, (second, first))):
+            pl.when((x_even == x_want) & (y_even == y_want))(
+                lambda up=up, down=down, xl=xl, xr=xr: fill(up, down, xl, xr)
+            )
 
 
 def down_kernel(
-    eps, src, scr, xl, xr, yl, yr,
+    eps, src, scr, xa, xb, ya, yb,
     u0_out, fx0_out, fy0_out, fz0_out, w0_out, r0_out,
-    fx1, fy1, fz1, w1, l1_own, l2_own, up, down,
+    fx1, fy1, fz1, w1, l1_own, l2_own, ship_a, ship_b,
     e, b, s, fx, fy, fz, w, d, ua, ub, b1, d1, va, vb,
 ):
+    x_even = is_even("gx", 1).astype(jnp.int32)
+    y_even = is_even("gy", 1)
+    row_a = pl.multiple_of(8 + 24 * y_even.astype(jnp.int32), 8)
+    row_b = pl.multiple_of(32 - 24 * y_even.astype(jnp.int32), 8)
     at = 0
     for ref, own, start, wide in ((e, eps, 0, 10), (b, src, 10, 9), (s, scr, 19, 9)):
         first = 10 - wide
         planes = 16 + 2 * wide
-        ref[first:10, 16:32] = xl[start : start + wide]
         ref[10:26, 16:32] = own[...]
-        ref[26 : 26 + wide, 16:32] = xr[start : start + wide]
-        ref[first : first + planes, 8:16] = yl[at : at + planes]
-        ref[first : first + planes, 32:40] = yr[at : at + planes]
-        for k in range(planes):
-            tile, row = 104 + (at + k) // 4, 2 * ((at + k) % 4)
-            below, above = yl[tile], yr[tile]
-            rows = row_of(below)
-            ref[first + k, 0:8] = jnp.where(
-                rows < 2, roll(above, -row, 0), jnp.where(rows >= 6, roll(below, 6 - row, 0), 0.0)
-            )
+        ref[pl.ds(first + (26 - first) * x_even, wide), 16:32] = xa[start : start + wide]
+        ref[pl.ds(26 - (26 - first) * x_even, wide), 16:32] = xb[start : start + wide]
+        ref[first : first + planes, pl.ds(row_a, 8)] = ya[at : at + planes]
+        ref[first : first + planes, pl.ds(row_b, 8)] = yb[at : at + planes]
+
+        def fill(below_ref, above_ref, ref=ref, first=first, planes=planes, at=at):
+            for k in range(planes):
+                tile, row = 104 + (at + k) // 4, 2 * ((at + k) % 4)
+                below, above = below_ref[tile], above_ref[tile]
+                rows = row_of(below)
+                ref[first + k, 0:8] = jnp.where(
+                    rows < 2, roll(above, -row, 0), jnp.where(rows >= 6, roll(below, 6 - row, 0), 0.0)
+                )
+
+        pl.when(y_even)(lambda fill=fill: fill(yb, ya))
+        pl.when(jnp.logical_not(y_even))(lambda fill=fill: fill(ya, yb))
         at += planes
 
     def stencil(plane):
@@ -185,11 +224,11 @@
         w[here] = weight
         ua[here] = weight * b[here]
 
-    loop(1, 34, 2, stencil)
+    loop(1, 34, 2, stencil, 8)
     faces = (fx, fy, fz)
-    sweep(ub, ua, b, faces, w, 2, 33, 2, 0)
-    sweep(ua, ub, b, faces, w, 3, 32, 2, 0)
-    remains(ub, ua, b, faces, d, 4, 31, 2, 0)
+    sweep(ub, ua, b, faces, w, 2, 33, 2, 0, 8)
+    sweep(ua, ub, b, faces, w, 3, 32, 2, 0, 8)
+    remains(ub, ua, b, faces, d, 4, 31, 2, 0, 8)
     u0_out[...] = ua[10:26, 16:32]
 
     def keep_window(plane):
@@ -198,7 +237,7 @@
             high, low = ref[plane + 7, 32:40], ref[plane + 7, 8:16]
             out[plane, 0:8] = jnp.where(row_of(high) < 4, high, low)
 
-    loop(0, 21, 1, keep_window)
+    loop(0, 21, 1, keep_window, 8)
 
     def to_level1(plane):
         x_face, y_face, z_face, diag = coarse_stencil(faces, d, 2 * plane, 0, 20, 0)
@@ -211,7 +250,7 @@
 
     for ref in (fx1, fy1, fz1, w1, d1, b1):
         ref[:, 16:24] = jnp.zeros((18, 8, LANES), F32)
-    loop(1, 16, 1, to_level1)
+    loop(1, 16, 1, to_level1, 8)
     even, odd = pl.ds(0, 20, stride=2), pl.ds(1, 20, stride=2)
     fx1[17, 0:20] = pair(fx[34, even, :] + fx[34, odd, :], 0)
 
@@ -220,7 +259,7 @@
         b1[plane, 0:20] = side
         va[plane, 0:20] = w1[plane, 0:20] * side
 
-    loop(2, 15, 1, side1)
+    loop(2, 15, 1, side1, 8)
     va[:, 20:24] = jnp.zeros((18, 4, LANES), F32)
     faces1 = (fx1, fy1, fz1)
     sweep(vb, va, b1, faces1, w1, 3, 14, 4, 1)
@@ -240,41 +279,55 @@
         l2_own[k // 2, 4 * (k % 2) : 4 * (k % 2) + 4] = stack
         packed = jnp.where(quarter == k, pair(block_sum(vb, 5 + 2 * k, 8, 4), 1), packed)
     l2_own[2, 0:4] = packed
-    up[0:3] = l2_own[...]
-    down[0:3] = l2_own[...]
+    ship_a[0:3] = l2_own[...]
+    ship_b[0:3] = l2_own[...]
     for t in range(4):
         first, second = l1_own[2 * t], l1_own[2 * t + 1]
         low = row_of(first) < 4
-        up[3 + t] = jnp.where(low, roll(first, -4, 0), second)
-        down[3 + t] = jnp.where(low, first, roll(second, 4, 0))
-
-
-def window_kernel(l2_own, l1_own, a1u, a1d, a2u, a2d, main, up, down, l1_ext):
+        up = jnp.where(low, roll(first, -4, 0), second)
+        down = jnp.where(low, first, roll(second, 4, 0))
+        ship_a[3 + t] = jnp.where(y_even, up, down)
+        ship_b[3 + t] = jnp.where(y_even, down, up)
+
+
+def window_kernel(l2_own, l1_own, a1a, a1b, a2a, a2b, main, ship_a, ship_b, l1_ext):
+    y_even = is_even("gy", 1)
+    pl.when(y_even)(lambda: join_y(l2_own, l1_own, a1b, a1a, a2a, a2b, main, l1_ext))
+    pl.when(jnp.logical_not(y_even))(lambda: join_y(l2_own, l1_own, a1a, a1b, a2a, a2b, main, l1_ext))
+    x_even = is_even("gx", 1).astype(jnp.int32)
+    ship_a[0:15] = main[...]
+    ship_b[0:15] = main[...]
+    ship_a[15:23] = l1_ext[pl.ds(8 * x_even, 8)]
+    ship_b[15:23] = l1_ext[pl.ds(8 - 8 * x_even, 8)]
+
+
+def join_y(l2_own, l1_own, a1u, a1d, a2a, a2b, main, l1_ext):
+    two_even = is_even("gy", 2)
     low = lax.broadcasted_iota(jnp.int32, (8, LANES), 0) < 4
     for k in range(5):
         t, turn = k // 2, 4 * (k % 2)
-        main[3 * k] = jnp.where(low, roll(a2u[t], -turn, 0), roll(a1u[t], 4 - turn, 0))
+        far_a, far_b = a2a[t], a2b[t]
+        far_u, far_d = jnp.where(two_even, far_b, far_a), jnp.where(two_even, far_a, far_b)
+        main[3 * k] = jnp.where(low, roll(far_u, -turn, 0), roll(a1u[t], 4 - turn, 0))
         main[3 * k + 1] = jnp.where(low, roll(l2_own[t], -turn, 0), roll(a1d[t], 4 - turn, 0))
-        main[3 * k + 2] = jnp.where(low, roll(a2d[t], -turn, 0), 0.0)
+        main[3 * k + 2] = jnp.where(low, roll(far_d, -turn, 0), 0.0)
     for k in range(8):
         t, turn = 3 + k // 2, 4 * (k % 2)
         l1_ext[2 * k] = jnp.where(low, roll(a1d[t], -turn, 0), roll(a1u[t], 4 - turn, 0))
         l1_ext[2 * k + 1] = l1_own[k]
-    up[0:15] = main[...]
-    down[0:15] = main[...]
-    up[15:23] = l1_ext[8:16]
-    down[15:23] = l1_ext[0:8]
 
 
 def level2_kernel(
-    main, c1u, c1d, c2u, c2d,
+    main, c1a, c1b, c2a, c2b,
     fx, fy, fz, w, r, u, payload,
     d, b, ua, ub, coarse,
 ):
-    for group, part in enumerate((c2u, c1u, main, c1d, c2d)):
+    one, two = is_even("gx", 1).astype(jnp.int32), is_even("gx", 2).astype(jnp.int32)
+    starts = (16 * two, 4 + 8 * one, 8, 12 - 8 * one, 16 - 16 * two)
+    for start, part in zip(starts, (c2a, c1a, main, c1b, c2b)):
         sides = jnp.concatenate([part[12], part[13], part[14]], axis=0)
         for k in range(4):
-            plane = 4 * group + k
+            plane = start + k
             tiles = jnp.concatenate([part[3 * k], part[3 * k + 1], part[3 * k + 2]], axis=0)
             fx[plane] = spread(tiles, 0, 2)
             fy[plane] = spread(tiles, 1, 2)
@@ -375,7 +428,7 @@
 
 def up_kernel(
     got, u0, fx0, fy0, fz0, w0, r0,
-    fx1, fy1, fz1, w1, l1_ext, c1u, c1d,
+    fx1, fy1, fz1, w1, l1_ext, c1a, c1b,
     fx2, fy2, fz2, w2, r2, u2,
     out,
     u3, e3, ea2, eb2, r1, u1, ea1, eb1, ea0, eb0,
@@ -415,7 +468,8 @@
     sweep(ea2, eb2, r2, faces, w2, 4, 15, 4, 2)
     sweep(eb2, ea2, r2, faces, w2, 5, 14, 2, 2)
 
-    for part, first, tile, count in ((c1u, 1, 15, 4), (l1_ext, 5, 0, 8), (c1d, 13, 15, 4)):
+    even = is_even("gx", 1).astype(jnp.int32)
+    for part, first, tile, count in ((c1a, 1 + 12 * even, 15, 4), (l1_ext, 5, 0, 8), (c1b, 13 - 12 * even, 15, 4)):
         for k in range(count):
             sides, own = part[tile + 2 * k], part[tile + 2 * k + 1]
             for ref, which in ((r1, 0), (u1, 1)):
@@ -470,37 +524,43 @@
     return (where >= 0) & (where < 8 * lax.axis_size("gx"))
 
 
-def shifted(values, axis, step):
-    count = lax.axis_size(axis)
-    pairs = [(k, k + step) for k in range(count) if 0 <= k + step < count]
+def swapped(values, axis, step, odd):
+    pairs = []
+    for k in range(lax.axis_size(axis) - step):
+        if (k // step) % 2 == odd:
+            pairs += [(k, k + step), (k + step, k)]
     return lax.ppermute(values, axis, pairs)
+
+
+def is_even(axis, step):
+    return lax.rem(lax.div(lax.axis_index(axis), step), 2) == 0
 
 
 def local(source, dielectric, screening):
     fields = (dielectric, source, screening)
-    last = jnp.concatenate([dielectric[6:], source[7:], screening[7:]], axis=0)
-    first = jnp.concatenate([dielectric[:10], source[:9], screening[:9]], axis=0)
-    xl, xr = shifted(last, "gx", 1), shifted(first, "gx", -1)
-    up, down = call(strips_kernel, [array(130, 8, LANES)] * 2, [], 16, 10_000, *fields, xl, xr)
-    yl, yr = shifted(up, "gy", 1), shifted(down, "gy", -1)
+    sems = [pltpu.SemaphoreType.DMA((6,))]
+    xa, xb = call(x_strips_kernel, [array(28, 16, LANES)] * 2, sems, 2, 10_000, *fields, space=pl.ANY)
+    xa, xb = swapped(xa, "gx", 1, 0), swapped(xb, "gx", 1, 1)
+    ya, yb = call(y_strips_kernel, [array(130, 8, LANES)] * 2, [], 2, 10_000, *fields, xa, xb)
+    ya, yb = swapped(ya, "gy", 1, 0), swapped(yb, "gy", 1, 1)
 
     big, mid = pltpu.VMEM((36, 40, LANES), F32), pltpu.VMEM((18, 24, LANES), F32)
     outs = [array(16, 16, LANES)] + [array(22, 24, LANES)] * 5 + [array(18, 24, LANES)] * 4
     outs += [array(8, 8, LANES), array(3, 8, LANES), array(7, 8, LANES), array(7, 8, LANES)]
-    made = call(down_kernel, outs, [big] * 10 + [mid] * 4, 24, 10_000_000, *fields, xl, xr, yl, yr)
-    fine, level1, (l1_own, l2_own, up, down) = made[0:6], made[6:10], made[10:14]
-
-    a1u, a1d = shifted(up, "gy", 1), shifted(down, "gy", -1)
-    a2u, a2d = shifted(l2_own, "gy", 2), shifted(l2_own, "gy", -2)
+    made = call(down_kernel, outs, [big] * 10 + [mid] * 4, 12, 10_000_000, *fields, xa, xb, ya, yb)
+    fine, level1, (l1_own, l2_own, sa, sb) = made[0:6], made[6:10], made[10:14]
+
+    a1a, a1b = swapped(sa, "gy", 1, 0), swapped(sb, "gy", 1, 1)
+    a2a, a2b = swapped(l2_own, "gy", 2, 0), swapped(l2_own, "gy", 2, 1)
     outs = [array(15, 8, LANES), array(23, 8, LANES), array(23, 8, LANES), array(16, 8, LANES)]
-    main, up, down, l1_ext = call(window_kernel, outs, [], 16, 10_000, l2_own, l1_own, a1u, a1d, a2u, a2d)
-    c1u, c1d = shifted(up, "gx", 1), shifted(down, "gx", -1)
-    c2u, c2d = shifted(main, "gx", 2), shifted(main, "gx", -2)
+    main, sa, sb, l1_ext = call(window_kernel, outs, [], 2, 10_000, l2_own, l1_own, a1a, a1b, a2a, a2b)
+    c1a, c1b = swapped(sa, "gx", 1, 0), swapped(sb, "gx", 1, 1)
+    c2a, c2b = swapped(main, "gx", 2, 0), swapped(main, "gx", 2, 1)
 
     two = pltpu.VMEM((20, 24, LANES), F32)
     outs = [array(20, 24, LANES)] * 6 + [array(640, LANES)]
     scratch = [two] * 4 + [pltpu.VMEM((5, 10, 8, LANES), F32)]
-    *level2, payload = call(level2_kernel, outs, scratch, 16, 5_000_000, main, c1u, c1d, c2u, c2d)
+    *level2, payload = call(level2_kernel, outs, scratch, 4, 5_000_000, main, c1a, c1b, c2a, c2b)
 
     n_x, n_y = lax.axis_size("gx"), lax.axis_size("gy")
     groups = [
@@ -508,13 +568,15 @@
         for p in range(2)
         for q in range(2)
     ]
+    payload = payload.reshape(320, 2, LANES)
     got = lax.all_to_all(payload, ("gx", "gy"), 0, 0, tiled=True, axis_index_groups=groups)
+    got = got.reshape(640, LANES)
 
     scratch = [pltpu.VMEM((2, 96, LANES), F32), pltpu.VMEM((12, 16, LANES), F32)]
     scratch += [two] * 2 + [mid] * 4 + [pltpu.VMEM((22, 24, LANES), F32)] * 2
     (result,) = call(
-        up_kernel, [array(16, 16, LANES)], scratch, 24, 10_000_000,
-        got, *fine, *level1, l1_ext, c1u, c1d, *level2,
+        up_kernel, [array(16, 16, LANES)], scratch, 6, 10_000_000,
+        got, *fine, *level1, l1_ext, c1a, c1b, *level2,
     )
     return result
 

time: 126 us -> 93 us (0.74)
  Pallas kernels: 24.4 us -> 13.5 us
  blocking collectives: 38.1 us -> 29.2 us
  starting transfers between devices: 36.1 us -> 27.5 us
  local copies, waits for them, and re-layouts: 8.08 us -> 2.72 us
    pallas_call x5 -> x6, Pallas kernels: 24.4 us -> 13.5 us  [call(): pl.pallas_call(body, out_shape=outs, in_specs=[pl.BlockSpec(memory_space=...]
    all_to_all x1, blocking collectives: 38.1 us -> 29.2 us  [local(): lax.all_to_all(payload, ('gx', 'gy'), 0, 0, tiled=True, axis_index_groups...]
    ppermute x12, starting transfers between devices: 36.1 us -> 27.5 us  [swapped(): return lax.ppermute(values, axis, pairs)]
    unnamed x22 -> x12, local copies, waits for them, and re-layouts: 5.15 us -> 2.72 us
    all_to_all x2 -> x0, local copies, waits for them, and re-layouts: 1.92 us -> none  [local(): lax.all_to_all(payload, ('gx', 'gy'), 0, 0, tiled=True, axis_index_groups...]
  transfers between devices with their start and end apart: 12 -> 12, of which waited for: 7 -> 5; matrix products, arithmetic and copies ran while one was open for 0% -> 0% of each run, Pallas kernels for 0% -> 0%
where the time goes in v2:
time: 93 us; the launch traced here: 92.2 us
  blocking collectives  29.2 us (31%)
  starting transfers between devices  27.5 us (30%)
  waiting for transfers between devices  19.1 us (21%)
  Pallas kernels  13.5 us (15%)
  local copies, waits for them, and re-layouts  2.72 us (3%)
    all_to_all x1, blocking collectives, local(): lax.all_to_all(payload, ('gx', 'gy'), 0, 0, tiled=True, axis_index_groups...  29.2 us
    ppermute x12, starting transfers between devices, swapped(): return lax.ppermute(values, axis, pairs)  27.5 us
    ppermute x12, waiting for transfers between devices, swapped(): return lax.ppermute(values, axis, pairs)  19.1 us
    pallas_call x6, Pallas kernels, call(): pl.pallas_call(body, out_shape=outs, in_specs=[pl.BlockSpec(memory_space=...  13.5 us
    unnamed x12, local copies, waits for them, and re-layouts  2.72 us
  transfers between devices with their start and end apart: 12, of which 5 were waited for; matrix products, arithmetic and copies ran while one was open for 0% of the time, Pallas kernels for 0%

profile of v2, /device:TPU:32, one launch (start us, length us, event | category | flops | bytes accessed | tf_op | source)
XLA Modules:
  0.0 92.2 jit_solution(9346008085673937086)
XLA Ops:
  0.0 0.9 copy-done
  0.9 0.9 copy-done.2
  1.8 0.9 copy-done.4
  2.7 0.6 shard_map.37
  3.3 1.7 %collective-permute-start = (f32[28,16,128]{2,1,0:T(8,128)S(1)}, f32[28,16,128]{2,1,0:T(8,128)S(1)}, u32[]{:S(2)}, u32[]{:S(2)}) collective-permute-start(f32[28,16,128]{2,1,0:T(8,128)S(1)} %get-tuple-element.34), channel_id=1, source_target_pairs={{0,16},{16,0},{32,48},{48,32},{64,80},{80,64},{96,112},{112,96},{1... | collective-permute-start | bytes 688136 | tf_op jit(solution)/shard_map/ppermute | solution.py:532
  5.0 0.8 collective-permute-start.1
  5.8 5.0 %collective-permute-done.xa = f32[28,16,128]{2,1,0:T(8,128)S(1)} collective-permute-done((f32[28,16,128]{2,1,0:T(8,128)S(1)}, f32[28,16,128]{2,1,0:T(8,128)S(1)}, u32[]{:S(2)}, u32[]{:S(2)}) %collective-permute-start) | collective-permute-done | bytes 229408 | tf_op jit(solution)/shard_map/ppermute | solution.py:532
  10.8 0.0 collective-permute-done.1.xb
  10.8 0.1 shard_map.38
  10.9 0.1 collective-permute-start.2
  11.0 2.5 %collective-permute-start.3 = (f32[130,8,128]{2,1,0:T(8,128)S(1)}, f32[130,8,128]{2,1,0:T(8,128)S(1)}, u32[]{:S(2)}, u32[]{:S(2)}) collective-permute-start(f32[130,8,128]{2,1,0:T(8,128)S(1)} %get-tuple-element.37), channel_id=1, source_target_pairs={{1,2},{2,1},{3,4},{4,3},{5,6},{6,5},{7,8},{8,7},{9,10},{10,9},{11,... | collective-permute-start | bytes 1597448 | tf_op jit(solution)/shard_map/ppermute | solution.py:532
  13.6 0.0 collective-permute-done.2.ya
  13.6 8.1 %collective-permute-done.3.yb = f32[130,8,128]{2,1,0:T(8,128)S(1)} collective-permute-done((f32[130,8,128]{2,1,0:T(8,128)S(1)}, f32[130,8,128]{2,1,0:T(8,128)S(1)}, u32[]{:S(2)}, u32[]{:S(2)}) %collective-permute-start.3) | collective-permute-done | bytes 532512 | tf_op jit(solution)/shard_map/ppermute | solution.py:532
  21.6 3.6 %shard_map.39 = (f32[16,16,128]{2,1,0:T(8,128)S(1)}, f32[22,24,128]{2,1,0:T(8,128)S(1)}, f32[22,24,128]{2,1,0:T(8,128)S(1)}, f32[22,24,128]{2,1,0:T(8,128)S(1)},...) custom-call(f32[16,16,128]{2,1,0:T(8,128)S(1)} %copy-done.1, ...), custom_call_target="tpu_custom_call" | custom-call | flops 10000000 | bytes 4386816 | tf_op jit(solution)/shard_map/pallas_call | solution.py:122
  25.3 0.6 collective-permute-start.4
  25.8 2.0 %collective-permute-start.5 = (f32[7,8,128]{2,1,0:T(8,128)S(1)}, f32[7,8,128]{2,1,0:T(8,128)S(1)}, u32[]{:S(2)}, u32[]{:S(2)}) collective-permute-start(f32[7,8,128]{2,1,0:T(8,128)S(1)} %get-tuple-element.41), channel_id=1, source_target_pairs={{1,2},{2,1},{3,4},{4,3},{5,6},{6,5},{7,8},{8,7},{9,10},{10,9},{11,... | collective-permute-start | bytes 86024 | tf_op jit(solution)/shard_map/ppermute | solution.py:532
  27.9 3.7 %collective-permute-start.7 = (f32[3,8,128]{2,1,0:T(8,128)S(1)}, f32[3,8,128]{2,1,0:T(8,128)S(1)}, u32[]{:S(2)}, u32[]{:S(2)}) collective-permute-start(f32[3,8,128]{2,1,0:T(8,128)S(1)} %get-tuple-element.38.l2_own), channel_id=1, source_target_pairs={{2,4},{4,2},{3,5},{5,3},{6,8},{8,6},{7,9},{9,7},{10,12},{12,10},{1... | collective-permute-start | bytes 36872 | tf_op jit(solution)/shard_map/ppermute | solution.py:532
  31.6 0.1 collective-permute-start.6
  31.7 1.8 %collective-permute-done.7.a2b = f32[3,8,128]{2,1,0:T(8,128)S(1)} collective-permute-done((f32[3,8,128]{2,1,0:T(8,128)S(1)}, f32[3,8,128]{2,1,0:T(8,128)S(1)}, u32[]{:S(2)}, u32[]{:S(2)}) %collective-permute-start.7) | collective-permute-done | bytes 12320 | tf_op jit(solution)/shard_map/ppermute | solution.py:532
  33.5 1.9 %collective-permute-done.6.a2a = f32[3,8,128]{2,1,0:T(8,128)S(1)} collective-permute-done((f32[3,8,128]{2,1,0:T(8,128)S(1)}, f32[3,8,128]{2,1,0:T(8,128)S(1)}, u32[]{:S(2)}, u32[]{:S(2)}) %collective-permute-start.6) | collective-permute-done | bytes 12320 | tf_op jit(solution)/shard_map/ppermute | solution.py:532
  35.4 0.0 collective-permute-done.4.a1a
  35.4 0.0 collective-permute-done.5.a1b
  35.4 4.5 %collective-permute-start.8 = (f32[23,8,128]{2,1,0:T(8,128)S(1)}, f32[23,8,128]{2,1,0:T(8,128)S(1)}, u32[]{:S(2)}, u32[]{:S(2)}) collective-permute-start(f32[23,8,128]{2,1,0:T(8,128)S(1)} %get-tuple-element.43), channel_id=1, source_target_pairs={{0,16},{16,0},{32,48},{48,32},{64,80},{80,64},{96,112},{112,96},{1... | collective-permute-start | bytes 282632 | tf_op jit(solution)/shard_map/ppermute | solution.py:532
  39.9 0.7 collective-permute-start.9
  40.6 0.7 collective-permute-start.11
  41.3 10.2 %collective-permute-start.10 = (f32[15,8,128]{2,1,0:T(8,128)S(1)}, f32[15,8,128]{2,1,0:T(8,128)S(1)}, u32[]{:S(2)}, u32[]{:S(2)}) collective-permute-start(f32[15,8,128]{2,1,0:T(8,128)S(1)} %get-tuple-element.42.main), channel_id=1, source_target_pairs={{0,32},{32,0},{16,48},{48,16},{64,96},{96,64},{80,112},{112,80},{1... | collective-permute-start | bytes 184328 | tf_op jit(solution)/shard_map/ppermute | solution.py:532
  51.5 0.0 collective-permute-done.11.c2b
  51.5 2.4 %collective-permute-done.10.c2a = f32[15,8,128]{2,1,0:T(8,128)S(1)} collective-permute-done((f32[15,8,128]{2,1,0:T(8,128)S(1)}, f32[15,8,128]{2,1,0:T(8,128)S(1)}, u32[]{:S(2)}, u32[]{:S(2)}) %collective-permute-start.10) | collective-permute-done | bytes 61472 | tf_op jit(solution)/shard_map/ppermute | solution.py:532
  53.8 0.0 collective-permute-done.8.c1a
  53.8 3.9 %shard_map.41 = (f32[20,24,128]{2,1,0:T(8,128)S(1)}, f32[20,24,128]{2,1,0:T(8,128)S(1)}, f32[20,24,128]{2,1,0:T(8,128)S(1)}, f32[20,24,128]{2,1,0:T(8,128)S(1)},...) custom-call(f32[15,8,128]{2,1,0:T(8,128)S(1)} %get-tuple-element.42.main, ...), custom_call_target="tpu_custom_call" | custom-call | flops 5000000 | bytes 2174976 | tf_op jit(solution)/shard_map/pallas_call | solution.py:122
  57.8 29.2 %all_to_all.5 = f32[320,2,128]{2,1,0:T(2,128)S(1)} all-to-all(f32[320,2,128]{2,1,0:T(2,128)S(1)} %bitcast.3), channel_id=1, replica_groups={{0,2,4,6,8,10,12,14,32,34,36,38,40,42,44,46,64,66,68,70,72,74,76,78,96,..., dimensions={0} | all-to-all | bytes 655360 | tf_op jit(solution)/shard_map/all_to_all | solution.py:572
  87.0 5.2 %shard_map.42 = f32[16,16,128]{2,1,0:T(8,128)} custom-call(f32[640,128]{1,0:T(8,128)S(1)} %bitcast.2, f32[16,16,128]{2,1,0:T(8,128)S(1)} %get-tuple-element.46.u0, f32[22,24,128]{2,1,0:T(8,128)S(1)} %get-tuple-element.47.fx0, f32[22,24,128]{2,1,0:T(8,128)S(1)} %get-tuple-element.48.fy0, f32[22,24,128]{2,1,0:T(8,128)S(1)} %get-tuple-element.49.fz0, ...), custom_call_target="tpu_custom_call" | custom-call | flops 10000000 | bytes 4554752 | tf_op jit(solution)/shard_map/pallas_call | solution.py:122
  (11 shorter events, 0.1 us)
Async XLA Ops:
  0.0 0.9 copy-start
  0.9 0.9 copy-start.2
  1.8 0.9 copy-start.4
  3.3 7.4 %collective-permute-start = (f32[28,16,128]{2,1,0:T(8,128)S(1)}, f32[28,16,128]{2,1,0:T(8,128)S(1)}, u32[]{:S(2)}, u32[]{:S(2)}) collective-permute-start(f32[28,16,128]{2,1,0:T(8,128)S(1)} %get-tuple-element.34), channel_id=1, source_target_pairs={{0,16},{16,0},{32,48},{48,32},{64,80},{80,64},{96,112},{112,96},{1... | collective-permute-start | bytes 688136 | tf_op jit(solution)/shard_map/ppermute | solution.py:532
  5.0 16.6 %copy-start.1 = (f32[16,16,128]{2,1,0:T(8,128)S(1)}, f32[16,16,128]{2,1,0:T(8,128)}, u32[]{:S(2)}) copy-start(f32[16,16,128]{2,1,0:T(8,128)} %eps.5) | copy-start | bytes 393220
  5.0 16.6 %copy-start.3 = (f32[16,16,128]{2,1,0:T(8,128)S(1)}, f32[16,16,128]{2,1,0:T(8,128)}, u32[]{:S(2)}) copy-start(f32[16,16,128]{2,1,0:T(8,128)} %src.5) | copy-start | bytes 393220
  5.0 16.6 %copy-start.5 = (f32[16,16,128]{2,1,0:T(8,128)S(1)}, f32[16,16,128]{2,1,0:T(8,128)}, u32[]{:S(2)}) copy-start(f32[16,16,128]{2,1,0:T(8,128)} %scr.5) | copy-start | bytes 393220
  5.0 5.8 %collective-permute-start.1 = (f32[28,16,128]{2,1,0:T(8,128)S(1)}, f32[28,16,128]{2,1,0:T(8,128)S(1)}, u32[]{:S(2)}, u32[]{:S(2)}) collective-permute-start(f32[28,16,128]{2,1,0:T(8,128)S(1)} %get-tuple-element.35), channel_id=1, source_target_pairs={{16,32},{32,16},{48,64},{64,48},{80,96},{96,80},{112,128},{128,112... | collective-permute-start | bytes 688136 | tf_op jit(solution)/shard_map/ppermute | solution.py:532
  10.9 2.6 %collective-permute-start.2 = (f32[130,8,128]{2,1,0:T(8,128)S(1)}, f32[130,8,128]{2,1,0:T(8,128)S(1)}, u32[]{:S(2)}, u32[]{:S(2)}) collective-permute-start(f32[130,8,128]{2,1,0:T(8,128)S(1)} %get-tuple-element.36), channel_id=1, source_target_pairs={{0,1},{1,0},{2,3},{3,2},{4,5},{5,4},{6,7},{7,6},{8,9},{9,8},{10,11... | collective-permute-start | bytes 1597448 | tf_op jit(solution)/shard_map/ppermute | solution.py:532
  11.0 10.6 %collective-permute-start.3 = (f32[130,8,128]{2,1,0:T(8,128)S(1)}, f32[130,8,128]{2,1,0:T(8,128)S(1)}, u32[]{:S(2)}, u32[]{:S(2)}) collective-permute-start(f32[130,8,128]{2,1,0:T(8,128)S(1)} %get-tuple-element.37), channel_id=1, source_target_pairs={{1,2},{2,1},{3,4},{4,3},{5,6},{6,5},{7,8},{8,7},{9,10},{10,9},{11,... | collective-permute-start | bytes 1597448 | tf_op jit(solution)/shard_map/ppermute | solution.py:532
  25.3 10.1 %collective-permute-start.4 = (f32[7,8,128]{2,1,0:T(8,128)S(1)}, f32[7,8,128]{2,1,0:T(8,128)S(1)}, u32[]{:S(2)}, u32[]{:S(2)}) collective-permute-start(f32[7,8,128]{2,1,0:T(8,128)S(1)} %get-tuple-element.40), channel_id=1, source_target_pairs={{0,1},{1,0},{2,3},{3,2},{4,5},{5,4},{6,7},{7,6},{8,9},{9,8},{10,11... | collective-permute-start | bytes 86024 | tf_op jit(solution)/shard_map/ppermute | solution.py:532
  25.8 9.5 %collective-permute-start.5 = (f32[7,8,128]{2,1,0:T(8,128)S(1)}, f32[7,8,128]{2,1,0:T(8,128)S(1)}, u32[]{:S(2)}, u32[]{:S(2)}) collective-permute-start(f32[7,8,128]{2,1,0:T(8,128)S(1)} %get-tuple-element.41), channel_id=1, source_target_pairs={{1,2},{2,1},{3,4},{4,3},{5,6},{6,5},{7,8},{8,7},{9,10},{10,9},{11,... | collective-permute-start | bytes 86024 | tf_op jit(solution)/shard_map/ppermute | solution.py:532
  27.9 5.6 %collective-permute-start.7 = (f32[3,8,128]{2,1,0:T(8,128)S(1)}, f32[3,8,128]{2,1,0:T(8,128)S(1)}, u32[]{:S(2)}, u32[]{:S(2)}) collective-permute-start(f32[3,8,128]{2,1,0:T(8,128)S(1)} %get-tuple-element.38.l2_own), channel_id=1, source_target_pairs={{2,4},{4,2},{3,5},{5,3},{6,8},{8,6},{7,9},{9,7},{10,12},{12,10},{1... | collective-permute-start | bytes 36872 | tf_op jit(solution)/shard_map/ppermute | solution.py:532
  31.6 3.8 %collective-permute-start.6 = (f32[3,8,128]{2,1,0:T(8,128)S(1)}, f32[3,8,128]{2,1,0:T(8,128)S(1)}, u32[]{:S(2)}, u32[]{:S(2)}) collective-permute-start(f32[3,8,128]{2,1,0:T(8,128)S(1)} %get-tuple-element.38.l2_own), channel_id=1, source_target_pairs={{0,2},{2,0},{1,3},{3,1},{4,6},{6,4},{5,7},{7,5},{8,10},{10,8},{9,1... | collective-permute-start | bytes 36872 | tf_op jit(solution)/shard_map/ppermute | solution.py:532
  35.4 18.4 %collective-permute-start.8 = (f32[23,8,128]{2,1,0:T(8,128)S(1)}, f32[23,8,128]{2,1,0:T(8,128)S(1)}, u32[]{:S(2)}, u32[]{:S(2)}) collective-permute-start(f32[23,8,128]{2,1,0:T(8,128)S(1)} %get-tuple-element.43), channel_id=1, source_target_pairs={{0,16},{16,0},{32,48},{48,32},{64,80},{80,64},{96,112},{112,96},{1... | collective-permute-start | bytes 282632 | tf_op jit(solution)/shard_map/ppermute | solution.py:532
  39.9 13.9 %collective-permute-start.9 = (f32[23,8,128]{2,1,0:T(8,128)S(1)}, f32[23,8,128]{2,1,0:T(8,128)S(1)}, u32[]{:S(2)}, u32[]{:S(2)}) collective-permute-start(f32[23,8,128]{2,1,0:T(8,128)S(1)} %get-tuple-element.44), channel_id=1, source_target_pairs={{16,32},{32,16},{48,64},{64,48},{80,96},{96,80},{112,128},{128,112... | collective-permute-start | bytes 282632 | tf_op jit(solution)/shard_map/ppermute | solution.py:532
  40.6 10.9 %collective-permute-start.11 = (f32[15,8,128]{2,1,0:T(8,128)S(1)}, f32[15,8,128]{2,1,0:T(8,128)S(1)}, u32[]{:S(2)}, u32[]{:S(2)}) collective-permute-start(f32[15,8,128]{2,1,0:T(8,128)S(1)} %get-tuple-element.42.main), channel_id=1, source_target_pairs={{32,64},{64,32},{48,80},{80,48},{96,128},{128,96},{112,144},{144,1... | collective-permute-start | bytes 184328 | tf_op jit(solution)/shard_map/ppermute | solution.py:532
  41.3 12.6 %collective-permute-start.10 = (f32[15,8,128]{2,1,0:T(8,128)S(1)}, f32[15,8,128]{2,1,0:T(8,128)S(1)}, u32[]{:S(2)}, u32[]{:S(2)}) collective-permute-start(f32[15,8,128]{2,1,0:T(8,128)S(1)} %get-tuple-element.42.main), channel_id=1, source_target_pairs={{0,32},{32,0},{16,48},{48,16},{64,96},{96,64},{80,112},{112,80},{1... | collective-permute-start | bytes 184328 | tf_op jit(solution)/shard_map/ppermute | solution.py:532

commit v3 on v2

v3 whole, which is shorter than its diff:
```python
import jax
import jax.numpy as jnp
from jax import lax
from jax.experimental import pallas as pl
from jax.experimental.pallas import tpu as pltpu
from jax.sharding import PartitionSpec as P

OMEGA = 0.8
F32 = jnp.float32
LANES = 128


def roll(values, shift, dim):
    return pltpu.roll(values, shift % values.shape[dim], dim)


def lane_of(values):
    return lax.broadcasted_iota(jnp.int32, values.shape, values.ndim - 1)


def row_of(values):
    return lax.broadcasted_iota(jnp.int32, values.shape, values.ndim - 2)


def bit_of(values, bit):
    return ((lane_of(values) >> bit) & 1) == 1


def pair(values, bit):
    step, dim = 1 << bit, values.ndim - 1
    other = jnp.where(bit_of(values, bit), roll(values, step, dim), roll(values, -step, dim))
    return values + other


def keep(values, bit, want):
    step, dim = 1 << bit, values.ndim - 1
    if want:
        return jnp.where(bit_of(values, bit), values, roll(values, -step, dim))
    return jnp.where(bit_of(values, bit), roll(values, step, dim), values)


def spread(values, which, bits):
    for bit in range(bits):
        values = keep(values, bit, (which >> bit) & 1)
    return values


def relax_factor(diag):
    good = diag > 0.0
    return jnp.where(good, OMEGA / jnp.where(good, diag, 1.0), 0.0)


def loop(first, last, step, body, unroll=4):
    count = (last - first + 1) // step
    assert count * step == last - first + 1
    trips = count // unroll

    def run(index, carry):
        for k in range(unroll):
            body(first + (index * unroll + k) * step)
        return carry

    if trips > 1:
        lax.fori_loop(0, trips, run, 0)
    else:
        trips = 0
    for k in range(trips * unroll, count):
        body(first + k * step)


def beside(vals, faces, plane, count, level, rows):
    fx, fy, fz = faces
    shift = 1 << level
    here = pl.ds(plane, count)
    v = vals[here, rows]
    y_face, z_face = fy[here, rows], fz[here, rows]
    total = fx[here, rows] * vals[pl.ds(plane - 1, count), rows]
    total = total + fx[pl.ds(plane + 1, count), rows] * vals[pl.ds(plane + 1, count), rows]
    total = total + y_face * roll(v, 1, 1) + roll(y_face * v, -1, 1)
    total = total + z_face * roll(v, shift, 2) + roll(z_face * v, -shift, 2)
    return v, total


def sweep(out, vals, side, faces, weight, first, last, step, level, unroll=4, rows=slice(None)):
    def body(plane):
        v, total = beside(vals, faces, plane, step, level, rows)
        here = pl.ds(plane, step)
        out[here, rows] = (1.0 - OMEGA) * v + weight[here, rows] * (side[here, rows] + total)

    loop(first, last, step, body, unroll)


def remains(out, vals, side, faces, diag, first, last, step, level, unroll=4, rows=slice(None)):
    def body(plane):
        v, total = beside(vals, faces, plane, step, level, rows)
        here = pl.ds(plane, step)
        out[here, rows] = side[here, rows] - diag[here, rows] * v + total

    loop(first, last, step, body, unroll)


def block_sum(ref, plane, start, count):
    even, odd = pl.ds(start, count, stride=2), pl.ds(start + 1, count, stride=2)
    low = ref[plane, even, :] + ref[plane, odd, :]
    return low + (ref[plane + 1, even, :] + ref[plane + 1, odd, :])


def coarse_stencil(faces, diag, plane, start, count, level):
    fx, fy, fz = faces
    even, odd = pl.ds(start, count, stride=2), pl.ds(start + 1, count, stride=2)
    x_low = fx[plane, even, :] + fx[plane, odd, :]
    x_mid = fx[plane + 1, even, :] + fx[plane + 1, odd, :]
    y_low = fy[plane, even, :] + fy[plane + 1, even, :]
    y_mid = fy[plane, odd, :] + fy[plane + 1, odd, :]
    z_sum = block_sum(fz, plane, start, count)
    d_sum = block_sum(diag, plane, start, count)
    d_new = pair(d_sum - 2.0 * (x_mid + y_mid), level) - 2.0 * keep(z_sum, level, 1)
    return pair(x_low, level), pair(y_low, level), keep(z_sum, level, 0), d_new


def call(body, outs, scratch, limit, flops, *args, space=pltpu.VMEM):
    nbytes = sum(4 * a.size for a in args) + sum(4 * o.size for o in outs)
    return pl.pallas_call(
        body,
        out_shape=outs,
        in_specs=[pl.BlockSpec(memory_space=space)] * len(args),
        out_specs=[pl.BlockSpec(memory_space=pltpu.VMEM)] * len(outs),
        scratch_shapes=scratch,
        compiler_params=pltpu.CompilerParams(vmem_limit_bytes=limit << 20),
        cost_estimate=pl.CostEstimate(flops=flops, bytes_accessed=nbytes, transcendentals=0),
    )(*args)


def array(*shape):
    return jax.ShapeDtypeStruct(shape, F32)


def y_strips_kernel(eps, src, scr, xa, xb, first, second):
    x_even = is_even("gx", 1)
    y_even = is_even("gy", 1)

    def fill(up, down, xl, xr):
        at = 0
        for own, start, wide in ((eps, 0, 9), (src, 10, 8), (scr, 19, 8)):
            for part, low, count in ((xl, start + 1, wide), (own, 0, 16), (xr, start, wide)):
                up[at : at + count] = part[low : low + count, 8:16]
                down[at : at + count] = part[low : low + count, 0:8]
                at += count
        edges = [(xl, 9)] + [(eps, k) for k in range(16)] + [(xr, 0)]
        edges += [(src, k) for k in range(16)] + [(scr, k) for k in range(16)]
        for k, (part, plane) in enumerate(edges):
            tile, row = 98 + k // 4, 2 * (k % 4)
            up[tile, row : row + 2] = part[plane, 6:8]
            down[tile, row : row + 2] = part[plane, 8:10]

    for x_want, (xl, xr) in ((True, (xb, xa)), (False, (xa, xb))):
        for y_want, (up, down) in ((True, (first, second)), (False, (second, first))):
            pl.when((x_even == x_want) & (y_even == y_want))(
                lambda up=up, down=down, xl=xl, xr=xr: fill(up, down, xl, xr)
            )


def down_kernel(
    eps, src, scr, xa, xb, ya, yb,
    u0_out, fx0_out, fy0_out, fz0_out, w0_out, r0_out,
    fx1, fy1, fz1, w1, l1_own, s2, b2, ship_a, ship_b,
    e, b, s, fx, fy, fz, w, d, ua, ub, b1, d1, va, vb,
):
    x_even = is_even("gx", 1).astype(jnp.int32)
    y_even = is_even("gy", 1)
    row_a = pl.multiple_of(8 + 24 * y_even.astype(jnp.int32), 8)
    row_b = pl.multiple_of(32 - 24 * y_even.astype(jnp.int32), 8)
    at, edge = 0, 0
    blank = jnp.zeros((8, LANES), F32)
    for ref, own, start, wide, margin in ((e, eps, 0, 10, 1), (b, src, 10, 9, 0), (s, scr, 19, 9, 0)):
        first, planes = 11 - wide, 14 + 2 * wide
        ref[10:26, 16:32] = own[...]
        ref[pl.ds(first - 1 + (27 - first) * x_even, wide), 16:32] = xa[start : start + wide]
        ref[pl.ds(26 - (27 - first) * x_even, wide), 16:32] = xb[start : start + wide]
        ref[first : first + planes, pl.ds(row_a, 8)] = ya[at : at + planes]
        ref[first : first + planes, pl.ds(row_b, 8)] = yb[at : at + planes]
        for plane in (first - 1, first + planes):
            ref[plane, 8:16] = blank
            ref[plane, 32:40] = blank
        for plane in range(first - 1, first + planes + 1):
            if not 10 - margin <= plane < 26 + margin:
                ref[plane, 0:8] = blank

        def fill(below_ref, above_ref, ref=ref, margin=margin, edge=edge):
            for k in range(16 + 2 * margin):
                tile, row = 98 + (edge + k) // 4, 2 * ((edge + k) % 4)
                below, above = below_ref[tile], above_ref[tile]
                rows = row_of(below)
                ref[10 - margin + k, 0:8] = jnp.where(
                    rows < 2, roll(above, -row, 0), jnp.where(rows >= 6, roll(below, 6 - row, 0), 0.0)
                )

        pl.when(y_even)(lambda fill=fill: fill(yb, ya))
        pl.when(jnp.logical_not(y_even))(lambda fill=fill: fill(ya, yb))
        at += planes
        edge += 16 + 2 * margin

    def stencil(plane):
        cells = e[pl.ds(plane - 1, 4)]
        centre = cells[1:3]
        x_face = 0.5 * (cells[0:3] + cells[1:4])
        y_face = 0.5 * (centre + roll(centre, 1, 1))
        lanes = lane_of(centre)
        z_face = jnp.where(lanes == 0, 0.0, 0.5 * (centre + roll(centre, 1, 2)))
        ends = jnp.where((lanes == 0) | (lanes == LANES - 1), 0.5 * centre, 0.0)
        here = pl.ds(plane, 2)
        screen = s[here]
        diag = x_face[0:2] + x_face[1:3] + y_face + roll(y_face, -1, 1)
        diag = diag + z_face + roll(z_face, -1, 2) + screen + ends
        diag = jnp.where(screen > 0.0, diag, 0.0)
        weight = relax_factor(diag)
        fx[pl.ds(plane, 3)] = x_face
        fy[here] = y_face
        fz[here] = z_face
        d[here] = diag
        w[here] = weight
        ua[here] = weight * b[here]

    loop(1, 34, 2, stencil, 8)
    faces = (fx, fy, fz)
    sweep(ub, ua, b, faces, w, 2, 33, 2, 0, 8)
    sweep(ua, ub, b, faces, w, 3, 32, 2, 0, 8, slice(8, 40))
    remains(ub, ua, b, faces, d, 4, 31, 2, 0, 8, slice(8, 40))
    u0_out[...] = ua[10:26, 16:32]

    def keep_window(plane):
        for out, ref in ((fx0_out, fx), (fy0_out, fy), (fz0_out, fz), (w0_out, w), (r0_out, ub)):
            out[plane, 8:24] = ref[plane + 7, 16:32]
            high, low = ref[plane + 7, 32:40], ref[plane + 7, 8:16]
            out[plane, 0:8] = jnp.where(row_of(high) < 4, high, low)

    loop(0, 21, 1, keep_window, 8)

    def to_level1(plane):
        x_face, y_face, z_face, diag = coarse_stencil(faces, d, 2 * plane, 0, 20, 0)
        fx1[plane, 0:20] = x_face
        fy1[plane, 0:20] = y_face
        fz1[plane, 0:20] = z_face
        fy1[plane, 20:21] = y_face[0:1]
        d1[plane, 0:20] = diag
        w1[plane, 0:20] = relax_factor(diag)

    for ref in (fx1, fy1, fz1, w1, d1, b1):
        ref[:, 16:24] = jnp.zeros((18, 8, LANES), F32)
    loop(1, 16, 1, to_level1, 8)
    even, odd = pl.ds(0, 20, stride=2), pl.ds(1, 20, stride=2)
    fx1[17, 0:20] = pair(fx[34, even, :] + fx[34, odd, :], 0)

    def side1(plane):
        side = pair(block_sum(ub, 2 * plane, 0, 20), 0)
        b1[plane, 0:20] = side
        va[plane, 0:20] = w1[plane, 0:20] * side

    loop(2, 15, 1, side1, 8)
    va[:, 20:24] = jnp.zeros((18, 4, LANES), F32)
    faces1 = (fx1, fy1, fz1)
    sweep(vb, va, b1, faces1, w1, 3, 14, 4, 1)
    sweep(va, vb, b1, faces1, w1, 4, 13, 2, 1)
    remains(vb, va, b1, faces1, d1, 5, 12, 4, 1)

    own = jnp.where(bit_of(va[5:13, 8:16], 0), va[5:13, 8:16], vb[5:13, 8:16])
    l1_own[...] = own
    quarter = lax.broadcasted_iota(jnp.int32, (8, LANES), 1) & 3
    for m in range(8):
        parts = coarse_stencil(faces1, d1, 1 + 2 * m, 4, 8, 1)
        stack = parts[3]
        for q in range(3):
            stack = jnp.where(quarter == q, parts[q], stack)
        s2[m] = stack
    packed = jnp.zeros((4, LANES), F32)
    for k in range(4):
        packed = jnp.where(quarter[0:4] == k, pair(block_sum(vb, 5 + 2 * k, 8, 4), 1), packed)
    b2[0, 0:4] = packed
    b2[0, 4:8] = jnp.zeros((4, LANES), F32)
    for ship in (ship_a, ship_b):
        ship[0:8] = s2[...]
        ship[8:9] = b2[...]
    for t in range(4):
        first, second = l1_own[2 * t], l1_own[2 * t + 1]
        low = row_of(first) < 4
        up = jnp.where(low, roll(first, -4, 0), second)
        down = jnp.where(low, first, roll(second, 4, 0))
        ship_a[9 + t] = jnp.where(y_even, up, down)
        ship_b[9 + t] = jnp.where(y_even, down, up)


def window_kernel(s2, b2, l1_own, a1a, a1b, s2_wide, b2_wide, l1_ext, ship_a, ship_b):
    y_even = is_even("gy", 1)
    rows = lax.broadcasted_iota(jnp.int32, (8, LANES), 0)

    def join(below, above):
        for m in range(8):
            s2_wide[2 * m] = jnp.where(rows < 6, below[m], roll(s2[m], 4, 0))
            s2_wide[2 * m + 1] = jnp.where(rows < 2, roll(s2[m], -4, 0), above[m])
        b2_wide[0] = jnp.where(rows < 6, roll(below[8], 2, 0), roll(b2[0], 6, 0))
        b2_wide[1] = jnp.where(rows < 2, roll(b2[0], -2, 0), roll(above[8], 2, 0))
        for k in range(8):
            t, turn = 9 + k // 2, 4 * (k % 2)
            l1_ext[2 * k] = jnp.where(rows < 4, roll(above[t], -turn, 0), roll(below[t], 4 - turn, 0))
            l1_ext[2 * k + 1] = l1_own[k]

    pl.when(y_even)(lambda: join(a1b, a1a))
    pl.when(jnp.logical_not(y_even))(lambda: join(a1a, a1b))
    up = is_even("gx", 1).astype(jnp.int32)
    for ship, way in ((ship_a, up), (ship_b, 1 - up)):
        ship[0:12] = s2_wide[pl.ds(4 - 4 * way, 12)]
        ship[12:14] = b2_wide[...]
        ship[14:22] = l1_ext[pl.ds(8 * way, 8)]


def level2_kernel(
    s2_wide, b2_wide, c1a, c1b,
    fx, fy, fz, w, payload,
    d, b, ua, ub, piece,
):
    up = is_even("gx", 1).astype(jnp.int32)
    b[0:2] = jnp.zeros((2, 16, LANES), F32)
    b[14:16] = jnp.zeros((2, 16, LANES), F32)
    for part, tile, first, count in ((s2_wide, 4, 6, 4), (c1a, 0, 10 * up, 6), (c1b, 0, 10 - 10 * up, 6)):
        for k in range(count):
            tiles = jnp.concatenate([part[tile + 2 * k], part[tile + 2 * k + 1]], axis=0)
            fx[first + k] = spread(tiles, 0, 2)
            fy[first + k] = spread(tiles, 1, 2)
            fz[first + k] = spread(tiles, 2, 2)
            diag = spread(tiles, 3, 2)
            d[first + k] = diag
            w[first + k] = relax_factor(diag)
    for part, tile, first in ((b2_wide, 0, 6), (c1a, 12, 2 + 8 * up), (c1b, 12, 10 - 8 * up)):
        tiles = jnp.concatenate([part[tile], part[tile + 1]], axis=0)
        for k in range(4):
            b[first + k] = spread(tiles, k, 2)

    def begin(plane):
        here = pl.ds(plane, 4)
        ua[here] = w[here] * b[here]

    loop(0, 15, 4, begin)
    faces = (fx, fy, fz)
    sweep(ub, ua, b, faces, w, 3, 12, 2, 2, 8)
    sweep(ua, ub, b, faces, w, 4, 11, 2, 2, 8)
    remains(ub, ua, b, faces, d, 6, 9, 2, 2, 8)

    gx, gy = lax.axis_index("gx"), lax.axis_index("gy")
    rows = lax.broadcasted_iota(jnp.int32, (2, LANES), 0)
    slot = lax.broadcasted_iota(jnp.int32, (2, LANES), 1) & 7
    lines = [jnp.zeros((2, LANES), F32) for _ in range(3)]
    for x in range(2):
        parts = coarse_stencil(faces, d, 6 + 2 * x, 6, 2, 2)
        x_face, y_face, z_face, diag = parts
        if x == 0:
            x_face = jnp.where(gx == 0, 0.0, x_face)
        y_face = jnp.where((gy == 0) & (rows == 0), 0.0, y_face)
        side = pair(block_sum(ub, 6 + 2 * x, 6, 2), 2)
        for index, values in enumerate((x_face, y_face, z_face, diag, side)):
            chosen = slot == x + 2 * (index % 2) + 4 * rows
            lines[index // 2] = jnp.where(chosen, values, lines[index // 2])
    for k in range(3):
        piece[k : k + 1] = jnp.sum(lines[k], axis=0, keepdims=True)
    quarter = lax.broadcasted_iota(jnp.int32, (4, LANES), 1) & 3
    for ref, row in ((ub, 3), (ua, 7)):
        stack = ref[9, 6:10]
        for k in range(3):
            stack = jnp.where(quarter == k, ref[6 + k, 6:10], stack)
        piece[row : row + 4] = stack
    piece[11:12] = jnp.zeros((1, LANES), F32)
    whole = piece[0:12]
    for k in range(payload.shape[0] // 12):
        payload[12 * k : 12 * k + 12] = whole


def relay_kernel(got, payload, around, piece):
    count = got.shape[0] // 12
    gy = lax.axis_index("gy")
    around[0:24] = jnp.zeros((24, LANES), F32)
    around[24 : 24 + 12 * count] = got[...]
    around[24 + 12 * count : 48 + 12 * count] = jnp.zeros((24, LANES), F32)
    piece[0:count] = got[pl.ds(0, count, stride=12), :]
    piece[count + 24 : 2 * count + 24] = got[pl.ds(1, count, stride=12), :]
    even, odd = got[pl.ds(2, count // 2, stride=24), :], got[pl.ds(14, count // 2, stride=24), :]
    piece[2 * count + 24 :] = jnp.where(bit_of(even, 1), roll(odd, 2, 1), even)
    for target, start, least, most in ((count, 3, -5, 9), (count + 14, 7, -3, 7)):
        for block in range(-2, 3):
            low, high = max(4 * block, least), min(4 * block + 4, most)
            if low < high:
                line = 12 * (gy + block + 2) + start + low - 4 * block
                piece[target + low - least : target + high - least] = around[pl.ds(line, high - low), :]
    whole = piece[...]
    size = piece.shape[0]
    for k in range(payload.shape[0] // size):
        payload[size * k : size * k + size] = whole


def piece_rows(n_y):
    return 5 * n_y // 2 + 24


def level3_beside(v, faces, stride):
    x_face, y_face, z_face = faces
    x_slot, y_bit = lane_of(v) & 3, bit_of(v, 2)
    low = jnp.where(x_slot == 0, roll(roll(v, -3, 1), stride, 0), roll(v, 1, 1))
    product = x_face * v
    high = jnp.where(x_slot == 3, roll(roll(product, 3, 1), -stride, 0), roll(product, -1, 1))
    total = x_face * low + high
    low = jnp.where(y_bit, roll(v, 4, 1), roll(roll(v, -4, 1), 1, 0))
    product = y_face * v
    high = jnp.where(y_bit, roll(roll(product, 4, 1), -1, 0), roll(product, -4, 1))
    total = total + y_face * low + high
    return total + z_face * roll(v, 8, 1) + roll(z_face * v, -8, 1)


def level4_beside(v, x_face, y_face, z_face, stride):
    x_bit = bit_of(v, 1)
    low = jnp.where(x_bit, roll(v, 2, 1), roll(roll(v, -2, 1), stride, 0))
    product = x_face * v
    high = jnp.where(x_bit, roll(roll(product, 2, 1), -stride, 0), roll(product, -2, 1))
    total = x_face * low + high
    total = total + y_face * roll(v, 1, 0) + roll(y_face * v, -1, 0)
    return total + z_face * roll(v, 16, 1) + roll(z_face * v, -16, 1)


def coarse_levels(got, b3, n_x, n_y):
    size = piece_rows(n_y)

    def lines(start, count):
        pair_of = []
        for parity in range(2):
            parts = [got[pl.ds((2 * a + parity) * size + start, count), :] for a in range(n_x // 2)]
            pair_of.append(jnp.concatenate(parts, axis=0))
        return pair_of

    fields = []
    for start in (0, n_y + 24):
        even, odd = lines(start, n_y)
        upper = bit_of(even, 1)
        fields.append(jnp.where(upper, roll(odd, 2, 1), even))
        fields.append(jnp.where(upper, odd, roll(even, -2, 1)))
    even, odd = lines(2 * n_y + 24, n_y // 2)
    upper = bit_of(even, 1)
    half = n_x // 2 * n_y // 2
    b3[pl.ds(0, half, stride=2), :] = jnp.where(upper, roll(odd, 2, 1), even)
    b3[pl.ds(1, half, stride=2), :] = jnp.where(upper, odd, roll(even, -2, 1))
    fields.append(b3[...])
    faces, diag, side = fields[0:3], fields[3], fields[4]
    weight = relax_factor(diag)

    def sweep3(v, side):
        return (1.0 - OMEGA) * v + weight * (side + level3_beside(v, faces, n_y))

    u = weight * side
    u = sweep3(u, side)
    u = sweep3(u, side)
    r = side - diag * u + level3_beside(u, faces, n_y)

    x_sum, y_sum, z_sum = pair(pair(faces[0], 2), 3), pair(pair(faces[1], 0), 3), pair(pair(faces[2], 0), 2)
    x4, y4, z4 = keep(x_sum, 0, 0), keep(y_sum, 2, 0), keep(z_sum, 3, 0)
    inner = keep(x_sum, 0, 1) + keep(y_sum, 2, 1) + keep(z_sum, 3, 1)
    w4 = relax_factor(pair(pair(pair(diag, 0), 2), 3) - 2.0 * inner)
    b4 = pair(pair(pair(r, 0), 2), 3)
    v = w4 * b4
    for _ in range(5):
        v = (1.0 - OMEGA) * v + w4 * (b4 + level4_beside(v, x4, y4, z4, n_y))
    for _ in range(3):
        v = sweep3(v, r)
    return u + v


def up_kernel(
    got, u0, fx0, fy0, fz0, w0, r0,
    fx1, fy1, fz1, w1, l1_ext, c1a, c1b,
    fx2, fy2, fz2, w2,
    out,
    u3, b3, e3, r2, u2, ea2, eb2, r1, u1, ea1, eb1, ea0, eb0,
):
    gx, gy = lax.axis_index("gx"), lax.axis_index("gy")
    n_x, n_y = lax.axis_size("gx"), lax.axis_size("gy")
    size = piece_rows(n_y)
    for block in range(5):
        device = jnp.clip(gx + block - 2, 0, n_x - 1)
        for ref, line in ((r2, n_y - 1), (u2, n_y + 11)):
            tiles = got[pl.ds(device * size + line, 16), :]
            for k in range(4):
                if 0 <= 4 * block - 2 + k < 16:
                    ref[4 * block - 2 + k] = spread(tiles, k, 2)

    u3[48 : 48 + n_x // 2 * n_y] = coarse_levels(got, b3, n_x, n_y)
    for block in range(5):
        device = gx + block
        line = 48 + (lax.div(device, 2) - 1) * n_y + gy - 2
        lower = u3[pl.ds(line, 8), :]
        lower = jnp.where(lax.rem(device, 2) == 1, keep(lower, 1, 1), keep(lower, 1, 0))
        for x in range(2):
            for y in range(2):
                values = keep(keep(lower, 0, x), 2, y)
                e3[2 * block + x, pl.ds(y, 5, stride=2), :] = values[0:5]

    for plane in range(16):
        values = e3[plane // 2 + 1][1:9]
        for k in range(2):
            ea2[plane, pl.ds(k, 8, stride=2), :] = values

    def inside(values, weight, first, last, step):
        def body(plane):
            here = pl.ds(plane, step)
            values[here] = jnp.where(weight[here] > 0.0, values[here], 0.0)

        loop(first, last, step, body)

    inside(ea2, w2, 0, 15, 4)
    faces = (fx2, fy2, fz2)
    sweep(eb2, ea2, r2, faces, w2, 1, 14, 2, 2)
    sweep(ea2, eb2, r2, faces, w2, 2, 13, 4, 2)
    sweep(eb2, ea2, r2, faces, w2, 3, 12, 2, 2)

    even = is_even("gx", 1).astype(jnp.int32)
    for part, first, tile, count in ((c1a, 1 + 12 * even, 14, 4), (l1_ext, 5, 0, 8), (c1b, 13 - 12 * even, 14, 4)):
        for k in range(count):
            sides, own = part[tile + 2 * k], part[tile + 2 * k + 1]
            for ref, which in ((r1, 0), (u1, 1)):
                edge = keep(sides, 0, which)
                ref[first + k, 0:8] = edge
                ref[first + k, 8:16] = keep(own, 0, which)
                ref[first + k, 16:24] = edge

    for plane in range(3, 13):
        values = (u2[plane] + eb2[plane])[3:13]
        for k in range(2):
            target = 2 * plane - 7 + k
            if 0 <= target < 18:
                ea1[target, pl.ds(2, 10, stride=2), :] = values
                ea1[target, pl.ds(3, 10, stride=2), :] = values
    inside(ea1, w1, 1, 16, 4)
    faces = (fx1, fy1, fz1)
    for plane in (0, 17):
        ea1[plane] = jnp.where(edge_inside(gx, plane), ea1[plane], 0.0)
    sweep(eb1, ea1, r1, faces, w1, 1, 16, 4, 1)
    sweep(ea1, eb1, r1, faces, w1, 2, 15, 2, 1)
    sweep(eb1, ea1, r1, faces, w1, 3, 14, 4, 1)

    for plane in range(3, 15):
        values = u1[plane] + eb1[plane]
        for k in range(2):
            target = 3 + 2 * (plane - 5) + k
            if 0 <= target < 22:
                for parity in range(2):
                    ea0[target, pl.ds(4 + parity, 10, stride=2), :] = values[6:16]
                    ea0[target, pl.ds(parity, 2, stride=2), :] = values[16:18]
    inside(ea0, w0, 0, 21, 2)
    faces = (fx0, fy0, fz0)
    sweep(eb0, ea0, r0, faces, w0, 1, 20, 2, 0)
    sweep(ea0, eb0, r0, faces, w0, 2, 19, 2, 0)

    def last(plane):
        v, total = beside(ea0, faces, plane, 2, 0, slice(None))
        here = pl.ds(plane, 2)
        values = (1.0 - OMEGA) * v + w0[here] * (r0[here] + total)
        out[pl.ds(plane - 3, 2)] = u0[pl.ds(plane - 3, 2)] + values[:, 8:24]

    loop(3, 18, 2, last)


def edge_inside(gx, plane):
    where = 8 * gx + plane - 5
    return (where >= 0) & (where < 8 * lax.axis_size("gx"))


def swapped(values, axis, step, odd):
    pairs = []
    for k in range(lax.axis_size(axis) - step):
        if (k // step) % 2 == odd:
            pairs += [(k, k + step), (k + step, k)]
    return lax.ppermute(values, axis, pairs)


def is_even(axis, step):
    return lax.rem(lax.div(lax.axis_index(axis), step), 2) == 0


def local(source, dielectric, screening):
    fields = (dielectric, source, screening)
    even = is_even("gx", 1).astype(jnp.int32)

    def strip(way):
        parts = [lax.dynamic_slice_in_dim(f, way * (16 - n), n, 0) for f, n in zip(fields, (10, 9, 9))]
        return jnp.concatenate(parts, axis=0)

    xa, xb = strip(even), strip(1 - even)
    xa, xb = swapped(xa, "gx", 1, 0), swapped(xb, "gx", 1, 1)
    ya, yb = call(y_strips_kernel, [array(111, 8, LANES)] * 2, [], 2, 10_000, *fields, xa, xb)
    ya, yb = swapped(ya, "gy", 1, 0), swapped(yb, "gy", 1, 1)

    big, mid = pltpu.VMEM((36, 40, LANES), F32), pltpu.VMEM((18, 24, LANES), F32)
    outs = [array(16, 16, LANES)] + [array(22, 24, LANES)] * 5 + [array(18, 24, LANES)] * 4
    outs += [array(8, 8, LANES), array(8, 8, LANES), array(1, 8, LANES), array(13, 8, LANES), array(13, 8, LANES)]
    made = call(down_kernel, outs, [big] * 10 + [mid] * 4, 12, 10_000_000, *fields, xa, xb, ya, yb)
    fine, level1, (l1_own, s2, b2, sa, sb) = made[0:6], made[6:10], made[10:15]

    a1a, a1b = swapped(sa, "gy", 1, 0), swapped(sb, "gy", 1, 1)
    outs = [array(16, 8, LANES), array(2, 8, LANES), array(16, 8, LANES), array(22, 8, LANES), array(22, 8, LANES)]
    s2, b2, l1_ext, sa, sb = call(window_kernel, outs, [], 2, 10_000, s2, b2, l1_own, a1a, a1b)
    c1a, c1b = swapped(sa, "gx", 1, 0), swapped(sb, "gx", 1, 1)

    n_x, n_y = lax.axis_size("gx"), lax.axis_size("gy")
    two, size = pltpu.VMEM((16, 16, LANES), F32), piece_rows(n_y)
    outs = [array(16, 16, LANES)] * 4 + [array(12 * n_y, LANES)]
    scratch = [two] * 4 + [pltpu.VMEM((16, LANES), F32)]
    *level2, payload = call(level2_kernel, outs, scratch, 4, 5_000_000, s2, b2, c1a, c1b)

    payload = payload.reshape(6 * n_y, 2, LANES)
    got = lax.all_to_all(payload, "gy", 0, 0, tiled=True).reshape(12 * n_y, LANES)
    scratch = [pltpu.VMEM((12 * n_y + 48, LANES), F32), pltpu.VMEM((size, LANES), F32)]
    (payload,) = call(relay_kernel, [array(n_x * size, LANES)], scratch, 2, 10_000, got)
    got = lax.all_to_all(payload, "gx", 0, 0, tiled=True)

    scratch = [pltpu.VMEM((n_x // 2 * n_y + extra, LANES), F32) for extra in (96, 0)]
    scratch += [pltpu.VMEM((12, 16, LANES), F32)]
    scratch += [two] * 4 + [mid] * 4 + [pltpu.VMEM((22, 24, LANES), F32)] * 2
    (result,) = call(
        up_kernel, [array(16, 16, LANES)], scratch, 6, 10_000_000,
        got, *fine, *level1, l1_ext, c1a, c1b, *level2,
    )
    return result


def solution(mesh):
    spec = P("gx", "gy", None)
    return jax.shard_map(local, mesh=mesh, in_specs=(spec,) * 3, out_specs=spec, check_vma=False)
```

time: 93 us -> 86.2 us (0.927)
  starting transfers between devices: 27.5 us -> 12.9 us
  blocking collectives: 29.2 us -> 41.6 us
  Pallas kernels: 13.5 us -> 11.5 us
  local copies, waits for them, and re-layouts: 2.72 us -> 1.06 us
  waiting for transfers between devices: 19.1 us -> 17.9 us
    ppermute x12 -> x8, starting transfers between devices: 27.5 us -> 12.9 us  [swapped(): return lax.ppermute(values, axis, pairs)]
    all_to_all x1 -> x2, blocking collectives: 29.2 us -> 41.6 us  [the longest x1 25 us: local(): got = lax.all_to_all(payload, 'gx', 0, 0, tiled=True)]
    unnamed x12 -> x6, local copies, waits for them, and re-layouts: 2.72 us -> 0.06 us
    pallas_call x6, Pallas kernels: 13.5 us -> 11.5 us  [call(): pl.pallas_call(body, out_shape=outs, in_specs=[pl.BlockSpec(memory_space=...]
    ppermute x12 -> x8, waiting for transfers between devices: 19.1 us -> 17.9 us  [swapped(): return lax.ppermute(values, axis, pairs)]
    dynamic_slice x0 -> x2, local copies, waits for them, and re-layouts: none -> 1.01 us  [strip(): lax.dynamic_slice_in_dim(f, way * (16 - n), n, 0)]
  transfers between devices with their start and end apart: 12 -> 8, of which waited for: 5 -> 4; matrix products, arithmetic and copies ran while one was open for 0% -> 0% of each run, Pallas kernels for 0% -> 0%
where the time goes in v3:
time: 86.2 us; the launch traced here: 85.2 us
  blocking collectives  41.6 us (48%)
  waiting for transfers between devices  17.9 us (21%)
  starting transfers between devices  12.9 us (15%)
  Pallas kernels  11.5 us (13%)
  local copies, waits for them, and re-layouts  1.06 us (1%)
    all_to_all x1, blocking collectives, local(): got = lax.all_to_all(payload, 'gx', 0, 0, tiled=True)  25 us
    ppermute x8, waiting for transfers between devices, swapped(): return lax.ppermute(values, axis, pairs)  17.9 us
    all_to_all x1, blocking collectives, local(): lax.all_to_all(payload, 'gy', 0, 0, tiled=True).reshape(12 * n_y, LANES)  16.6 us
    ppermute x8, starting transfers between devices, swapped(): return lax.ppermute(values, axis, pairs)  12.9 us
    pallas_call x6, Pallas kernels, call(): pl.pallas_call(body, out_shape=outs, in_specs=[pl.BlockSpec(memory_space=...  11.5 us
  transfers between devices with their start and end apart: 8, of which 4 were waited for; matrix products, arithmetic and copies ran while one was open for 0% of the time, Pallas kernels for 0%

profile of v3, /device:TPU:32, one launch (start us, length us, event | category | flops | bytes accessed | tf_op | source)
XLA Modules:
  0.0 85.2 jit_solution(13781947289383173154)
XLA Ops:
  0.0 0.0 copy-start.1
  0.0 0.0 copy-start.2
  0.0 1.0 %constant_dynamic-slice_fusion.2 = (f32[10,16,128]{2,1,0:T(8,128)S(1)}, f32[10,16,128]{2,1,0:T(8,128)S(1)}) fusion(f32[16,16,128]{2,1,0:T(8,128)} %eps.3, s32[]{:T(128)S(6)} %select_n.4, s32[]{:T(128)S(6)} %mul.14), kind=kLoop, calls=%fused_computation.4 | loop fusion | bytes 327688 | tf_op jit(solution)/shard_map/dynamic_slice | solution.py:588
  1.0 0.0 copy-done.1
  1.0 0.0 copy-done.2
  1.1 1.7 %collective-permute-start = (f32[28,16,128]{2,1,0:T(8,128)S(1)}, f32[28,16,128]{2,1,0:T(8,128)S(1)}, u32[]{:S(2)}, u32[]{:S(2)}) collective-permute-start(f32[28,16,128]{2,1,0:T(8,128)S(1)} %pad_maximum_fusion), channel_id=1, source_target_pairs={{0,16},{16,0},{32,48},{48,32},{64,80},{80,64},{96,112},{112,96},{1... | collective-permute-start | bytes 688136 | tf_op jit(solution)/shard_map/ppermute | solution.py:576
  2.8 0.0 copy-start
  2.8 0.8 collective-permute-start.1
  3.6 4.9 %collective-permute-done.xa = f32[28,16,128]{2,1,0:T(8,128)S(1)} collective-permute-done((f32[28,16,128]{2,1,0:T(8,128)S(1)}, f32[28,16,128]{2,1,0:T(8,128)S(1)}, u32[]{:S(2)}, u32[]{:S(2)}) %collective-permute-start) | collective-permute-done | bytes 229408 | tf_op jit(solution)/shard_map/ppermute | solution.py:576
  8.5 0.0 collective-permute-done.1.xb
  8.5 0.0 copy-done
  8.5 0.1 shard_map.37
  8.6 0.1 collective-permute-start.2
  8.7 2.5 %collective-permute-start.3 = (f32[111,8,128]{2,1,0:T(8,128)S(1)}, f32[111,8,128]{2,1,0:T(8,128)S(1)}, u32[]{:S(2)}, u32[]{:S(2)}) collective-permute-start(f32[111,8,128]{2,1,0:T(8,128)S(1)} %get-tuple-element.33), channel_id=1, source_target_pairs={{1,2},{2,1},{3,4},{4,3},{5,6},{6,5},{7,8},{8,7},{9,10},{10,9},{11,... | collective-permute-start | bytes 1363976 | tf_op jit(solution)/shard_map/ppermute | solution.py:576
  11.3 0.0 collective-permute-done.2.ya
  11.3 7.2 %collective-permute-done.3.yb = f32[111,8,128]{2,1,0:T(8,128)S(1)} collective-permute-done((f32[111,8,128]{2,1,0:T(8,128)S(1)}, f32[111,8,128]{2,1,0:T(8,128)S(1)}, u32[]{:S(2)}, u32[]{:S(2)}) %collective-permute-start.3) | collective-permute-done | bytes 454688 | tf_op jit(solution)/shard_map/ppermute | solution.py:576
  18.5 3.5 %shard_map.38 = (f32[16,16,128]{2,1,0:T(8,128)S(1)}, f32[22,24,128]{2,1,0:T(8,128)S(1)}, f32[22,24,128]{2,1,0:T(8,128)S(1)}, f32[22,24,128]{2,1,0:T(8,128)S(1)},...) custom-call(f32[16,16,128]{2,1,0:T(8,128)S(1)} %copy-done, ...), custom_call_target="tpu_custom_call" | custom-call | flops 10000000 | bytes 4304896 | tf_op jit(solution)/shard_map/pallas_call | solution.py:123
  22.0 0.6 collective-permute-start.4
  22.6 2.0 %collective-permute-start.5 = (f32[13,8,128]{2,1,0:T(8,128)S(1)}, f32[13,8,128]{2,1,0:T(8,128)S(1)}, u32[]{:S(2)}, u32[]{:S(2)}) collective-permute-start(f32[13,8,128]{2,1,0:T(8,128)S(1)} %get-tuple-element.38), channel_id=1, source_target_pairs={{1,2},{2,1},{3,4},{4,3},{5,6},{6,5},{7,8},{8,7},{9,10},{10,9},{11,... | collective-permute-start | bytes 159752 | tf_op jit(solution)/shard_map/ppermute | solution.py:576
  24.6 0.0 collective-permute-done.4.a1a
  24.6 3.4 %collective-permute-done.5.a1b = f32[13,8,128]{2,1,0:T(8,128)S(1)} collective-permute-done((f32[13,8,128]{2,1,0:T(8,128)S(1)}, f32[13,8,128]{2,1,0:T(8,128)S(1)}, u32[]{:S(2)}, u32[]{:S(2)}) %collective-permute-start.5) | collective-permute-done | bytes 53280 | tf_op jit(solution)/shard_map/ppermute | solution.py:576
  28.0 4.5 %collective-permute-start.6 = (f32[22,8,128]{2,1,0:T(8,128)S(1)}, f32[22,8,128]{2,1,0:T(8,128)S(1)}, u32[]{:S(2)}, u32[]{:S(2)}) collective-permute-start(f32[22,8,128]{2,1,0:T(8,128)S(1)} %get-tuple-element.41), channel_id=1, source_target_pairs={{0,16},{16,0},{32,48},{48,32},{64,80},{80,64},{96,112},{112,96},{1... | collective-permute-start | bytes 270344 | tf_op jit(solution)/shard_map/ppermute | solution.py:576
  32.6 0.7 collective-permute-start.7
  33.2 2.4 %collective-permute-done.6.c1a = f32[22,8,128]{2,1,0:T(8,128)S(1)} collective-permute-done((f32[22,8,128]{2,1,0:T(8,128)S(1)}, f32[22,8,128]{2,1,0:T(8,128)S(1)}, u32[]{:S(2)}, u32[]{:S(2)}) %collective-permute-start.6) | collective-permute-done | bytes 90144 | tf_op jit(solution)/shard_map/ppermute | solution.py:576
  35.7 0.0 collective-permute-done.7.c1b
  35.7 1.0 %shard_map.40 = (f32[16,16,128]{2,1,0:T(8,128)S(1)}, f32[16,16,128]{2,1,0:T(8,128)S(1)}, f32[16,16,128]{2,1,0:T(8,128)S(1)}, f32[16,16,128]{2,1,0:T(8,128)S(1)}, f32[192,128]{1,0:T(8,128)S(1)}) custom-call(f32[16,8,128]{2,1,0:T(8,128)S(1)} %get-tuple-element.39.s2_wide, f32[2,8,128]{2,1,0:T(8,128)S(1)} %get-tuple-element.40.b2_wide, ...), custom_call_target="tpu_custom_call" | custom-call | flops 5000000 | bytes 876544 | tf_op jit(solution)/shard_map/pallas_call | solution.py:123
  36.7 16.6 %all_to_all.16 = f32[96,2,128]{2,1,0:T(2,128)S(1)} all-to-all(f32[96,2,128]{2,1,0:T(2,128)S(1)} %bitcast.7), channel_id=1, replica_groups=mesh['gx'=16,'gy'=16] {'gy'}, dimensions={0} | all-to-all | bytes 196608 | tf_op jit(solution)/shard_map/all_to_all | solution.py:614
  53.3 0.1 shard_map.41
  53.3 25.0 %all_to_all.17 = f32[16,64,128]{2,1,0:T(8,128)S(1)} all-to-all(f32[16,64,128]{2,1,0:T(8,128)S(1)} %bitcast.4), channel_id=1, replica_groups=mesh['gx'=16,'gy'=16] {'gx'}, dimensions={0} | all-to-all | bytes 1048576 | tf_op jit(solution)/shard_map/all_to_all | solution.py:617
  78.4 6.8 %shard_map.42 = f32[16,16,128]{2,1,0:T(8,128)} custom-call(f32[1024,128]{1,0:T(8,128)S(1)} %bitcast.5, f32[16,16,128]{2,1,0:T(8,128)S(1)} %get-tuple-element.44.u0, f32[22,24,128]{2,1,0:T(8,128)S(1)} %get-tuple-element.45.fx0, f32[22,24,128]{2,1,0:T(8,128)S(1)} %get-tuple-element.46.fy0, f32[22,24,128]{2,1,0:T(8,128)S(1)} %get-tuple-element.47.fz0, ...), custom_call_target="tpu_custom_call" | custom-call | flops 10000000 | bytes 3792896 | tf_op jit(solution)/shard_map/pallas_call | solution.py:123
  (4 shorter events, 0.1 us)
Async XLA Ops:
  0.0 1.0 %copy-start.1 = (f32[16,16,128]{2,1,0:T(8,128)S(1)}, f32[16,16,128]{2,1,0:T(8,128)}, u32[]{:S(2)}) copy-start(f32[16,16,128]{2,1,0:T(8,128)} %src.3) | copy-start | bytes 393220
  0.0 1.0 %copy-start.2 = (f32[16,16,128]{2,1,0:T(8,128)S(1)}, f32[16,16,128]{2,1,0:T(8,128)}, u32[]{:S(2)}) copy-start(f32[16,16,128]{2,1,0:T(8,128)} %scr.3) | copy-start | bytes 393220
  1.1 7.4 %collective-permute-start = (f32[28,16,128]{2,1,0:T(8,128)S(1)}, f32[28,16,128]{2,1,0:T(8,128)S(1)}, u32[]{:S(2)}, u32[]{:S(2)}) collective-permute-start(f32[28,16,128]{2,1,0:T(8,128)S(1)} %pad_maximum_fusion), channel_id=1, source_target_pairs={{0,16},{16,0},{32,48},{48,32},{64,80},{80,64},{96,112},{112,96},{1... | collective-permute-start | bytes 688136 | tf_op jit(solution)/shard_map/ppermute | solution.py:576
  2.8 5.8 %copy-start = (f32[16,16,128]{2,1,0:T(8,128)S(1)}, f32[16,16,128]{2,1,0:T(8,128)}, u32[]{:S(2)}) copy-start(f32[16,16,128]{2,1,0:T(8,128)} %eps.3) | copy-start | bytes 393220
  2.8 5.7 %collective-permute-start.1 = (f32[28,16,128]{2,1,0:T(8,128)S(1)}, f32[28,16,128]{2,1,0:T(8,128)S(1)}, u32[]{:S(2)}, u32[]{:S(2)}) collective-permute-start(f32[28,16,128]{2,1,0:T(8,128)S(1)} %pad_maximum_fusion.1), channel_id=1, source_target_pairs={{16,32},{32,16},{48,64},{64,48},{80,96},{96,80},{112,128},{128,112... | collective-permute-start | bytes 688136 | tf_op jit(solution)/shard_map/ppermute | solution.py:576
  8.6 2.6 %collective-permute-start.2 = (f32[111,8,128]{2,1,0:T(8,128)S(1)}, f32[111,8,128]{2,1,0:T(8,128)S(1)}, u32[]{:S(2)}, u32[]{:S(2)}) collective-permute-start(f32[111,8,128]{2,1,0:T(8,128)S(1)} %get-tuple-element.32), channel_id=1, source_target_pairs={{0,1},{1,0},{2,3},{3,2},{4,5},{5,4},{6,7},{7,6},{8,9},{9,8},{10,11... | collective-permute-start | bytes 1363976 | tf_op jit(solution)/shard_map/ppermute | solution.py:576
  8.7 9.8 %collective-permute-start.3 = (f32[111,8,128]{2,1,0:T(8,128)S(1)}, f32[111,8,128]{2,1,0:T(8,128)S(1)}, u32[]{:S(2)}, u32[]{:S(2)}) collective-permute-start(f32[111,8,128]{2,1,0:T(8,128)S(1)} %get-tuple-element.33), channel_id=1, source_target_pairs={{1,2},{2,1},{3,4},{4,3},{5,6},{6,5},{7,8},{8,7},{9,10},{10,9},{11,... | collective-permute-start | bytes 1363976 | tf_op jit(solution)/shard_map/ppermute | solution.py:576
  22.0 2.6 %collective-permute-start.4 = (f32[13,8,128]{2,1,0:T(8,128)S(1)}, f32[13,8,128]{2,1,0:T(8,128)S(1)}, u32[]{:S(2)}, u32[]{:S(2)}) collective-permute-start(f32[13,8,128]{2,1,0:T(8,128)S(1)} %get-tuple-element.37), channel_id=1, source_target_pairs={{0,1},{1,0},{2,3},{3,2},{4,5},{5,4},{6,7},{7,6},{8,9},{9,8},{10,11... | collective-permute-start | bytes 159752 | tf_op jit(solution)/shard_map/ppermute | solution.py:576
  22.6 5.4 %collective-permute-start.5 = (f32[13,8,128]{2,1,0:T(8,128)S(1)}, f32[13,8,128]{2,1,0:T(8,128)S(1)}, u32[]{:S(2)}, u32[]{:S(2)}) collective-permute-start(f32[13,8,128]{2,1,0:T(8,128)S(1)} %get-tuple-element.38), channel_id=1, source_target_pairs={{1,2},{2,1},{3,4},{4,3},{5,6},{6,5},{7,8},{8,7},{9,10},{10,9},{11,... | collective-permute-start | bytes 159752 | tf_op jit(solution)/shard_map/ppermute | solution.py:576
  28.0 7.6 %collective-permute-start.6 = (f32[22,8,128]{2,1,0:T(8,128)S(1)}, f32[22,8,128]{2,1,0:T(8,128)S(1)}, u32[]{:S(2)}, u32[]{:S(2)}) collective-permute-start(f32[22,8,128]{2,1,0:T(8,128)S(1)} %get-tuple-element.41), channel_id=1, source_target_pairs={{0,16},{16,0},{32,48},{48,32},{64,80},{80,64},{96,112},{112,96},{1... | collective-permute-start | bytes 270344 | tf_op jit(solution)/shard_map/ppermute | solution.py:576
  32.6 3.1 %collective-permute-start.7 = (f32[22,8,128]{2,1,0:T(8,128)S(1)}, f32[22,8,128]{2,1,0:T(8,128)S(1)}, u32[]{:S(2)}, u32[]{:S(2)}) collective-permute-start(f32[22,8,128]{2,1,0:T(8,128)S(1)} %get-tuple-element.42), channel_id=1, source_target_pairs={{16,32},{32,16},{48,64},{64,48},{80,96},{96,80},{112,128},{128,112... | collective-permute-start | bytes 270344 | tf_op jit(solution)/shard_map/ppermute | solution.py:576

commit v4 on v3

--- a/solution.py
+++ b/solution.py
@@ -136,8 +136,8 @@
 
 
 def y_strips_kernel(eps, src, scr, xa, xb, first, second):
-    x_even = is_even("gx", 1)
-    y_even = is_even("gy", 1)
+    x_up = first_up("gx", 1)
+    y_up = first_up("gy", 1)
 
     def fill(up, down, xl, xr):
         at = 0
@@ -155,7 +155,7 @@
 
     for x_want, (xl, xr) in ((True, (xb, xa)), (False, (xa, xb))):
         for y_want, (up, down) in ((True, (first, second)), (False, (second, first))):
-            pl.when((x_even == x_want) & (y_even == y_want))(
+            pl.when((x_up == x_want) & (y_up == y_want))(
                 lambda up=up, down=down, xl=xl, xr=xr: fill(up, down, xl, xr)
             )
 
@@ -166,17 +166,17 @@
     fx1, fy1, fz1, w1, l1_own, s2, b2, ship_a, ship_b,
     e, b, s, fx, fy, fz, w, d, ua, ub, b1, d1, va, vb,
 ):
-    x_even = is_even("gx", 1).astype(jnp.int32)
-    y_even = is_even("gy", 1)
-    row_a = pl.multiple_of(8 + 24 * y_even.astype(jnp.int32), 8)
-    row_b = pl.multiple_of(32 - 24 * y_even.astype(jnp.int32), 8)
+    x_up = first_up("gx", 1).astype(jnp.int32)
+    y_up = first_up("gy", 1)
+    row_a = pl.multiple_of(8 + 24 * y_up.astype(jnp.int32), 8)
+    row_b = pl.multiple_of(32 - 24 * y_up.astype(jnp.int32), 8)
     at, edge = 0, 0
     blank = jnp.zeros((8, LANES), F32)
     for ref, own, start, wide, margin in ((e, eps, 0, 10, 1), (b, src, 10, 9, 0), (s, scr, 19, 9, 0)):
         first, planes = 11 - wide, 14 + 2 * wide
         ref[10:26, 16:32] = own[...]
-        ref[pl.ds(first - 1 + (27 - first) * x_even, wide), 16:32] = xa[start : start + wide]
-        ref[pl.ds(26 - (27 - first) * x_even, wide), 16:32] = xb[start : start + wide]
+        ref[pl.ds(first - 1 + (27 - first) * x_up, wide), 16:32] = xa[start : start + wide]
+        ref[pl.ds(26 - (27 - first) * x_up, wide), 16:32] = xb[start : start + wide]
         ref[first : first + planes, pl.ds(row_a, 8)] = ya[at : at + planes]
         ref[first : first + planes, pl.ds(row_b, 8)] = yb[at : at + planes]
         for plane in (first - 1, first + planes):
@@ -195,8 +195,8 @@
                     rows < 2, roll(above, -row, 0), jnp.where(rows >= 6, roll(below, 6 - row, 0), 0.0)
                 )
 
-        pl.when(y_even)(lambda fill=fill: fill(yb, ya))
-        pl.when(jnp.logical_not(y_even))(lambda fill=fill: fill(ya, yb))
+        pl.when(y_up)(lambda fill=fill: fill(yb, ya))
+        pl.when(jnp.logical_not(y_up))(lambda fill=fill: fill(ya, yb))
         at += planes
         edge += 16 + 2 * margin
 
@@ -285,12 +285,12 @@
         low = row_of(first) < 4
         up = jnp.where(low, roll(first, -4, 0), second)
         down = jnp.where(low, first, roll(second, 4, 0))
-        ship_a[9 + t] = jnp.where(y_even, up, down)
-        ship_b[9 + t] = jnp.where(y_even, down, up)
+        ship_a[9 + t] = jnp.where(y_up, up, down)
+        ship_b[9 + t] = jnp.where(y_up, down, up)
 
 
 def window_kernel(s2, b2, l1_own, a1a, a1b, s2_wide, b2_wide, l1_ext, ship_a, ship_b):
-    y_even = is_even("gy", 1)
+    y_up = first_up("gy", 1)
     rows = lax.broadcasted_iota(jnp.int32, (8, LANES), 0)
 
     def join(below, above):
@@ -304,9 +304,9 @@
             l1_ext[2 * k] = jnp.where(rows < 4, roll(above[t], -turn, 0), roll(below[t], 4 - turn, 0))
             l1_ext[2 * k + 1] = l1_own[k]
 
-    pl.when(y_even)(lambda: join(a1b, a1a))
-    pl.when(jnp.logical_not(y_even))(lambda: join(a1a, a1b))
-    up = is_even("gx", 1).astype(jnp.int32)
+    pl.when(y_up)(lambda: join(a1b, a1a))
+    pl.when(jnp.logical_not(y_up))(lambda: join(a1a, a1b))
+    up = first_up("gx", 1).astype(jnp.int32)
     for ship, way in ((ship_a, up), (ship_b, 1 - up)):
         ship[0:12] = s2_wide[pl.ds(4 - 4 * way, 12)]
         ship[12:14] = b2_wide[...]
@@ -318,7 +318,7 @@
     fx, fy, fz, w, payload,
     d, b, ua, ub, piece,
 ):
-    up = is_even("gx", 1).astype(jnp.int32)
+    up = first_up("gx", 1).astype(jnp.int32)
     b[0:2] = jnp.zeros((2, 16, LANES), F32)
     b[14:16] = jnp.zeros((2, 16, LANES), F32)
     for part, tile, first, count in ((s2_wide, 4, 6, 4), (c1a, 0, 10 * up, 6), (c1b, 0, 10 - 10 * up, 6)):
@@ -357,7 +357,7 @@
         y_face = jnp.where((gy == 0) & (rows == 0), 0.0, y_face)
         side = pair(block_sum(ub, 6 + 2 * x, 6, 2), 2)
         for index, values in enumerate((x_face, y_face, z_face, diag, side)):
-            chosen = slot == x + 2 * (index % 2) + 4 * rows
+            chosen = slot == (x + 2 * rows if index == 4 else x + 2 * (index % 2) + 4 * rows)
             lines[index // 2] = jnp.where(chosen, values, lines[index // 2])
     for k in range(3):
         piece[k : k + 1] = jnp.sum(lines[k], axis=0, keepdims=True)
@@ -379,11 +379,13 @@
     around[0:24] = jnp.zeros((24, LANES), F32)
     around[24 : 24 + 12 * count] = got[...]
     around[24 + 12 * count : 48 + 12 * count] = jnp.zeros((24, LANES), F32)
-    piece[0:count] = got[pl.ds(0, count, stride=12), :]
-    piece[count + 24 : 2 * count + 24] = got[pl.ds(1, count, stride=12), :]
+    first, second = got[pl.ds(0, count, stride=12), :], got[pl.ds(1, count, stride=12), :]
+    upper = bit_of(first, 2)
+    piece[pl.ds(0, count, stride=2), :] = jnp.where(upper, roll(second, 4, 1), first)
+    piece[pl.ds(1, count, stride=2), :] = jnp.where(upper, second, roll(first, -4, 1))
     even, odd = got[pl.ds(2, count // 2, stride=24), :], got[pl.ds(14, count // 2, stride=24), :]
-    piece[2 * count + 24 :] = jnp.where(bit_of(even, 1), roll(odd, 2, 1), even)
-    for target, start, least, most in ((count, 3, -5, 9), (count + 14, 7, -3, 7)):
+    piece[2 * count + 24 :] = jnp.where(bit_of(even, 2), roll(odd, 4, 1), even)
+    for target, start, least, most in ((2 * count, 3, -5, 9), (2 * count + 14, 7, -3, 7)):
         for block in range(-2, 3):
             low, high = max(4 * block, least), min(4 * block + 4, most)
             if low < high:
@@ -399,74 +401,92 @@
     return 5 * n_y // 2 + 24
 
 
-def level3_beside(v, faces, stride):
-    x_face, y_face, z_face = faces
-    x_slot, y_bit = lane_of(v) & 3, bit_of(v, 2)
-    low = jnp.where(x_slot == 0, roll(roll(v, -3, 1), stride, 0), roll(v, 1, 1))
-    product = x_face * v
-    high = jnp.where(x_slot == 3, roll(roll(product, 3, 1), -stride, 0), roll(product, -1, 1))
-    total = x_face * low + high
-    low = jnp.where(y_bit, roll(v, 4, 1), roll(roll(v, -4, 1), 1, 0))
-    product = y_face * v
-    high = jnp.where(y_bit, roll(roll(product, 4, 1), -1, 0), roll(product, -4, 1))
-    total = total + y_face * low + high
-    return total + z_face * roll(v, 8, 1) + roll(z_face * v, -8, 1)
-
-
-def level4_beside(v, x_face, y_face, z_face, stride):
-    x_bit = bit_of(v, 1)
-    low = jnp.where(x_bit, roll(v, 2, 1), roll(roll(v, -2, 1), stride, 0))
-    product = x_face * v
-    high = jnp.where(x_bit, roll(roll(product, 2, 1), -stride, 0), roll(product, -2, 1))
-    total = x_face * low + high
-    total = total + y_face * roll(v, 1, 0) + roll(y_face * v, -1, 0)
-    return total + z_face * roll(v, 16, 1) + roll(z_face * v, -16, 1)
+def x_low(values, rows):
+    slot = lane_of(values) & 7
+    return jnp.where(slot == 0, roll(roll(values, -7, 1), rows, 0), roll(values, 1, 1))
+
+
+def x_high(values, rows):
+    slot = lane_of(values) & 7
+    return jnp.where(slot == 7, roll(roll(values, 7, 1), -rows, 0), roll(values, -1, 1))
+
+
+def yz_beside(v, y_face, z_face, level):
+    total = y_face * roll(v, 1 + level, 0) + roll(y_face * v, -1 - level, 0)
+    return total + z_face * roll(v, 8 + 8 * level, 1) + roll(z_face * v, -8 - 8 * level, 1)
+
+
+def level3_beside(v, faces, rows):
+    (x0, x1), y_faces, z_faces = faces
+    totals = [x0 * x_low(v[1], rows) + x1 * v[1], x1 * v[0] + x_high(x0 * v[0], rows)]
+    return [totals[k] + yz_beside(v[k], y_faces[k], z_faces[k], 0) for k in range(2)]
+
+
+def row_pair(values):
+    odd = (row_of(values) & 1) == 1
+    return values + jnp.where(odd, roll(values, 1, 0), roll(values, -1, 0))
+
+
+def row_keep(values, want):
+    odd = (row_of(values) & 1) == 1
+    if want:
+        return jnp.where(odd, values, roll(values, -1, 0))
+    return jnp.where(odd, roll(values, 1, 0), values)
+
+
+def exchange_slots(tiles):
+    for bit in range(3):
+        step = 1 << bit
+        upper = bit_of(tiles[0], bit)
+        made = list(tiles)
+        for k in range(8):
+            if not k & step:
+                made[k] = jnp.where(upper, roll(tiles[k + step], step, 1), tiles[k])
+                made[k + step] = jnp.where(upper, tiles[k + step], roll(tiles[k], -step, 1))
+        tiles = made
+    return tiles
 
 
 def coarse_levels(got, b3, n_x, n_y):
-    size = piece_rows(n_y)
-
-    def lines(start, count):
-        pair_of = []
-        for parity in range(2):
-            parts = [got[pl.ds((2 * a + parity) * size + start, count), :] for a in range(n_x // 2)]
-            pair_of.append(jnp.concatenate(parts, axis=0))
-        return pair_of
-
+    size, rows = piece_rows(n_y), 2 * n_y
+    groups = []
+    for g in range(n_x // 8):
+        lines = [(8 * g + q) * size for q in range(8)]
+        groups.append(exchange_slots([got[line : line + rows] for line in lines]))
+        sides = exchange_slots([got[line + rows + 24 : line + size] for line in lines])
+        for k in range(8):
+            b3[k % 2, pl.ds(g * rows + k // 2, n_y // 2, stride=4), :] = sides[k]
     fields = []
-    for start in (0, n_y + 24):
-        even, odd = lines(start, n_y)
-        upper = bit_of(even, 1)
-        fields.append(jnp.where(upper, roll(odd, 2, 1), even))
-        fields.append(jnp.where(upper, odd, roll(even, -2, 1)))
-    even, odd = lines(2 * n_y + 24, n_y // 2)
-    upper = bit_of(even, 1)
-    half = n_x // 2 * n_y // 2
-    b3[pl.ds(0, half, stride=2), :] = jnp.where(upper, roll(odd, 2, 1), even)
-    b3[pl.ds(1, half, stride=2), :] = jnp.where(upper, odd, roll(even, -2, 1))
-    fields.append(b3[...])
-    faces, diag, side = fields[0:3], fields[3], fields[4]
-    weight = relax_factor(diag)
+    for index in range(4):
+        fields.append([jnp.concatenate([g[2 * index + x] for g in groups], axis=0) for x in range(2)])
+    faces, diag = fields[0:3], fields[3]
+    side = [b3[0], b3[1]]
+    weight = [relax_factor(d) for d in diag]
 
     def sweep3(v, side):
-        return (1.0 - OMEGA) * v + weight * (side + level3_beside(v, faces, n_y))
-
-    u = weight * side
+        total = level3_beside(v, faces, rows)
+        return [(1.0 - OMEGA) * v[k] + weight[k] * (side[k] + total[k]) for k in range(2)]
+
+    u = [weight[k] * side[k] for k in range(2)]
     u = sweep3(u, side)
     u = sweep3(u, side)
-    r = side - diag * u + level3_beside(u, faces, n_y)
-
-    x_sum, y_sum, z_sum = pair(pair(faces[0], 2), 3), pair(pair(faces[1], 0), 3), pair(pair(faces[2], 0), 2)
-    x4, y4, z4 = keep(x_sum, 0, 0), keep(y_sum, 2, 0), keep(z_sum, 3, 0)
-    inner = keep(x_sum, 0, 1) + keep(y_sum, 2, 1) + keep(z_sum, 3, 1)
-    w4 = relax_factor(pair(pair(pair(diag, 0), 2), 3) - 2.0 * inner)
-    b4 = pair(pair(pair(r, 0), 2), 3)
+    total = level3_beside(u, faces, rows)
+    r = [side[k] - diag[k] * u[k] + total[k] for k in range(2)]
+
+    (x0, x1), (y0, y1), (z0, z1) = faces
+    y_sum, z_sum = pair(y0 + y1, 3), row_pair(z0 + z1)
+    x4, y4, z4 = row_pair(pair(x0, 3)), row_keep(y_sum, 0), keep(z_sum, 3, 0)
+    inner = row_keep(y_sum, 1) + keep(z_sum, 3, 1)
+    w4 = relax_factor(row_pair(pair(diag[0] + diag[1] - 2.0 * x1, 3)) - 2.0 * inner)
+    b4 = row_pair(pair(r[0] + r[1], 3))
     v = w4 * b4
     for _ in range(5):
-        v = (1.0 - OMEGA) * v + w4 * (b4 + level4_beside(v, x4, y4, z4, n_y))
+        total = x4 * x_low(v, rows) + x_high(x4 * v, rows) + yz_beside(v, y4, z4, 1)
+        v = (1.0 - OMEGA) * v + w4 * (b4 + total)
+    c = [v, v]
     for _ in range(3):
-        v = sweep3(v, r)
-    return u + v
+        c = sweep3(c, r)
+    return [u[k] + c[k] for k in range(2)]
 
 
 def up_kernel(
@@ -481,22 +501,21 @@
     size = piece_rows(n_y)
     for block in range(5):
         device = jnp.clip(gx + block - 2, 0, n_x - 1)
-        for ref, line in ((r2, n_y - 1), (u2, n_y + 11)):
+        for ref, line in ((r2, 2 * n_y - 1), (u2, 2 * n_y + 11)):
             tiles = got[pl.ds(device * size + line, 16), :]
             for k in range(4):
                 if 0 <= 4 * block - 2 + k < 16:
                     ref[4 * block - 2 + k] = spread(tiles, k, 2)
 
-    u3[48 : 48 + n_x // 2 * n_y] = coarse_levels(got, b3, n_x, n_y)
+    solved = coarse_levels(got, b3, n_x, n_y)
+    for x in range(2):
+        u3[x, 8 : 8 + solved[x].shape[0]] = solved[x]
     for block in range(5):
-        device = gx + block
-        line = 48 + (lax.div(device, 2) - 1) * n_y + gy - 2
-        lower = u3[pl.ds(line, 8), :]
-        lower = jnp.where(lax.rem(device, 2) == 1, keep(lower, 1, 1), keep(lower, 1, 0))
+        device = jnp.clip(gx + block - 2, 0, n_x - 1)
+        line = 4 + lax.div(device, 8) * 2 * n_y + 2 * gy
         for x in range(2):
-            for y in range(2):
-                values = keep(keep(lower, 0, x), 2, y)
-                e3[2 * block + x, pl.ds(y, 5, stride=2), :] = values[0:5]
+            values = pltpu.roll(u3[x, pl.ds(line, 16), :], lax.rem(LANES - lax.rem(device, 8), LANES), 1)
+            e3[2 * block + x] = spread(values, 0, 3)
 
     for plane in range(16):
         values = e3[plane // 2 + 1][1:9]
@@ -516,7 +535,7 @@
     sweep(ea2, eb2, r2, faces, w2, 2, 13, 4, 2)
     sweep(eb2, ea2, r2, faces, w2, 3, 12, 2, 2)
 
-    even = is_even("gx", 1).astype(jnp.int32)
+    even = first_up("gx", 1).astype(jnp.int32)
     for part, first, tile, count in ((c1a, 1 + 12 * even, 14, 4), (l1_ext, 5, 0, 8), (c1b, 13 - 12 * even, 14, 4)):
         for k in range(count):
             sides, own = part[tile + 2 * k], part[tile + 2 * k + 1]
@@ -568,21 +587,21 @@
     return (where >= 0) & (where < 8 * lax.axis_size("gx"))
 
 
-def swapped(values, axis, step, odd):
+def swapped(values, axis, step, second):
     pairs = []
     for k in range(lax.axis_size(axis) - step):
-        if (k // step) % 2 == odd:
+        if (k // step) % 2 != second:
             pairs += [(k, k + step), (k + step, k)]
     return lax.ppermute(values, axis, pairs)
 
 
-def is_even(axis, step):
-    return lax.rem(lax.div(lax.axis_index(axis), step), 2) == 0
+def first_up(axis, step):
+    return lax.rem(lax.div(lax.axis_index(axis), step), 2) == 1
 
 
 def local(source, dielectric, screening):
     fields = (dielectric, source, screening)
-    even = is_even("gx", 1).astype(jnp.int32)
+    even = first_up("gx", 1).astype(jnp.int32)
 
     def strip(way):
         parts = [lax.dynamic_slice_in_dim(f, way * (16 - n), n, 0) for f, n in zip(fields, (10, 9, 9))]
@@ -616,7 +635,7 @@
     (payload,) = call(relay_kernel, [array(n_x * size, LANES)], scratch, 2, 10_000, got)
     got = lax.all_to_all(payload, "gx", 0, 0, tiled=True)
 
-    scratch = [pltpu.VMEM((n_x // 2 * n_y + extra, LANES), F32) for extra in (96, 0)]
+    scratch = [pltpu.VMEM((2, n_x // 4 * n_y + extra, LANES), F32) for extra in (24, 0)]
     scratch += [pltpu.VMEM((12, 16, LANES), F32)]
     scratch += [two] * 4 + [mid] * 4 + [pltpu.VMEM((22, 24, LANES), F32)] * 2
     (result,) = call(

time: 86.2 us -> 83.6 us (0.970)
  starting transfers between devices: 12.9 us -> 17.6 us
  blocking collectives: 41.6 us -> 38.6 us
  waiting for transfers between devices: 17.9 us -> 15.3 us
  Pallas kernels: 11.5 us -> 9.87 us
    ppermute x8, starting transfers between devices: 12.9 us -> 17.6 us  [swapped(): return lax.ppermute(values, axis, pairs)]
    all_to_all x1, blocking collectives: 25 us -> 21.3 us  [local(): got = lax.all_to_all(payload, 'gx', 0, 0, tiled=True)]
    ppermute x8, waiting for transfers between devices: 17.9 us -> 15.3 us  [swapped(): return lax.ppermute(values, axis, pairs)]
    pallas_call x6, Pallas kernels: 11.5 us -> 9.87 us  [call(): pl.pallas_call(body, out_shape=outs, in_specs=[pl.BlockSpec(memory_space=...]
where the time goes in v4:
time: 83.6 us; the launch traced here: 82.5 us
  blocking collectives  38.6 us (46%)
  starting transfers between devices  17.6 us (21%)
  waiting for transfers between devices  15.3 us (18%)
  Pallas kernels  9.87 us (12%)
  local copies, waits for them, and re-layouts  1.06 us (1%)
    all_to_all x1, blocking collectives, local(): got = lax.all_to_all(payload, 'gx', 0, 0, tiled=True)  21.3 us
    ppermute x8, starting transfers between devices, swapped(): return lax.ppermute(values, axis, pairs)  17.6 us
    all_to_all x1, blocking collectives, local(): lax.all_to_all(payload, 'gy', 0, 0, tiled=True).reshape(12 * n_y, LANES)  17.3 us
    ppermute x8, waiting for transfers between devices, swapped(): return lax.ppermute(values, axis, pairs)  15.3 us
    pallas_call x6, Pallas kernels, call(): pl.pallas_call(body, out_shape=outs, in_specs=[pl.BlockSpec(memory_space=...  9.87 us
  transfers between devices with their start and end apart: 8, of which 4 were waited for; matrix products, arithmetic and copies ran while one was open for 0% of the time, Pallas kernels for 0%

profile of v4, /device:TPU:32, one launch (start us, length us, event | category | flops | bytes accessed | tf_op | source)
XLA Modules:
  0.0 82.5 jit_solution(3514933960378661221)
XLA Ops:
  0.0 0.0 copy-start.1
  0.0 0.0 copy-start.2
  0.0 1.0 %constant_dynamic-slice_fusion.2 = (f32[10,16,128]{2,1,0:T(8,128)S(1)}, f32[10,16,128]{2,1,0:T(8,128)S(1)}) fusion(f32[16,16,128]{2,1,0:T(8,128)} %eps.3, s32[]{:T(128)S(6)} %select_n.4, s32[]{:T(128)S(6)} %mul.14), kind=kLoop, calls=%fused_computation.4 | loop fusion | bytes 327688 | tf_op jit(solution)/shard_map/dynamic_slice | solution.py:607
  1.0 0.0 copy-done.1
  1.0 0.0 copy-done.2
  1.1 0.7 collective-permute-start
  1.8 0.0 copy-start
  1.8 4.5 %collective-permute-start.1 = (f32[28,16,128]{2,1,0:T(8,128)S(1)}, f32[28,16,128]{2,1,0:T(8,128)S(1)}, u32[]{:S(2)}, u32[]{:S(2)}) collective-permute-start(f32[28,16,128]{2,1,0:T(8,128)S(1)} %pad_maximum_fusion.1), channel_id=1, source_target_pairs={{0,16},{16,0},{32,48},{48,32},{64,80},{80,64},{96,112},{112,96},{1... | collective-permute-start | bytes 688136 | tf_op jit(solution)/shard_map/ppermute | solution.py:595
  6.3 0.0 collective-permute-done.xa
  6.3 5.3 %collective-permute-done.1.xb = f32[28,16,128]{2,1,0:T(8,128)S(1)} collective-permute-done((f32[28,16,128]{2,1,0:T(8,128)S(1)}, f32[28,16,128]{2,1,0:T(8,128)S(1)}, u32[]{:S(2)}, u32[]{:S(2)}) %collective-permute-start.1) | collective-permute-done | bytes 229408 | tf_op jit(solution)/shard_map/ppermute | solution.py:595
  11.6 0.0 copy-done
  11.6 0.1 shard_map.37
  11.7 1.9 %collective-permute-start.2 = (f32[111,8,128]{2,1,0:T(8,128)S(1)}, f32[111,8,128]{2,1,0:T(8,128)S(1)}, u32[]{:S(2)}, u32[]{:S(2)}) collective-permute-start(f32[111,8,128]{2,1,0:T(8,128)S(1)} %get-tuple-element.32), channel_id=1, source_target_pairs={{1,2},{2,1},{3,4},{4,3},{5,6},{6,5},{7,8},{8,7},{9,10},{10,9},{11,... | collective-permute-start | bytes 1363976 | tf_op jit(solution)/shard_map/ppermute | solution.py:595
  13.6 2.1 %collective-permute-start.3 = (f32[111,8,128]{2,1,0:T(8,128)S(1)}, f32[111,8,128]{2,1,0:T(8,128)S(1)}, u32[]{:S(2)}, u32[]{:S(2)}) collective-permute-start(f32[111,8,128]{2,1,0:T(8,128)S(1)} %get-tuple-element.33), channel_id=1, source_target_pairs={{0,1},{1,0},{2,3},{3,2},{4,5},{5,4},{6,7},{7,6},{8,9},{9,8},{10,11... | collective-permute-start | bytes 1363976 | tf_op jit(solution)/shard_map/ppermute | solution.py:595
  15.7 5.7 %collective-permute-done.2.ya = f32[111,8,128]{2,1,0:T(8,128)S(1)} collective-permute-done((f32[111,8,128]{2,1,0:T(8,128)S(1)}, f32[111,8,128]{2,1,0:T(8,128)S(1)}, u32[]{:S(2)}, u32[]{:S(2)}) %collective-permute-start.2) | collective-permute-done | bytes 454688 | tf_op jit(solution)/shard_map/ppermute | solution.py:595
  21.5 0.0 collective-permute-done.3.yb
  21.5 3.5 %shard_map.38 = (f32[16,16,128]{2,1,0:T(8,128)S(1)}, f32[22,24,128]{2,1,0:T(8,128)S(1)}, f32[22,24,128]{2,1,0:T(8,128)S(1)}, f32[22,24,128]{2,1,0:T(8,128)S(1)},...) custom-call(f32[16,16,128]{2,1,0:T(8,128)S(1)} %copy-done, ...), custom_call_target="tpu_custom_call" | custom-call | flops 10000000 | bytes 4304896 | tf_op jit(solution)/shard_map/pallas_call | solution.py:123
  25.0 1.9 %collective-permute-start.4 = (f32[13,8,128]{2,1,0:T(8,128)S(1)}, f32[13,8,128]{2,1,0:T(8,128)S(1)}, u32[]{:S(2)}, u32[]{:S(2)}) collective-permute-start(f32[13,8,128]{2,1,0:T(8,128)S(1)} %get-tuple-element.37), channel_id=1, source_target_pairs={{1,2},{2,1},{3,4},{4,3},{5,6},{6,5},{7,8},{8,7},{9,10},{10,9},{11,... | collective-permute-start | bytes 159752 | tf_op jit(solution)/shard_map/ppermute | solution.py:595
  26.9 2.1 %collective-permute-start.5 = (f32[13,8,128]{2,1,0:T(8,128)S(1)}, f32[13,8,128]{2,1,0:T(8,128)S(1)}, u32[]{:S(2)}, u32[]{:S(2)}) collective-permute-start(f32[13,8,128]{2,1,0:T(8,128)S(1)} %get-tuple-element.38), channel_id=1, source_target_pairs={{0,1},{1,0},{2,3},{3,2},{4,5},{5,4},{6,7},{7,6},{8,9},{9,8},{10,11... | collective-permute-start | bytes 159752 | tf_op jit(solution)/shard_map/ppermute | solution.py:595
  29.0 1.4 %collective-permute-done.4.a1a = f32[13,8,128]{2,1,0:T(8,128)S(1)} collective-permute-done((f32[13,8,128]{2,1,0:T(8,128)S(1)}, f32[13,8,128]{2,1,0:T(8,128)S(1)}, u32[]{:S(2)}, u32[]{:S(2)}) %collective-permute-start.4) | collective-permute-done | bytes 53280 | tf_op jit(solution)/shard_map/ppermute | solution.py:595
  30.4 0.0 collective-permute-done.5.a1b
  30.5 0.7 collective-permute-start.6
  31.1 3.8 %collective-permute-start.7 = (f32[22,8,128]{2,1,0:T(8,128)S(1)}, f32[22,8,128]{2,1,0:T(8,128)S(1)}, u32[]{:S(2)}, u32[]{:S(2)}) collective-permute-start(f32[22,8,128]{2,1,0:T(8,128)S(1)} %get-tuple-element.42), channel_id=1, source_target_pairs={{0,16},{16,0},{32,48},{48,32},{64,80},{80,64},{96,112},{112,96},{1... | collective-permute-start | bytes 270344 | tf_op jit(solution)/shard_map/ppermute | solution.py:595
  34.9 0.0 collective-permute-done.6.c1a
  34.9 2.8 %collective-permute-done.7.c1b = f32[22,8,128]{2,1,0:T(8,128)S(1)} collective-permute-done((f32[22,8,128]{2,1,0:T(8,128)S(1)}, f32[22,8,128]{2,1,0:T(8,128)S(1)}, u32[]{:S(2)}, u32[]{:S(2)}) %collective-permute-start.7) | collective-permute-done | bytes 90144 | tf_op jit(solution)/shard_map/ppermute | solution.py:595
  37.7 1.0 %shard_map.40 = (f32[16,16,128]{2,1,0:T(8,128)S(1)}, f32[16,16,128]{2,1,0:T(8,128)S(1)}, f32[16,16,128]{2,1,0:T(8,128)S(1)}, f32[16,16,128]{2,1,0:T(8,128)S(1)}, f32[192,128]{1,0:T(8,128)S(1)}) custom-call(f32[16,8,128]{2,1,0:T(8,128)S(1)} %get-tuple-element.39.s2_wide, f32[2,8,128]{2,1,0:T(8,128)S(1)} %get-tuple-element.40.b2_wide, ...), custom_call_target="tpu_custom_call" | custom-call | flops 5000000 | bytes 876544 | tf_op jit(solution)/shard_map/pallas_call | solution.py:123
  38.8 17.3 %all_to_all.16 = f32[96,2,128]{2,1,0:T(2,128)S(1)} all-to-all(f32[96,2,128]{2,1,0:T(2,128)S(1)} %bitcast.7), channel_id=1, replica_groups=mesh['gx'=16,'gy'=16] {'gy'}, dimensions={0} | all-to-all | bytes 196608 | tf_op jit(solution)/shard_map/all_to_all | solution.py:633
  56.0 0.1 shard_map.41
  56.1 21.3 %all_to_all.17 = f32[16,64,128]{2,1,0:T(8,128)S(1)} all-to-all(f32[16,64,128]{2,1,0:T(8,128)S(1)} %bitcast.4), channel_id=1, replica_groups=mesh['gx'=16,'gy'=16] {'gx'}, dimensions={0} | all-to-all | bytes 1048576 | tf_op jit(solution)/shard_map/all_to_all | solution.py:636
  77.4 5.1 %shard_map.42 = f32[16,16,128]{2,1,0:T(8,128)} custom-call(f32[1024,128]{1,0:T(8,128)S(1)} %bitcast.5, f32[16,16,128]{2,1,0:T(8,128)S(1)} %get-tuple-element.44.u0, f32[22,24,128]{2,1,0:T(8,128)S(1)} %get-tuple-element.45.fx0, f32[22,24,128]{2,1,0:T(8,128)S(1)} %get-tuple-element.46.fy0, f32[22,24,128]{2,1,0:T(8,128)S(1)} %get-tuple-element.47.fz0, ...), custom_call_target="tpu_custom_call" | custom-call | flops 10000000 | bytes 3792896 | tf_op jit(solution)/shard_map/pallas_call | solution.py:123
  (4 shorter events, 0.1 us)
Async XLA Ops:
  0.0 1.0 %copy-start.1 = (f32[16,16,128]{2,1,0:T(8,128)S(1)}, f32[16,16,128]{2,1,0:T(8,128)}, u32[]{:S(2)}) copy-start(f32[16,16,128]{2,1,0:T(8,128)} %src.3) | copy-start | bytes 393220
  0.0 1.0 %copy-start.2 = (f32[16,16,128]{2,1,0:T(8,128)S(1)}, f32[16,16,128]{2,1,0:T(8,128)}, u32[]{:S(2)}) copy-start(f32[16,16,128]{2,1,0:T(8,128)} %scr.3) | copy-start | bytes 393220
  1.1 5.2 %collective-permute-start = (f32[28,16,128]{2,1,0:T(8,128)S(1)}, f32[28,16,128]{2,1,0:T(8,128)S(1)}, u32[]{:S(2)}, u32[]{:S(2)}) collective-permute-start(f32[28,16,128]{2,1,0:T(8,128)S(1)} %pad_maximum_fusion), channel_id=1, source_target_pairs={{16,32},{32,16},{48,64},{64,48},{80,96},{96,80},{112,128},{128,112... | collective-permute-start | bytes 688136 | tf_op jit(solution)/shard_map/ppermute | solution.py:595
  1.8 9.8 %copy-start = (f32[16,16,128]{2,1,0:T(8,128)S(1)}, f32[16,16,128]{2,1,0:T(8,128)}, u32[]{:S(2)}) copy-start(f32[16,16,128]{2,1,0:T(8,128)} %eps.3) | copy-start | bytes 393220
  1.8 9.8 %collective-permute-start.1 = (f32[28,16,128]{2,1,0:T(8,128)S(1)}, f32[28,16,128]{2,1,0:T(8,128)S(1)}, u32[]{:S(2)}, u32[]{:S(2)}) collective-permute-start(f32[28,16,128]{2,1,0:T(8,128)S(1)} %pad_maximum_fusion.1), channel_id=1, source_target_pairs={{0,16},{16,0},{32,48},{48,32},{64,80},{80,64},{96,112},{112,96},{1... | collective-permute-start | bytes 688136 | tf_op jit(solution)/shard_map/ppermute | solution.py:595
  11.7 9.8 %collective-permute-start.2 = (f32[111,8,128]{2,1,0:T(8,128)S(1)}, f32[111,8,128]{2,1,0:T(8,128)S(1)}, u32[]{:S(2)}, u32[]{:S(2)}) collective-permute-start(f32[111,8,128]{2,1,0:T(8,128)S(1)} %get-tuple-element.32), channel_id=1, source_target_pairs={{1,2},{2,1},{3,4},{4,3},{5,6},{6,5},{7,8},{8,7},{9,10},{10,9},{11,... | collective-permute-start | bytes 1363976 | tf_op jit(solution)/shard_map/ppermute | solution.py:595
  13.6 7.8 %collective-permute-start.3 = (f32[111,8,128]{2,1,0:T(8,128)S(1)}, f32[111,8,128]{2,1,0:T(8,128)S(1)}, u32[]{:S(2)}, u32[]{:S(2)}) collective-permute-start(f32[111,8,128]{2,1,0:T(8,128)S(1)} %get-tuple-element.33), channel_id=1, source_target_pairs={{0,1},{1,0},{2,3},{3,2},{4,5},{5,4},{6,7},{7,6},{8,9},{9,8},{10,11... | collective-permute-start | bytes 1363976 | tf_op jit(solution)/shard_map/ppermute | solution.py:595
  25.0 5.5 %collective-permute-start.4 = (f32[13,8,128]{2,1,0:T(8,128)S(1)}, f32[13,8,128]{2,1,0:T(8,128)S(1)}, u32[]{:S(2)}, u32[]{:S(2)}) collective-permute-start(f32[13,8,128]{2,1,0:T(8,128)S(1)} %get-tuple-element.37), channel_id=1, source_target_pairs={{1,2},{2,1},{3,4},{4,3},{5,6},{6,5},{7,8},{8,7},{9,10},{10,9},{11,... | collective-permute-start | bytes 159752 | tf_op jit(solution)/shard_map/ppermute | solution.py:595
  26.9 3.5 %collective-permute-start.5 = (f32[13,8,128]{2,1,0:T(8,128)S(1)}, f32[13,8,128]{2,1,0:T(8,128)S(1)}, u32[]{:S(2)}, u32[]{:S(2)}) collective-permute-start(f32[13,8,128]{2,1,0:T(8,128)S(1)} %get-tuple-element.38), channel_id=1, source_target_pairs={{0,1},{1,0},{2,3},{3,2},{4,5},{5,4},{6,7},{7,6},{8,9},{9,8},{10,11... | collective-permute-start | bytes 159752 | tf_op jit(solution)/shard_map/ppermute | solution.py:595
  30.5 4.4 %collective-permute-start.6 = (f32[22,8,128]{2,1,0:T(8,128)S(1)}, f32[22,8,128]{2,1,0:T(8,128)S(1)}, u32[]{:S(2)}, u32[]{:S(2)}) collective-permute-start(f32[22,8,128]{2,1,0:T(8,128)S(1)} %get-tuple-element.41), channel_id=1, source_target_pairs={{16,32},{32,16},{48,64},{64,48},{80,96},{96,80},{112,128},{128,112... | collective-permute-start | bytes 270344 | tf_op jit(solution)/shard_map/ppermute | solution.py:595
  31.1 6.6 %collective-permute-start.7 = (f32[22,8,128]{2,1,0:T(8,128)S(1)}, f32[22,8,128]{2,1,0:T(8,128)S(1)}, u32[]{:S(2)}, u32[]{:S(2)}) collective-permute-start(f32[22,8,128]{2,1,0:T(8,128)S(1)} %get-tuple-element.42), channel_id=1, source_target_pairs={{0,16},{16,0},{32,48},{48,32},{64,80},{80,64},{96,112},{112,96},{1... | collective-permute-start | bytes 270344 | tf_op jit(solution)/shard_map/ppermute | solution.py:595

commit v5 on v4

--- a/solution.py
+++ b/solution.py
@@ -50,7 +50,7 @@
     return jnp.where(good, OMEGA / jnp.where(good, diag, 1.0), 0.0)
 
 
-def loop(first, last, step, body, unroll=4):
+def loop(first, last, step, body, unroll=16):
     count = (last - first + 1) // step
     assert count * step == last - first + 1
     trips = count // unroll
@@ -68,7 +68,7 @@
         body(first + k * step)
 
 
-def beside(vals, faces, plane, count, level, rows):
+def beside(vals, faces, plane, count, level, rows, sides=None):
     fx, fy, fz = faces
     shift = 1 << level
     here = pl.ds(plane, count)
@@ -76,23 +76,27 @@
     y_face, z_face = fy[here, rows], fz[here, rows]
     total = fx[here, rows] * vals[pl.ds(plane - 1, count), rows]
     total = total + fx[pl.ds(plane + 1, count), rows] * vals[pl.ds(plane + 1, count), rows]
-    total = total + y_face * roll(v, 1, 1) + roll(y_face * v, -1, 1)
+    if sides is None:
+        total = total + y_face * roll(v, 1, 1) + roll(y_face * v, -1, 1)
+    else:
+        low, high = sides
+        total = total + y_face * vals[here, low] + fy[here, high] * vals[here, high]
     total = total + z_face * roll(v, shift, 2) + roll(z_face * v, -shift, 2)
     return v, total
 
 
-def sweep(out, vals, side, faces, weight, first, last, step, level, unroll=4, rows=slice(None)):
+def sweep(out, vals, side, faces, weight, first, last, step, level, unroll=16, rows=slice(None), sides=None):
     def body(plane):
-        v, total = beside(vals, faces, plane, step, level, rows)
+        v, total = beside(vals, faces, plane, step, level, rows, sides)
         here = pl.ds(plane, step)
         out[here, rows] = (1.0 - OMEGA) * v + weight[here, rows] * (side[here, rows] + total)
 
     loop(first, last, step, body, unroll)
 
 
-def remains(out, vals, side, faces, diag, first, last, step, level, unroll=4, rows=slice(None)):
+def remains(out, vals, side, faces, diag, first, last, step, level, unroll=16, rows=slice(None), sides=None):
     def body(plane):
-        v, total = beside(vals, faces, plane, step, level, rows)
+        v, total = beside(vals, faces, plane, step, level, rows, sides)
         here = pl.ds(plane, step)
         out[here, rows] = side[here, rows] - diag[here, rows] * v + total
 
@@ -135,21 +139,37 @@
     return jax.ShapeDtypeStruct(shape, F32)
 
 
+def shared_tiles(reach):
+    for dx in range(1, reach - 3):
+        other = 2 * reach - 8 - dx
+        yield (dx, other, reach - dx) if dx < other < reach else (dx, 0, 8)
+
+
 def y_strips_kernel(eps, src, scr, xa, xb, first, second):
     x_up = first_up("gx", 1)
     y_up = first_up("gy", 1)
 
     def fill(up, down, xl, xr):
-        at = 0
-        for own, start, wide in ((eps, 0, 9), (src, 10, 8), (scr, 19, 8)):
-            for part, low, count in ((xl, start + 1, wide), (own, 0, 16), (xr, start, wide)):
-                up[at : at + count] = part[low : low + count, 8:16]
-                down[at : at + count] = part[low : low + count, 0:8]
-                at += count
+        for index, own in enumerate((eps, src, scr)):
+            up[16 * index : 16 * index + 16] = own[:, 8:16]
+            down[16 * index : 16 * index + 16] = own[:, 0:8]
+        at = 48
+        rows = lax.broadcasted_iota(jnp.int32, (8, LANES), 0)
+        for start, reach in ((0, 10), (10, 9), (19, 9)):
+            for part, plane_of in ((xl, lambda dx: reach - dx), (xr, lambda dx: dx - 1)):
+                for dx, other, most in shared_tiles(reach):
+                    plane = start + plane_of(dx)
+                    above, below = part[plane, 8:16], part[plane, 0:8]
+                    if other:
+                        plane = start + plane_of(other)
+                        above = jnp.where(rows >= 8 - most, above, roll(part[plane, 8:16], 8 - most, 0))
+                        below = jnp.where(rows < most, below, roll(part[plane, 0:8], most, 0))
+                    up[at], down[at] = above, below
+                    at += 1
         edges = [(xl, 9)] + [(eps, k) for k in range(16)] + [(xr, 0)]
         edges += [(src, k) for k in range(16)] + [(scr, k) for k in range(16)]
         for k, (part, plane) in enumerate(edges):
-            tile, row = 98 + k // 4, 2 * (k % 4)
+            tile, row = 80 + k // 4, 2 * (k % 4)
             up[tile, row : row + 2] = part[plane, 6:8]
             down[tile, row : row + 2] = part[plane, 8:10]
 
@@ -170,25 +190,34 @@
     y_up = first_up("gy", 1)
     row_a = pl.multiple_of(8 + 24 * y_up.astype(jnp.int32), 8)
     row_b = pl.multiple_of(32 - 24 * y_up.astype(jnp.int32), 8)
-    at, edge = 0, 0
+    at, edge = 48, 0
     blank = jnp.zeros((8, LANES), F32)
-    for ref, own, start, wide, margin in ((e, eps, 0, 10, 1), (b, src, 10, 9, 0), (s, scr, 19, 9, 0)):
-        first, planes = 11 - wide, 14 + 2 * wide
+    for index, (ref, own, start, reach, margin) in enumerate(((e, eps, 0, 10, 1), (b, src, 10, 9, 0), (s, scr, 19, 9, 0))):
+        first = 10 - reach
         ref[10:26, 16:32] = own[...]
-        ref[pl.ds(first - 1 + (27 - first) * x_up, wide), 16:32] = xa[start : start + wide]
-        ref[pl.ds(26 - (27 - first) * x_up, wide), 16:32] = xb[start : start + wide]
-        ref[first : first + planes, pl.ds(row_a, 8)] = ya[at : at + planes]
-        ref[first : first + planes, pl.ds(row_b, 8)] = yb[at : at + planes]
-        for plane in (first - 1, first + planes):
+        ref[pl.ds(first + (26 - first) * x_up, reach), 16:32] = xa[start : start + reach]
+        ref[pl.ds(26 - (26 - first) * x_up, reach), 16:32] = xb[start : start + reach]
+        ref[10:26, pl.ds(row_a, 8)] = ya[16 * index : 16 * index + 16]
+        ref[10:26, pl.ds(row_b, 8)] = yb[16 * index : 16 * index + 16]
+        for plane in (first, 25 + reach):
             ref[plane, 8:16] = blank
             ref[plane, 32:40] = blank
-        for plane in range(first - 1, first + planes + 1):
+        for plane in range(first, 26 + reach):
             if not 10 - margin <= plane < 26 + margin:
                 ref[plane, 0:8] = blank
 
-        def fill(below_ref, above_ref, ref=ref, margin=margin, edge=edge):
+        def fill(below_ref, above_ref, ref=ref, reach=reach, margin=margin, at=at, edge=edge):
+            for plane_of in (lambda dx: 10 - dx, lambda dx: 25 + dx):
+                for dx, other, most in shared_tiles(reach):
+                    below, above = below_ref[at], above_ref[at]
+                    ref[plane_of(dx), 8:16] = below
+                    ref[plane_of(dx), 32:40] = above
+                    if other:
+                        ref[plane_of(other), 8:16] = roll(below, most, 0)
+                        ref[plane_of(other), 32:40] = roll(above, -most, 0)
+                    at += 1
             for k in range(16 + 2 * margin):
-                tile, row = 98 + (edge + k) // 4, 2 * ((edge + k) % 4)
+                tile, row = 80 + (edge + k) // 4, 2 * ((edge + k) % 4)
                 below, above = below_ref[tile], above_ref[tile]
                 rows = row_of(below)
                 ref[10 - margin + k, 0:8] = jnp.where(
@@ -197,11 +226,11 @@
 
         pl.when(y_up)(lambda fill=fill: fill(yb, ya))
         pl.when(jnp.logical_not(y_up))(lambda fill=fill: fill(ya, yb))
-        at += planes
+        at += 2 * (reach - 4)
         edge += 16 + 2 * margin
 
     def stencil(plane):
-        cells = e[pl.ds(plane - 1, 4)]
+        cells = e[pl.ds(plane - 1, 4), 0:40]
         centre = cells[1:3]
         x_face = 0.5 * (cells[0:3] + cells[1:4])
         y_face = 0.5 * (centre + roll(centre, 1, 1))
@@ -209,23 +238,27 @@
         z_face = jnp.where(lanes == 0, 0.0, 0.5 * (centre + roll(centre, 1, 2)))
         ends = jnp.where((lanes == 0) | (lanes == LANES - 1), 0.5 * centre, 0.0)
         here = pl.ds(plane, 2)
-        screen = s[here]
+        screen = s[here, 0:40]
         diag = x_face[0:2] + x_face[1:3] + y_face + roll(y_face, -1, 1)
         diag = diag + z_face + roll(z_face, -1, 2) + screen + ends
         diag = jnp.where(screen > 0.0, diag, 0.0)
         weight = relax_factor(diag)
-        fx[pl.ds(plane, 3)] = x_face
-        fy[here] = y_face
-        fz[here] = z_face
-        d[here] = diag
-        w[here] = weight
-        ua[here] = weight * b[here]
+        value = weight * b[here, 0:40]
+        fx[pl.ds(plane, 3), 0:40] = x_face
+        fy[here, 0:40] = y_face
+        fy[here, 40:48] = y_face[:, 0:8]
+        fz[here, 0:40] = z_face
+        d[here, 0:40] = diag
+        w[here, 0:40] = weight
+        ua[here, 0:40] = value
+        ua[here, 40:48] = value[:, 0:8]
 
     loop(1, 34, 2, stencil, 8)
     faces = (fx, fy, fz)
-    sweep(ub, ua, b, faces, w, 2, 33, 2, 0, 8)
-    sweep(ua, ub, b, faces, w, 3, 32, 2, 0, 8, slice(8, 40))
-    remains(ub, ua, b, faces, d, 4, 31, 2, 0, 8, slice(8, 40))
+    rows, sides = slice(8, 40), (slice(7, 39), slice(9, 41))
+    sweep(ub, ua, b, faces, w, 2, 33, 2, 0, 8, rows, sides)
+    sweep(ua, ub, b, faces, w, 3, 32, 2, 0, 8, rows, sides)
+    remains(ub, ua, b, faces, d, 4, 31, 2, 0, 8, rows, sides)
     u0_out[...] = ua[10:26, 16:32]
 
     def keep_window(plane):
@@ -609,13 +642,13 @@
 
     xa, xb = strip(even), strip(1 - even)
     xa, xb = swapped(xa, "gx", 1, 0), swapped(xb, "gx", 1, 1)
-    ya, yb = call(y_strips_kernel, [array(111, 8, LANES)] * 2, [], 2, 10_000, *fields, xa, xb)
+    ya, yb = call(y_strips_kernel, [array(93, 8, LANES)] * 2, [], 2, 10_000, *fields, xa, xb)
     ya, yb = swapped(ya, "gy", 1, 0), swapped(yb, "gy", 1, 1)
 
-    big, mid = pltpu.VMEM((36, 40, LANES), F32), pltpu.VMEM((18, 24, LANES), F32)
+    big, mid = pltpu.VMEM((36, 48, LANES), F32), pltpu.VMEM((18, 24, LANES), F32)
     outs = [array(16, 16, LANES)] + [array(22, 24, LANES)] * 5 + [array(18, 24, LANES)] * 4
     outs += [array(8, 8, LANES), array(8, 8, LANES), array(1, 8, LANES), array(13, 8, LANES), array(13, 8, LANES)]
-    made = call(down_kernel, outs, [big] * 10 + [mid] * 4, 12, 10_000_000, *fields, xa, xb, ya, yb)
+    made = call(down_kernel, outs, [big] * 10 + [mid] * 4, 14, 10_000_000, *fields, xa, xb, ya, yb)
     fine, level1, (l1_own, s2, b2, sa, sb) = made[0:6], made[6:10], made[10:15]
 
     a1a, a1b = swapped(sa, "gy", 1, 0), swapped(sb, "gy", 1, 1)

time: 83.6 us -> 82.3 us (0.984)
  no operation moved by 1% of the time
where the time goes in v5:
time: 82.3 us; the launch traced here: 81.2 us
  blocking collectives  38.6 us (47%)
  starting transfers between devices  17.6 us (21%)
  waiting for transfers between devices  14.5 us (18%)
  Pallas kernels  9.33 us (11%)
  local copies, waits for them, and re-layouts  1.06 us (1%)
    all_to_all x1, blocking collectives, local(): got = lax.all_to_all(payload, 'gx', 0, 0, tiled=True)  21.3 us
    ppermute x8, starting transfers between devices, swapped(): return lax.ppermute(values, axis, pairs)  17.6 us
    all_to_all x1, blocking collectives, local(): lax.all_to_all(payload, 'gy', 0, 0, tiled=True).reshape(12 * n_y, LANES)  17.3 us
    ppermute x8, waiting for transfers between devices, swapped(): return lax.ppermute(values, axis, pairs)  14.5 us
    pallas_call x6, Pallas kernels, call(): pl.pallas_call(body, out_shape=outs, in_specs=[pl.BlockSpec(memory_space=...  9.33 us
  transfers between devices with their start and end apart: 8, of which 4 were waited for; matrix products, arithmetic and copies ran while one was open for 0% of the time, Pallas kernels for 0%

profile of v5, /device:TPU:32, one launch (start us, length us, event | category | flops | bytes accessed | tf_op | source)
XLA Modules:
  0.0 81.2 jit_solution(18000831546823124738)
XLA Ops:
  0.0 0.0 copy-start.1
  0.0 0.0 copy-start.2
  0.0 1.0 %constant_dynamic-slice_fusion.2 = (f32[10,16,128]{2,1,0:T(8,128)S(1)}, f32[10,16,128]{2,1,0:T(8,128)S(1)}) fusion(f32[16,16,128]{2,1,0:T(8,128)} %eps.3, s32[]{:T(128)S(6)} %select_n.4, s32[]{:T(128)S(6)} %mul.14), kind=kLoop, calls=%fused_computation.4 | loop fusion | bytes 327688 | tf_op jit(solution)/shard_map/dynamic_slice | solution.py:640
  1.0 0.0 copy-done.1
  1.0 0.0 copy-done.2
  1.1 0.7 collective-permute-start
  1.8 0.0 copy-start
  1.8 4.5 %collective-permute-start.1 = (f32[28,16,128]{2,1,0:T(8,128)S(1)}, f32[28,16,128]{2,1,0:T(8,128)S(1)}, u32[]{:S(2)}, u32[]{:S(2)}) collective-permute-start(f32[28,16,128]{2,1,0:T(8,128)S(1)} %pad_maximum_fusion.1), channel_id=1, source_target_pairs={{0,16},{16,0},{32,48},{48,32},{64,80},{80,64},{96,112},{112,96},{1... | collective-permute-start | bytes 688136 | tf_op jit(solution)/shard_map/ppermute | solution.py:628
  6.3 0.0 collective-permute-done.xa
  6.3 5.3 %collective-permute-done.1.xb = f32[28,16,128]{2,1,0:T(8,128)S(1)} collective-permute-done((f32[28,16,128]{2,1,0:T(8,128)S(1)}, f32[28,16,128]{2,1,0:T(8,128)S(1)}, u32[]{:S(2)}, u32[]{:S(2)}) %collective-permute-start.1) | collective-permute-done | bytes 229408 | tf_op jit(solution)/shard_map/ppermute | solution.py:628
  11.6 0.0 copy-done
  11.6 0.1 shard_map.37
  11.7 1.9 %collective-permute-start.2 = (f32[93,8,128]{2,1,0:T(8,128)S(1)}, f32[93,8,128]{2,1,0:T(8,128)S(1)}, u32[]{:S(2)}, u32[]{:S(2)}) collective-permute-start(f32[93,8,128]{2,1,0:T(8,128)S(1)} %get-tuple-element.32), channel_id=1, source_target_pairs={{1,2},{2,1},{3,4},{4,3},{5,6},{6,5},{7,8},{8,7},{9,10},{10,9},{11,... | collective-permute-start | bytes 1142792 | tf_op jit(solution)/shard_map/ppermute | solution.py:628
  13.6 2.1 %collective-permute-start.3 = (f32[93,8,128]{2,1,0:T(8,128)S(1)}, f32[93,8,128]{2,1,0:T(8,128)S(1)}, u32[]{:S(2)}, u32[]{:S(2)}) collective-permute-start(f32[93,8,128]{2,1,0:T(8,128)S(1)} %get-tuple-element.33), channel_id=1, source_target_pairs={{0,1},{1,0},{2,3},{3,2},{4,5},{5,4},{6,7},{7,6},{8,9},{9,8},{10,11... | collective-permute-start | bytes 1142792 | tf_op jit(solution)/shard_map/ppermute | solution.py:628
  15.7 4.9 %collective-permute-done.2.ya = f32[93,8,128]{2,1,0:T(8,128)S(1)} collective-permute-done((f32[93,8,128]{2,1,0:T(8,128)S(1)}, f32[93,8,128]{2,1,0:T(8,128)S(1)}, u32[]{:S(2)}, u32[]{:S(2)}) %collective-permute-start.2) | collective-permute-done | bytes 380960 | tf_op jit(solution)/shard_map/ppermute | solution.py:628
  20.7 0.0 collective-permute-done.3.yb
  20.7 3.4 %shard_map.38 = (f32[16,16,128]{2,1,0:T(8,128)S(1)}, f32[22,24,128]{2,1,0:T(8,128)S(1)}, f32[22,24,128]{2,1,0:T(8,128)S(1)}, f32[22,24,128]{2,1,0:T(8,128)S(1)},...) custom-call(f32[16,16,128]{2,1,0:T(8,128)S(1)} %copy-done, ...), custom_call_target="tpu_custom_call" | custom-call | flops 10000000 | bytes 4157440 | tf_op jit(solution)/shard_map/pallas_call | solution.py:127
  24.0 1.9 %collective-permute-start.4 = (f32[13,8,128]{2,1,0:T(8,128)S(1)}, f32[13,8,128]{2,1,0:T(8,128)S(1)}, u32[]{:S(2)}, u32[]{:S(2)}) collective-permute-start(f32[13,8,128]{2,1,0:T(8,128)S(1)} %get-tuple-element.37), channel_id=1, source_target_pairs={{1,2},{2,1},{3,4},{4,3},{5,6},{6,5},{7,8},{8,7},{9,10},{10,9},{11,... | collective-permute-start | bytes 159752 | tf_op jit(solution)/shard_map/ppermute | solution.py:628
  26.0 2.1 %collective-permute-start.5 = (f32[13,8,128]{2,1,0:T(8,128)S(1)}, f32[13,8,128]{2,1,0:T(8,128)S(1)}, u32[]{:S(2)}, u32[]{:S(2)}) collective-permute-start(f32[13,8,128]{2,1,0:T(8,128)S(1)} %get-tuple-element.38), channel_id=1, source_target_pairs={{0,1},{1,0},{2,3},{3,2},{4,5},{5,4},{6,7},{7,6},{8,9},{9,8},{10,11... | collective-permute-start | bytes 159752 | tf_op jit(solution)/shard_map/ppermute | solution.py:628
  28.1 1.4 %collective-permute-done.4.a1a = f32[13,8,128]{2,1,0:T(8,128)S(1)} collective-permute-done((f32[13,8,128]{2,1,0:T(8,128)S(1)}, f32[13,8,128]{2,1,0:T(8,128)S(1)}, u32[]{:S(2)}, u32[]{:S(2)}) %collective-permute-start.4) | collective-permute-done | bytes 53280 | tf_op jit(solution)/shard_map/ppermute | solution.py:628
  29.5 0.0 collective-permute-done.5.a1b
  29.5 0.7 collective-permute-start.6
  30.2 3.8 %collective-permute-start.7 = (f32[22,8,128]{2,1,0:T(8,128)S(1)}, f32[22,8,128]{2,1,0:T(8,128)S(1)}, u32[]{:S(2)}, u32[]{:S(2)}) collective-permute-start(f32[22,8,128]{2,1,0:T(8,128)S(1)} %get-tuple-element.42), channel_id=1, source_target_pairs={{0,16},{16,0},{32,48},{48,32},{64,80},{80,64},{96,112},{112,96},{1... | collective-permute-start | bytes 270344 | tf_op jit(solution)/shard_map/ppermute | solution.py:628
  34.0 0.0 collective-permute-done.6.c1a
  34.0 2.8 %collective-permute-done.7.c1b = f32[22,8,128]{2,1,0:T(8,128)S(1)} collective-permute-done((f32[22,8,128]{2,1,0:T(8,128)S(1)}, f32[22,8,128]{2,1,0:T(8,128)S(1)}, u32[]{:S(2)}, u32[]{:S(2)}) %collective-permute-start.7) | collective-permute-done | bytes 90144 | tf_op jit(solution)/shard_map/ppermute | solution.py:628
  36.8 1.0 %shard_map.40 = (f32[16,16,128]{2,1,0:T(8,128)S(1)}, f32[16,16,128]{2,1,0:T(8,128)S(1)}, f32[16,16,128]{2,1,0:T(8,128)S(1)}, f32[16,16,128]{2,1,0:T(8,128)S(1)}, f32[192,128]{1,0:T(8,128)S(1)}) custom-call(f32[16,8,128]{2,1,0:T(8,128)S(1)} %get-tuple-element.39.s2_wide, f32[2,8,128]{2,1,0:T(8,128)S(1)} %get-tuple-element.40.b2_wide, ...), custom_call_target="tpu_custom_call" | custom-call | flops 5000000 | bytes 876544 | tf_op jit(solution)/shard_map/pallas_call | solution.py:127
  37.8 17.3 %all_to_all.16 = f32[96,2,128]{2,1,0:T(2,128)S(1)} all-to-all(f32[96,2,128]{2,1,0:T(2,128)S(1)} %bitcast.7), channel_id=1, replica_groups=mesh['gx'=16,'gy'=16] {'gy'}, dimensions={0} | all-to-all | bytes 196608 | tf_op jit(solution)/shard_map/all_to_all | solution.py:666
  55.1 0.1 shard_map.41
  55.2 21.3 %all_to_all.17 = f32[16,64,128]{2,1,0:T(8,128)S(1)} all-to-all(f32[16,64,128]{2,1,0:T(8,128)S(1)} %bitcast.4), channel_id=1, replica_groups=mesh['gx'=16,'gy'=16] {'gx'}, dimensions={0} | all-to-all | bytes 1048576 | tf_op jit(solution)/shard_map/all_to_all | solution.py:669
  76.5 4.7 %shard_map.42 = f32[16,16,128]{2,1,0:T(8,128)} custom-call(f32[1024,128]{1,0:T(8,128)S(1)} %bitcast.5, f32[16,16,128]{2,1,0:T(8,128)S(1)} %get-tuple-element.44.u0, f32[22,24,128]{2,1,0:T(8,128)S(1)} %get-tuple-element.45.fx0, f32[22,24,128]{2,1,0:T(8,128)S(1)} %get-tuple-element.46.fy0, f32[22,24,128]{2,1,0:T(8,128)S(1)} %get-tuple-element.47.fz0, ...), custom_call_target="tpu_custom_call" | custom-call | flops 10000000 | bytes 3792896 | tf_op jit(solution)/shard_map/pallas_call | solution.py:127
  (4 shorter events, 0.1 us)
Async XLA Ops:
  0.0 1.0 %copy-start.1 = (f32[16,16,128]{2,1,0:T(8,128)S(1)}, f32[16,16,128]{2,1,0:T(8,128)}, u32[]{:S(2)}) copy-start(f32[16,16,128]{2,1,0:T(8,128)} %src.3) | copy-start | bytes 393220
  0.0 1.0 %copy-start.2 = (f32[16,16,128]{2,1,0:T(8,128)S(1)}, f32[16,16,128]{2,1,0:T(8,128)}, u32[]{:S(2)}) copy-start(f32[16,16,128]{2,1,0:T(8,128)} %scr.3) | copy-start | bytes 393220
  1.1 5.2 %collective-permute-start = (f32[28,16,128]{2,1,0:T(8,128)S(1)}, f32[28,16,128]{2,1,0:T(8,128)S(1)}, u32[]{:S(2)}, u32[]{:S(2)}) collective-permute-start(f32[28,16,128]{2,1,0:T(8,128)S(1)} %pad_maximum_fusion), channel_id=1, source_target_pairs={{16,32},{32,16},{48,64},{64,48},{80,96},{96,80},{112,128},{128,112... | collective-permute-start | bytes 688136 | tf_op jit(solution)/shard_map/ppermute | solution.py:628
  1.8 9.8 %copy-start = (f32[16,16,128]{2,1,0:T(8,128)S(1)}, f32[16,16,128]{2,1,0:T(8,128)}, u32[]{:S(2)}) copy-start(f32[16,16,128]{2,1,0:T(8,128)} %eps.3) | copy-start | bytes 393220
  1.8 9.8 %collective-permute-start.1 = (f32[28,16,128]{2,1,0:T(8,128)S(1)}, f32[28,16,128]{2,1,0:T(8,128)S(1)}, u32[]{:S(2)}, u32[]{:S(2)}) collective-permute-start(f32[28,16,128]{2,1,0:T(8,128)S(1)} %pad_maximum_fusion.1), channel_id=1, source_target_pairs={{0,16},{16,0},{32,48},{48,32},{64,80},{80,64},{96,112},{112,96},{1... | collective-permute-start | bytes 688136 | tf_op jit(solution)/shard_map/ppermute | solution.py:628
  11.7 9.0 %collective-permute-start.2 = (f32[93,8,128]{2,1,0:T(8,128)S(1)}, f32[93,8,128]{2,1,0:T(8,128)S(1)}, u32[]{:S(2)}, u32[]{:S(2)}) collective-permute-start(f32[93,8,128]{2,1,0:T(8,128)S(1)} %get-tuple-element.32), channel_id=1, source_target_pairs={{1,2},{2,1},{3,4},{4,3},{5,6},{6,5},{7,8},{8,7},{9,10},{10,9},{11,... | collective-permute-start | bytes 1142792 | tf_op jit(solution)/shard_map/ppermute | solution.py:628
  13.6 7.0 %collective-permute-start.3 = (f32[93,8,128]{2,1,0:T(8,128)S(1)}, f32[93,8,128]{2,1,0:T(8,128)S(1)}, u32[]{:S(2)}, u32[]{:S(2)}) collective-permute-start(f32[93,8,128]{2,1,0:T(8,128)S(1)} %get-tuple-element.33), channel_id=1, source_target_pairs={{0,1},{1,0},{2,3},{3,2},{4,5},{5,4},{6,7},{7,6},{8,9},{9,8},{10,11... | collective-permute-start | bytes 1142792 | tf_op jit(solution)/shard_map/ppermute | solution.py:628
  24.0 5.5 %collective-permute-start.4 = (f32[13,8,128]{2,1,0:T(8,128)S(1)}, f32[13,8,128]{2,1,0:T(8,128)S(1)}, u32[]{:S(2)}, u32[]{:S(2)}) collective-permute-start(f32[13,8,128]{2,1,0:T(8,128)S(1)} %get-tuple-element.37), channel_id=1, source_target_pairs={{1,2},{2,1},{3,4},{4,3},{5,6},{6,5},{7,8},{8,7},{9,10},{10,9},{11,... | collective-permute-start | bytes 159752 | tf_op jit(solution)/shard_map/ppermute | solution.py:628
  26.0 3.5 %collective-permute-start.5 = (f32[13,8,128]{2,1,0:T(8,128)S(1)}, f32[13,8,128]{2,1,0:T(8,128)S(1)}, u32[]{:S(2)}, u32[]{:S(2)}) collective-permute-start(f32[13,8,128]{2,1,0:T(8,128)S(1)} %get-tuple-element.38), channel_id=1, source_target_pairs={{0,1},{1,0},{2,3},{3,2},{4,5},{5,4},{6,7},{7,6},{8,9},{9,8},{10,11... | collective-permute-start | bytes 159752 | tf_op jit(solution)/shard_map/ppermute | solution.py:628
  29.5 4.4 %collective-permute-start.6 = (f32[22,8,128]{2,1,0:T(8,128)S(1)}, f32[22,8,128]{2,1,0:T(8,128)S(1)}, u32[]{:S(2)}, u32[]{:S(2)}) collective-permute-start(f32[22,8,128]{2,1,0:T(8,128)S(1)} %get-tuple-element.41), channel_id=1, source_target_pairs={{16,32},{32,16},{48,64},{64,48},{80,96},{96,80},{112,128},{128,112... | collective-permute-start | bytes 270344 | tf_op jit(solution)/shard_map/ppermute | solution.py:628
  30.2 6.6 %collective-permute-start.7 = (f32[22,8,128]{2,1,0:T(8,128)S(1)}, f32[22,8,128]{2,1,0:T(8,128)S(1)}, u32[]{:S(2)}, u32[]{:S(2)}) collective-permute-start(f32[22,8,128]{2,1,0:T(8,128)S(1)} %get-tuple-element.42), channel_id=1, source_target_pairs={{0,16},{16,0},{32,48},{48,32},{64,80},{80,64},{96,112},{112,96},{1... | collective-permute-start | bytes 270344 | tf_op jit(solution)/shard_map/ppermute | solution.py:628

commit v6 on v5

--- a/solution.py
+++ b/solution.py
@@ -145,16 +145,29 @@
         yield (dx, other, reach - dx) if dx < other < reach else (dx, 0, 8)
 
 
-def y_strips_kernel(eps, src, scr, xa, xb, first, second):
-    x_up = first_up("gx", 1)
-    y_up = first_up("gy", 1)
-
-    def fill(up, down, xl, xr):
+def either_way(up, first, second, fill):
+    pl.when(up)(lambda: fill(first, second))
+    pl.when(jnp.logical_not(up))(lambda: fill(second, first))
+
+
+def y_own_kernel(eps, src, scr, first, second):
+    def fill(up, down):
         for index, own in enumerate((eps, src, scr)):
             up[16 * index : 16 * index + 16] = own[:, 8:16]
             down[16 * index : 16 * index + 16] = own[:, 0:8]
-        at = 48
-        rows = lax.broadcasted_iota(jnp.int32, (8, LANES), 0)
+            for plane in range(16):
+                tile, row = 48 + 4 * index + plane // 4, 2 * (plane % 4)
+                up[tile, row : row + 2] = own[plane, 6:8]
+                down[tile, row : row + 2] = own[plane, 8:10]
+
+    either_way(first_up("gy", 1), first, second, fill)
+
+
+def y_corner_kernel(xa, xb, first, second):
+    rows = lax.broadcasted_iota(jnp.int32, (8, LANES), 0)
+
+    def fill(up, down, xl, xr):
+        at = 0
         for start, reach in ((0, 10), (10, 9), (19, 9)):
             for part, plane_of in ((xl, lambda dx: reach - dx), (xr, lambda dx: dx - 1)):
                 for dx, other, most in shared_tiles(reach):
@@ -166,22 +179,21 @@
                         below = jnp.where(rows < most, below, roll(part[plane, 0:8], most, 0))
                     up[at], down[at] = above, below
                     at += 1
-        edges = [(xl, 9)] + [(eps, k) for k in range(16)] + [(xr, 0)]
-        edges += [(src, k) for k in range(16)] + [(scr, k) for k in range(16)]
-        for k, (part, plane) in enumerate(edges):
-            tile, row = 80 + k // 4, 2 * (k % 4)
-            up[tile, row : row + 2] = part[plane, 6:8]
-            down[tile, row : row + 2] = part[plane, 8:10]
-
-    for x_want, (xl, xr) in ((True, (xb, xa)), (False, (xa, xb))):
-        for y_want, (up, down) in ((True, (first, second)), (False, (second, first))):
-            pl.when((x_up == x_want) & (y_up == y_want))(
-                lambda up=up, down=down, xl=xl, xr=xr: fill(up, down, xl, xr)
-            )
+        for ref, row in ((up, 6), (down, 8)):
+            ref[at] = jnp.zeros((8, LANES), F32)
+            ref[at, 0:2] = xl[9, row : row + 2]
+            ref[at, 2:4] = xr[0, row : row + 2]
+
+    either_way(
+        first_up("gx", 1),
+        xb,
+        xa,
+        lambda xl, xr: either_way(first_up("gy", 1), first, second, lambda up, down: fill(up, down, xl, xr)),
+    )
 
 
 def down_kernel(
-    eps, src, scr, xa, xb, ya, yb,
+    eps, src, scr, xa, xb, ya, yb, za, zb,
     u0_out, fx0_out, fy0_out, fz0_out, w0_out, r0_out,
     fx1, fy1, fz1, w1, l1_own, s2, b2, ship_a, ship_b,
     e, b, s, fx, fy, fz, w, d, ua, ub, b1, d1, va, vb,
@@ -190,7 +202,7 @@
     y_up = first_up("gy", 1)
     row_a = pl.multiple_of(8 + 24 * y_up.astype(jnp.int32), 8)
     row_b = pl.multiple_of(32 - 24 * y_up.astype(jnp.int32), 8)
-    at, edge = 48, 0
+    at = 0
     blank = jnp.zeros((8, LANES), F32)
     for index, (ref, own, start, reach, margin) in enumerate(((e, eps, 0, 10, 1), (b, src, 10, 9, 0), (s, scr, 19, 9, 0))):
         first = 10 - reach
@@ -206,28 +218,29 @@
             if not 10 - margin <= plane < 26 + margin:
                 ref[plane, 0:8] = blank
 
-        def fill(below_ref, above_ref, ref=ref, reach=reach, margin=margin, at=at, edge=edge):
+        def fill(below_ref, above_ref, below_side, above_side, ref=ref, index=index, reach=reach, margin=margin, at=at):
             for plane_of in (lambda dx: 10 - dx, lambda dx: 25 + dx):
                 for dx, other, most in shared_tiles(reach):
-                    below, above = below_ref[at], above_ref[at]
+                    below, above = below_side[at], above_side[at]
                     ref[plane_of(dx), 8:16] = below
                     ref[plane_of(dx), 32:40] = above
                     if other:
                         ref[plane_of(other), 8:16] = roll(below, most, 0)
                         ref[plane_of(other), 32:40] = roll(above, -most, 0)
                     at += 1
-            for k in range(16 + 2 * margin):
-                tile, row = 80 + (edge + k) // 4, 2 * ((edge + k) % 4)
-                below, above = below_ref[tile], above_ref[tile]
+            edges = [(below_ref, above_ref, 48 + 4 * index + k // 4, 2 * (k % 4), 10 + k) for k in range(16)]
+            if margin:
+                edges += [(below_side, above_side, 32, 0, 9), (below_side, above_side, 32, 2, 26)]
+            for low_ref, high_ref, tile, row, plane in edges:
+                below, above = low_ref[tile], high_ref[tile]
                 rows = row_of(below)
-                ref[10 - margin + k, 0:8] = jnp.where(
+                ref[plane, 0:8] = jnp.where(
                     rows < 2, roll(above, -row, 0), jnp.where(rows >= 6, roll(below, 6 - row, 0), 0.0)
                 )
 
-        pl.when(y_up)(lambda fill=fill: fill(yb, ya))
-        pl.when(jnp.logical_not(y_up))(lambda fill=fill: fill(ya, yb))
+        pl.when(y_up)(lambda fill=fill: fill(yb, ya, zb, za))
+        pl.when(jnp.logical_not(y_up))(lambda fill=fill: fill(ya, yb, za, zb))
         at += 2 * (reach - 4)
-        edge += 16 + 2 * margin
 
     def stencil(plane):
         cells = e[pl.ds(plane - 1, 4), 0:40]
@@ -642,13 +655,15 @@
 
     xa, xb = strip(even), strip(1 - even)
     xa, xb = swapped(xa, "gx", 1, 0), swapped(xb, "gx", 1, 1)
-    ya, yb = call(y_strips_kernel, [array(93, 8, LANES)] * 2, [], 2, 10_000, *fields, xa, xb)
+    ya, yb = call(y_own_kernel, [array(60, 8, LANES)] * 2, [], 2, 10_000, *fields)
     ya, yb = swapped(ya, "gy", 1, 0), swapped(yb, "gy", 1, 1)
+    za, zb = call(y_corner_kernel, [array(33, 8, LANES)] * 2, [], 2, 10_000, xa, xb)
+    za, zb = swapped(za, "gy", 1, 0), swapped(zb, "gy", 1, 1)
 
     big, mid = pltpu.VMEM((36, 48, LANES), F32), pltpu.VMEM((18, 24, LANES), F32)
     outs = [array(16, 16, LANES)] + [array(22, 24, LANES)] * 5 + [array(18, 24, LANES)] * 4
     outs += [array(8, 8, LANES), array(8, 8, LANES), array(1, 8, LANES), array(13, 8, LANES), array(13, 8, LANES)]
-    made = call(down_kernel, outs, [big] * 10 + [mid] * 4, 14, 10_000_000, *fields, xa, xb, ya, yb)
+    made = call(down_kernel, outs, [big] * 10 + [mid] * 4, 14, 10_000_000, *fields, xa, xb, ya, yb, za, zb)
     fine, level1, (l1_own, s2, b2, sa, sb) = made[0:6], made[6:10], made[10:15]
 
     a1a, a1b = swapped(sa, "gy", 1, 0), swapped(sb, "gy", 1, 1)

time: 82.3 us -> 79.6 us (0.967)
  waiting for transfers between devices: 14.5 us -> 7.74 us
  starting transfers between devices: 17.6 us -> 21.7 us
    ppermute x8 -> x10, waiting for transfers between devices: 14.5 us -> 7.74 us  [swapped(): return lax.ppermute(values, axis, pairs)]
    ppermute x8 -> x10, starting transfers between devices: 17.6 us -> 21.7 us  [swapped(): return lax.ppermute(values, axis, pairs)]
    pallas_call x6 -> x7, Pallas kernels: 9.33 us -> 9.34 us  [call(): pl.pallas_call(body, out_shape=outs, in_specs=[pl.BlockSpec(memory_space=...]
  transfers between devices with their start and end apart: 8 -> 10, of which waited for: 4 -> 4; matrix products, arithmetic and copies ran while one was open for 0% -> 0% of each run, Pallas kernels for 0% -> 0%
where the time goes in v6:
time: 79.6 us; the launch traced here: 78.5 us
  blocking collectives  38.5 us (48%)
  starting transfers between devices  21.7 us (27%)
  Pallas kernels  9.34 us (12%)
  waiting for transfers between devices  7.74 us (10%)
  local copies, waits for them, and re-layouts  1.06 us (1%)
    ppermute x10, starting transfers between devices, swapped(): return lax.ppermute(values, axis, pairs)  21.7 us
    all_to_all x1, blocking collectives, local(): got = lax.all_to_all(payload, 'gx', 0, 0, tiled=True)  21.3 us
    all_to_all x1, blocking collectives, local(): lax.all_to_all(payload, 'gy', 0, 0, tiled=True).reshape(12 * n_y, LANES)  17.3 us
    pallas_call x7, Pallas kernels, call(): pl.pallas_call(body, out_shape=outs, in_specs=[pl.BlockSpec(memory_space=...  9.34 us
    ppermute x10, waiting for transfers between devices, swapped(): return lax.ppermute(values, axis, pairs)  7.74 us
  transfers between devices with their start and end apart: 10, of which 4 were waited for; matrix products, arithmetic and copies ran while one was open for 0% of the time, Pallas kernels for 0%

profile of v6, /device:TPU:32, one launch (start us, length us, event | category | flops | bytes accessed | tf_op | source)
XLA Modules:
  0.0 78.5 jit_solution(5274960389762607035)
XLA Ops:
  0.0 1.0 %constant_dynamic-slice_fusion.2 = (f32[10,16,128]{2,1,0:T(8,128)S(1)}, f32[10,16,128]{2,1,0:T(8,128)S(1)}) fusion(f32[16,16,128]{2,1,0:T(8,128)} %eps.3, s32[]{:T(128)S(6)} %select_n.4, s32[]{:T(128)S(6)} %mul.14), kind=kLoop, calls=%fused_computation.4 | loop fusion | bytes 327688 | tf_op jit(solution)/shard_map/dynamic_slice | solution.py:653
  1.0 0.0 copy-done.1
  1.0 0.0 copy-done.2
  1.1 0.7 collective-permute-start
  1.8 0.0 copy-start
  1.8 4.5 %collective-permute-start.1 = (f32[28,16,128]{2,1,0:T(8,128)S(1)}, f32[28,16,128]{2,1,0:T(8,128)S(1)}, u32[]{:S(2)}, u32[]{:S(2)}) collective-permute-start(f32[28,16,128]{2,1,0:T(8,128)S(1)} %pad_maximum_fusion.1), channel_id=1, source_target_pairs={{0,16},{16,0},{32,48},{48,32},{64,80},{80,64},{96,112},{112,96},{1... | collective-permute-start | bytes 688136 | tf_op jit(solution)/shard_map/ppermute | solution.py:641
  6.3 0.0 copy-done
  6.3 0.1 shard_map.37
  6.4 1.9 %collective-permute-start.2 = (f32[60,8,128]{2,1,0:T(8,128)S(1)}, f32[60,8,128]{2,1,0:T(8,128)S(1)}, u32[]{:S(2)}, u32[]{:S(2)}) collective-permute-start(f32[60,8,128]{2,1,0:T(8,128)S(1)} %get-tuple-element.34), channel_id=1, source_target_pairs={{1,2},{2,1},{3,4},{4,3},{5,6},{6,5},{7,8},{8,7},{9,10},{10,9},{11,... | collective-permute-start | bytes 737288 | tf_op jit(solution)/shard_map/ppermute | solution.py:641
  8.3 2.1 %collective-permute-start.3 = (f32[60,8,128]{2,1,0:T(8,128)S(1)}, f32[60,8,128]{2,1,0:T(8,128)S(1)}, u32[]{:S(2)}, u32[]{:S(2)}) collective-permute-start(f32[60,8,128]{2,1,0:T(8,128)S(1)} %get-tuple-element.35), channel_id=1, source_target_pairs={{0,1},{1,0},{2,3},{3,2},{4,5},{5,4},{6,7},{7,6},{8,9},{9,8},{10,11... | collective-permute-start | bytes 737288 | tf_op jit(solution)/shard_map/ppermute | solution.py:641
  10.4 0.0 collective-permute-done.xa
  10.4 1.2 %collective-permute-done.1.xb = f32[28,16,128]{2,1,0:T(8,128)S(1)} collective-permute-done((f32[28,16,128]{2,1,0:T(8,128)S(1)}, f32[28,16,128]{2,1,0:T(8,128)S(1)}, u32[]{:S(2)}, u32[]{:S(2)}) %collective-permute-start.1) | collective-permute-done | bytes 229408 | tf_op jit(solution)/shard_map/ppermute | solution.py:641
  11.6 1.9 %collective-permute-start.4 = (f32[33,8,128]{2,1,0:T(8,128)S(1)}, f32[33,8,128]{2,1,0:T(8,128)S(1)}, u32[]{:S(2)}, u32[]{:S(2)}) collective-permute-start(f32[33,8,128]{2,1,0:T(8,128)S(1)} %get-tuple-element.36), channel_id=1, source_target_pairs={{1,2},{2,1},{3,4},{4,3},{5,6},{6,5},{7,8},{8,7},{9,10},{10,9},{11,... | collective-permute-start | bytes 405512 | tf_op jit(solution)/shard_map/ppermute | solution.py:641
  13.6 2.1 %collective-permute-start.5 = (f32[33,8,128]{2,1,0:T(8,128)S(1)}, f32[33,8,128]{2,1,0:T(8,128)S(1)}, u32[]{:S(2)}, u32[]{:S(2)}) collective-permute-start(f32[33,8,128]{2,1,0:T(8,128)S(1)} %get-tuple-element.37), channel_id=1, source_target_pairs={{0,1},{1,0},{2,3},{3,2},{4,5},{5,4},{6,7},{7,6},{8,9},{9,8},{10,11... | collective-permute-start | bytes 405512 | tf_op jit(solution)/shard_map/ppermute | solution.py:641
  15.7 0.0 collective-permute-done.2.ya
  15.7 0.0 collective-permute-done.3.yb
  15.7 2.3 %collective-permute-done.4.za = f32[33,8,128]{2,1,0:T(8,128)S(1)} collective-permute-done((f32[33,8,128]{2,1,0:T(8,128)S(1)}, f32[33,8,128]{2,1,0:T(8,128)S(1)}, u32[]{:S(2)}, u32[]{:S(2)}) %collective-permute-start.4) | collective-permute-done | bytes 135200 | tf_op jit(solution)/shard_map/ppermute | solution.py:641
  18.0 0.0 collective-permute-done.5.zb
  18.0 3.4 %shard_map.39 = (f32[16,16,128]{2,1,0:T(8,128)S(1)}, f32[22,24,128]{2,1,0:T(8,128)S(1)}, f32[22,24,128]{2,1,0:T(8,128)S(1)}, f32[22,24,128]{2,1,0:T(8,128)S(1)},...) custom-call(f32[16,16,128]{2,1,0:T(8,128)S(1)} %copy-done, ...), custom_call_target="tpu_custom_call" | custom-call | flops 10000000 | bytes 4157440 | tf_op jit(solution)/shard_map/pallas_call | solution.py:127
  21.4 1.9 %collective-permute-start.6 = (f32[13,8,128]{2,1,0:T(8,128)S(1)}, f32[13,8,128]{2,1,0:T(8,128)S(1)}, u32[]{:S(2)}, u32[]{:S(2)}) collective-permute-start(f32[13,8,128]{2,1,0:T(8,128)S(1)} %get-tuple-element.41), channel_id=1, source_target_pairs={{1,2},{2,1},{3,4},{4,3},{5,6},{6,5},{7,8},{8,7},{9,10},{10,9},{11,... | collective-permute-start | bytes 159752 | tf_op jit(solution)/shard_map/ppermute | solution.py:641
  23.3 2.1 %collective-permute-start.7 = (f32[13,8,128]{2,1,0:T(8,128)S(1)}, f32[13,8,128]{2,1,0:T(8,128)S(1)}, u32[]{:S(2)}, u32[]{:S(2)}) collective-permute-start(f32[13,8,128]{2,1,0:T(8,128)S(1)} %get-tuple-element.42), channel_id=1, source_target_pairs={{0,1},{1,0},{2,3},{3,2},{4,5},{5,4},{6,7},{7,6},{8,9},{9,8},{10,11... | collective-permute-start | bytes 159752 | tf_op jit(solution)/shard_map/ppermute | solution.py:641
  25.4 1.4 %collective-permute-done.6.a1a = f32[13,8,128]{2,1,0:T(8,128)S(1)} collective-permute-done((f32[13,8,128]{2,1,0:T(8,128)S(1)}, f32[13,8,128]{2,1,0:T(8,128)S(1)}, u32[]{:S(2)}, u32[]{:S(2)}) %collective-permute-start.6) | collective-permute-done | bytes 53280 | tf_op jit(solution)/shard_map/ppermute | solution.py:641
  26.8 0.0 collective-permute-done.7.a1b
  26.9 0.7 collective-permute-start.8
  27.5 3.8 %collective-permute-start.9 = (f32[22,8,128]{2,1,0:T(8,128)S(1)}, f32[22,8,128]{2,1,0:T(8,128)S(1)}, u32[]{:S(2)}, u32[]{:S(2)}) collective-permute-start(f32[22,8,128]{2,1,0:T(8,128)S(1)} %get-tuple-element.46), channel_id=1, source_target_pairs={{0,16},{16,0},{32,48},{48,32},{64,80},{80,64},{96,112},{112,96},{1... | collective-permute-start | bytes 270344 | tf_op jit(solution)/shard_map/ppermute | solution.py:641
  31.3 0.0 collective-permute-done.8.c1a
  31.3 2.8 %collective-permute-done.9.c1b = f32[22,8,128]{2,1,0:T(8,128)S(1)} collective-permute-done((f32[22,8,128]{2,1,0:T(8,128)S(1)}, f32[22,8,128]{2,1,0:T(8,128)S(1)}, u32[]{:S(2)}, u32[]{:S(2)}) %collective-permute-start.9) | collective-permute-done | bytes 90144 | tf_op jit(solution)/shard_map/ppermute | solution.py:641
  34.1 1.0 %shard_map.41 = (f32[16,16,128]{2,1,0:T(8,128)S(1)}, f32[16,16,128]{2,1,0:T(8,128)S(1)}, f32[16,16,128]{2,1,0:T(8,128)S(1)}, f32[16,16,128]{2,1,0:T(8,128)S(1)}, f32[192,128]{1,0:T(8,128)S(1)}) custom-call(f32[16,8,128]{2,1,0:T(8,128)S(1)} %get-tuple-element.43.s2_wide, f32[2,8,128]{2,1,0:T(8,128)S(1)} %get-tuple-element.44.b2_wide, ...), custom_call_target="tpu_custom_call" | custom-call | flops 5000000 | bytes 876544 | tf_op jit(solution)/shard_map/pallas_call | solution.py:127
  35.2 17.3 %all_to_all.16 = f32[96,2,128]{2,1,0:T(2,128)S(1)} all-to-all(f32[96,2,128]{2,1,0:T(2,128)S(1)} %bitcast.7), channel_id=1, replica_groups=mesh['gx'=16,'gy'=16] {'gy'}, dimensions={0} | all-to-all | bytes 196608 | tf_op jit(solution)/shard_map/all_to_all | solution.py:681
  52.4 0.1 shard_map.42
  52.6 21.3 %all_to_all.17 = f32[16,64,128]{2,1,0:T(8,128)S(1)} all-to-all(f32[16,64,128]{2,1,0:T(8,128)S(1)} %bitcast.4), channel_id=1, replica_groups=mesh['gx'=16,'gy'=16] {'gx'}, dimensions={0} | all-to-all | bytes 1048576 | tf_op jit(solution)/shard_map/all_to_all | solution.py:684
  73.8 4.7 %shard_map.43 = f32[16,16,128]{2,1,0:T(8,128)} custom-call(f32[1024,128]{1,0:T(8,128)S(1)} %bitcast.5, f32[16,16,128]{2,1,0:T(8,128)S(1)} %get-tuple-element.48.u0, f32[22,24,128]{2,1,0:T(8,128)S(1)} %get-tuple-element.49.fx0, f32[22,24,128]{2,1,0:T(8,128)S(1)} %get-tuple-element.50.fy0, f32[22,24,128]{2,1,0:T(8,128)S(1)} %get-tuple-element.51.fz0, ...), custom_call_target="tpu_custom_call" | custom-call | flops 10000000 | bytes 3792896 | tf_op jit(solution)/shard_map/pallas_call | solution.py:127
  (7 shorter events, 0.1 us)
Async XLA Ops:
  0.0 1.0 %copy-start.1 = (f32[16,16,128]{2,1,0:T(8,128)S(1)}, f32[16,16,128]{2,1,0:T(8,128)}, u32[]{:S(2)}) copy-start(f32[16,16,128]{2,1,0:T(8,128)} %src.3) | copy-start | bytes 393220
  0.0 1.0 %copy-start.2 = (f32[16,16,128]{2,1,0:T(8,128)S(1)}, f32[16,16,128]{2,1,0:T(8,128)}, u32[]{:S(2)}) copy-start(f32[16,16,128]{2,1,0:T(8,128)} %scr.3) | copy-start | bytes 393220
  1.1 9.3 %collective-permute-start = (f32[28,16,128]{2,1,0:T(8,128)S(1)}, f32[28,16,128]{2,1,0:T(8,128)S(1)}, u32[]{:S(2)}, u32[]{:S(2)}) collective-permute-start(f32[28,16,128]{2,1,0:T(8,128)S(1)} %pad_maximum_fusion), channel_id=1, source_target_pairs={{16,32},{32,16},{48,64},{64,48},{80,96},{96,80},{112,128},{128,112... | collective-permute-start | bytes 688136 | tf_op jit(solution)/shard_map/ppermute | solution.py:641
  1.8 4.5 %copy-start = (f32[16,16,128]{2,1,0:T(8,128)S(1)}, f32[16,16,128]{2,1,0:T(8,128)}, u32[]{:S(2)}) copy-start(f32[16,16,128]{2,1,0:T(8,128)} %eps.3) | copy-start | bytes 393220
  1.8 9.8 %collective-permute-start.1 = (f32[28,16,128]{2,1,0:T(8,128)S(1)}, f32[28,16,128]{2,1,0:T(8,128)S(1)}, u32[]{:S(2)}, u32[]{:S(2)}) collective-permute-start(f32[28,16,128]{2,1,0:T(8,128)S(1)} %pad_maximum_fusion.1), channel_id=1, source_target_pairs={{0,16},{16,0},{32,48},{48,32},{64,80},{80,64},{96,112},{112,96},{1... | collective-permute-start | bytes 688136 | tf_op jit(solution)/shard_map/ppermute | solution.py:641
  6.4 9.3 %collective-permute-start.2 = (f32[60,8,128]{2,1,0:T(8,128)S(1)}, f32[60,8,128]{2,1,0:T(8,128)S(1)}, u32[]{:S(2)}, u32[]{:S(2)}) collective-permute-start(f32[60,8,128]{2,1,0:T(8,128)S(1)} %get-tuple-element.34), channel_id=1, source_target_pairs={{1,2},{2,1},{3,4},{4,3},{5,6},{6,5},{7,8},{8,7},{9,10},{10,9},{11,... | collective-permute-start | bytes 737288 | tf_op jit(solution)/shard_map/ppermute | solution.py:641
  8.3 7.4 %collective-permute-start.3 = (f32[60,8,128]{2,1,0:T(8,128)S(1)}, f32[60,8,128]{2,1,0:T(8,128)S(1)}, u32[]{:S(2)}, u32[]{:S(2)}) collective-permute-start(f32[60,8,128]{2,1,0:T(8,128)S(1)} %get-tuple-element.35), channel_id=1, source_target_pairs={{0,1},{1,0},{2,3},{3,2},{4,5},{5,4},{6,7},{7,6},{8,9},{9,8},{10,11... | collective-permute-start | bytes 737288 | tf_op jit(solution)/shard_map/ppermute | solution.py:641
  11.6 6.3 %collective-permute-start.4 = (f32[33,8,128]{2,1,0:T(8,128)S(1)}, f32[33,8,128]{2,1,0:T(8,128)S(1)}, u32[]{:S(2)}, u32[]{:S(2)}) collective-permute-start(f32[33,8,128]{2,1,0:T(8,128)S(1)} %get-tuple-element.36), channel_id=1, source_target_pairs={{1,2},{2,1},{3,4},{4,3},{5,6},{6,5},{7,8},{8,7},{9,10},{10,9},{11,... | collective-permute-start | bytes 405512 | tf_op jit(solution)/shard_map/ppermute | solution.py:641
  13.6 4.4 %collective-permute-start.5 = (f32[33,8,128]{2,1,0:T(8,128)S(1)}, f32[33,8,128]{2,1,0:T(8,128)S(1)}, u32[]{:S(2)}, u32[]{:S(2)}) collective-permute-start(f32[33,8,128]{2,1,0:T(8,128)S(1)} %get-tuple-element.37), channel_id=1, source_target_pairs={{0,1},{1,0},{2,3},{3,2},{4,5},{5,4},{6,7},{7,6},{8,9},{9,8},{10,11... | collective-permute-start | bytes 405512 | tf_op jit(solution)/shard_map/ppermute | solution.py:641
  21.4 5.5 %collective-permute-start.6 = (f32[13,8,128]{2,1,0:T(8,128)S(1)}, f32[13,8,128]{2,1,0:T(8,128)S(1)}, u32[]{:S(2)}, u32[]{:S(2)}) collective-permute-start(f32[13,8,128]{2,1,0:T(8,128)S(1)} %get-tuple-element.41), channel_id=1, source_target_pairs={{1,2},{2,1},{3,4},{4,3},{5,6},{6,5},{7,8},{8,7},{9,10},{10,9},{11,... | collective-permute-start | bytes 159752 | tf_op jit(solution)/shard_map/ppermute | solution.py:641
  23.3 3.5 %collective-permute-start.7 = (f32[13,8,128]{2,1,0:T(8,128)S(1)}, f32[13,8,128]{2,1,0:T(8,128)S(1)}, u32[]{:S(2)}, u32[]{:S(2)}) collective-permute-start(f32[13,8,128]{2,1,0:T(8,128)S(1)} %get-tuple-element.42), channel_id=1, source_target_pairs={{0,1},{1,0},{2,3},{3,2},{4,5},{5,4},{6,7},{7,6},{8,9},{9,8},{10,11... | collective-permute-start | bytes 159752 | tf_op jit(solution)/shard_map/ppermute | solution.py:641
  26.9 4.4 %collective-permute-start.8 = (f32[22,8,128]{2,1,0:T(8,128)S(1)}, f32[22,8,128]{2,1,0:T(8,128)S(1)}, u32[]{:S(2)}, u32[]{:S(2)}) collective-permute-start(f32[22,8,128]{2,1,0:T(8,128)S(1)} %get-tuple-element.45), channel_id=1, source_target_pairs={{16,32},{32,16},{48,64},{64,48},{80,96},{96,80},{112,128},{128,112... | collective-permute-start | bytes 270344 | tf_op jit(solution)/shard_map/ppermute | solution.py:641
  27.5 6.6 %collective-permute-start.9 = (f32[22,8,128]{2,1,0:T(8,128)S(1)}, f32[22,8,128]{2,1,0:T(8,128)S(1)}, u32[]{:S(2)}, u32[]{:S(2)}) collective-permute-start(f32[22,8,128]{2,1,0:T(8,128)S(1)} %get-tuple-element.46), channel_id=1, source_target_pairs={{0,16},{16,0},{32,48},{48,32},{64,80},{80,64},{96,112},{112,96},{1... | collective-permute-start | bytes 270344 | tf_op jit(solution)/shard_map/ppermute | solution.py:641

commit v7 on v6

--- a/solution.py
+++ b/solution.py
@@ -293,7 +293,7 @@
 
     for ref in (fx1, fy1, fz1, w1, d1, b1):
         ref[:, 16:24] = jnp.zeros((18, 8, LANES), F32)
-    loop(1, 16, 1, to_level1, 8)
+    loop(1, 16, 1, to_level1, 16)
     even, odd = pl.ds(0, 20, stride=2), pl.ds(1, 20, stride=2)
     fx1[17, 0:20] = pair(fx[34, even, :] + fx[34, odd, :], 0)
 
@@ -302,7 +302,7 @@
         b1[plane, 0:20] = side
         va[plane, 0:20] = w1[plane, 0:20] * side
 
-    loop(2, 15, 1, side1, 8)
+    loop(2, 15, 1, side1, 14)
     va[:, 20:24] = jnp.zeros((18, 4, LANES), F32)
     faces1 = (fx1, fy1, fz1)
     sweep(vb, va, b1, faces1, w1, 3, 14, 4, 1)

time: 79.6 us -> 79.4 us (level)
  no operation moved by 1% of the time
where the time goes in v7:
time: 79.4 us; the launch traced here: 78.3 us
  blocking collectives  38.5 us (48%)
  starting transfers between devices  21.7 us (27%)
  Pallas kernels  9.16 us (12%)
  waiting for transfers between devices  7.74 us (10%)
  local copies, waits for them, and re-layouts  1.06 us (1%)
    ppermute x10, starting transfers between devices, swapped(): return lax.ppermute(values, axis, pairs)  21.7 us
    all_to_all x1, blocking collectives, local(): got = lax.all_to_all(payload, 'gx', 0, 0, tiled=True)  21.3 us
    all_to_all x1, blocking collectives, local(): lax.all_to_all(payload, 'gy', 0, 0, tiled=True).reshape(12 * n_y, LANES)  17.3 us
    pallas_call x7, Pallas kernels, call(): pl.pallas_call(body, out_shape=outs, in_specs=[pl.BlockSpec(memory_space=...  9.16 us
    ppermute x10, waiting for transfers between devices, swapped(): return lax.ppermute(values, axis, pairs)  7.74 us
  transfers between devices with their start and end apart: 10, of which 4 were waited for; matrix products, arithmetic and copies ran while one was open for 0% of the time, Pallas kernels for 0%

profile of v7, /device:TPU:32, one launch (start us, length us, event | category | flops | bytes accessed | tf_op | source)
XLA Modules:
  0.0 78.3 jit_solution(11525398201705754226)
XLA Ops:
  0.0 1.0 %constant_dynamic-slice_fusion.2 = (f32[10,16,128]{2,1,0:T(8,128)S(1)}, f32[10,16,128]{2,1,0:T(8,128)S(1)}) fusion(f32[16,16,128]{2,1,0:T(8,128)} %eps.3, s32[]{:T(128)S(6)} %select_n.4, s32[]{:T(128)S(6)} %mul.14), kind=kLoop, calls=%fused_computation.4 | loop fusion | bytes 327688 | tf_op jit(solution)/shard_map/dynamic_slice | solution.py:653
  1.0 0.0 copy-done.1
  1.0 0.0 copy-done.2
  1.1 0.7 collective-permute-start
  1.8 0.0 copy-start
  1.8 4.5 %collective-permute-start.1 = (f32[28,16,128]{2,1,0:T(8,128)S(1)}, f32[28,16,128]{2,1,0:T(8,128)S(1)}, u32[]{:S(2)}, u32[]{:S(2)}) collective-permute-start(f32[28,16,128]{2,1,0:T(8,128)S(1)} %pad_maximum_fusion.1), channel_id=1, source_target_pairs={{0,16},{16,0},{32,48},{48,32},{64,80},{80,64},{96,112},{112,96},{1... | collective-permute-start | bytes 688136 | tf_op jit(solution)/shard_map/ppermute | solution.py:641
  6.3 0.0 copy-done
  6.3 0.1 shard_map.37
  6.4 1.9 %collective-permute-start.2 = (f32[60,8,128]{2,1,0:T(8,128)S(1)}, f32[60,8,128]{2,1,0:T(8,128)S(1)}, u32[]{:S(2)}, u32[]{:S(2)}) collective-permute-start(f32[60,8,128]{2,1,0:T(8,128)S(1)} %get-tuple-element.34), channel_id=1, source_target_pairs={{1,2},{2,1},{3,4},{4,3},{5,6},{6,5},{7,8},{8,7},{9,10},{10,9},{11,... | collective-permute-start | bytes 737288 | tf_op jit(solution)/shard_map/ppermute | solution.py:641
  8.3 2.1 %collective-permute-start.3 = (f32[60,8,128]{2,1,0:T(8,128)S(1)}, f32[60,8,128]{2,1,0:T(8,128)S(1)}, u32[]{:S(2)}, u32[]{:S(2)}) collective-permute-start(f32[60,8,128]{2,1,0:T(8,128)S(1)} %get-tuple-element.35), channel_id=1, source_target_pairs={{0,1},{1,0},{2,3},{3,2},{4,5},{5,4},{6,7},{7,6},{8,9},{9,8},{10,11... | collective-permute-start | bytes 737288 | tf_op jit(solution)/shard_map/ppermute | solution.py:641
  10.4 0.0 collective-permute-done.xa
  10.4 1.2 %collective-permute-done.1.xb = f32[28,16,128]{2,1,0:T(8,128)S(1)} collective-permute-done((f32[28,16,128]{2,1,0:T(8,128)S(1)}, f32[28,16,128]{2,1,0:T(8,128)S(1)}, u32[]{:S(2)}, u32[]{:S(2)}) %collective-permute-start.1) | collective-permute-done | bytes 229408 | tf_op jit(solution)/shard_map/ppermute | solution.py:641
  11.6 1.9 %collective-permute-start.4 = (f32[33,8,128]{2,1,0:T(8,128)S(1)}, f32[33,8,128]{2,1,0:T(8,128)S(1)}, u32[]{:S(2)}, u32[]{:S(2)}) collective-permute-start(f32[33,8,128]{2,1,0:T(8,128)S(1)} %get-tuple-element.36), channel_id=1, source_target_pairs={{1,2},{2,1},{3,4},{4,3},{5,6},{6,5},{7,8},{8,7},{9,10},{10,9},{11,... | collective-permute-start | bytes 405512 | tf_op jit(solution)/shard_map/ppermute | solution.py:641
  13.6 2.1 %collective-permute-start.5 = (f32[33,8,128]{2,1,0:T(8,128)S(1)}, f32[33,8,128]{2,1,0:T(8,128)S(1)}, u32[]{:S(2)}, u32[]{:S(2)}) collective-permute-start(f32[33,8,128]{2,1,0:T(8,128)S(1)} %get-tuple-element.37), channel_id=1, source_target_pairs={{0,1},{1,0},{2,3},{3,2},{4,5},{5,4},{6,7},{7,6},{8,9},{9,8},{10,11... | collective-permute-start | bytes 405512 | tf_op jit(solution)/shard_map/ppermute | solution.py:641
  15.7 0.0 collective-permute-done.2.ya
  15.7 0.0 collective-permute-done.3.yb
  15.7 2.3 %collective-permute-done.4.za = f32[33,8,128]{2,1,0:T(8,128)S(1)} collective-permute-done((f32[33,8,128]{2,1,0:T(8,128)S(1)}, f32[33,8,128]{2,1,0:T(8,128)S(1)}, u32[]{:S(2)}, u32[]{:S(2)}) %collective-permute-start.4) | collective-permute-done | bytes 135200 | tf_op jit(solution)/shard_map/ppermute | solution.py:641
  18.0 0.0 collective-permute-done.5.zb
  18.0 3.2 %shard_map.39 = (f32[16,16,128]{2,1,0:T(8,128)S(1)}, f32[22,24,128]{2,1,0:T(8,128)S(1)}, f32[22,24,128]{2,1,0:T(8,128)S(1)}, f32[22,24,128]{2,1,0:T(8,128)S(1)},...) custom-call(f32[16,16,128]{2,1,0:T(8,128)S(1)} %copy-done, ...), custom_call_target="tpu_custom_call" | custom-call | flops 10000000 | bytes 4157440 | tf_op jit(solution)/shard_map/pallas_call | solution.py:127
  21.2 1.9 %collective-permute-start.6 = (f32[13,8,128]{2,1,0:T(8,128)S(1)}, f32[13,8,128]{2,1,0:T(8,128)S(1)}, u32[]{:S(2)}, u32[]{:S(2)}) collective-permute-start(f32[13,8,128]{2,1,0:T(8,128)S(1)} %get-tuple-element.41), channel_id=1, source_target_pairs={{1,2},{2,1},{3,4},{4,3},{5,6},{6,5},{7,8},{8,7},{9,10},{10,9},{11,... | collective-permute-start | bytes 159752 | tf_op jit(solution)/shard_map/ppermute | solution.py:641
  23.1 2.1 %collective-permute-start.7 = (f32[13,8,128]{2,1,0:T(8,128)S(1)}, f32[13,8,128]{2,1,0:T(8,128)S(1)}, u32[]{:S(2)}, u32[]{:S(2)}) collective-permute-start(f32[13,8,128]{2,1,0:T(8,128)S(1)} %get-tuple-element.42), channel_id=1, source_target_pairs={{0,1},{1,0},{2,3},{3,2},{4,5},{5,4},{6,7},{7,6},{8,9},{9,8},{10,11... | collective-permute-start | bytes 159752 | tf_op jit(solution)/shard_map/ppermute | solution.py:641
  25.2 1.4 %collective-permute-done.6.a1a = f32[13,8,128]{2,1,0:T(8,128)S(1)} collective-permute-done((f32[13,8,128]{2,1,0:T(8,128)S(1)}, f32[13,8,128]{2,1,0:T(8,128)S(1)}, u32[]{:S(2)}, u32[]{:S(2)}) %collective-permute-start.6) | collective-permute-done | bytes 53280 | tf_op jit(solution)/shard_map/ppermute | solution.py:641
  26.6 0.0 collective-permute-done.7.a1b
  26.7 0.7 collective-permute-start.8
  27.3 3.8 %collective-permute-start.9 = (f32[22,8,128]{2,1,0:T(8,128)S(1)}, f32[22,8,128]{2,1,0:T(8,128)S(1)}, u32[]{:S(2)}, u32[]{:S(2)}) collective-permute-start(f32[22,8,128]{2,1,0:T(8,128)S(1)} %get-tuple-element.46), channel_id=1, source_target_pairs={{0,16},{16,0},{32,48},{48,32},{64,80},{80,64},{96,112},{112,96},{1... | collective-permute-start | bytes 270344 | tf_op jit(solution)/shard_map/ppermute | solution.py:641
  31.1 0.0 collective-permute-done.8.c1a
  31.1 2.8 %collective-permute-done.9.c1b = f32[22,8,128]{2,1,0:T(8,128)S(1)} collective-permute-done((f32[22,8,128]{2,1,0:T(8,128)S(1)}, f32[22,8,128]{2,1,0:T(8,128)S(1)}, u32[]{:S(2)}, u32[]{:S(2)}) %collective-permute-start.9) | collective-permute-done | bytes 90144 | tf_op jit(solution)/shard_map/ppermute | solution.py:641
  33.9 1.0 %shard_map.41 = (f32[16,16,128]{2,1,0:T(8,128)S(1)}, f32[16,16,128]{2,1,0:T(8,128)S(1)}, f32[16,16,128]{2,1,0:T(8,128)S(1)}, f32[16,16,128]{2,1,0:T(8,128)S(1)}, f32[192,128]{1,0:T(8,128)S(1)}) custom-call(f32[16,8,128]{2,1,0:T(8,128)S(1)} %get-tuple-element.43.s2_wide, f32[2,8,128]{2,1,0:T(8,128)S(1)} %get-tuple-element.44.b2_wide, ...), custom_call_target="tpu_custom_call" | custom-call | flops 5000000 | bytes 876544 | tf_op jit(solution)/shard_map/pallas_call | solution.py:127
  35.0 17.3 %all_to_all.16 = f32[96,2,128]{2,1,0:T(2,128)S(1)} all-to-all(f32[96,2,128]{2,1,0:T(2,128)S(1)} %bitcast.7), channel_id=1, replica_groups=mesh['gx'=16,'gy'=16] {'gy'}, dimensions={0} | all-to-all | bytes 196608 | tf_op jit(solution)/shard_map/all_to_all | solution.py:681
  52.3 0.1 shard_map.42
  52.4 21.3 %all_to_all.17 = f32[16,64,128]{2,1,0:T(8,128)S(1)} all-to-all(f32[16,64,128]{2,1,0:T(8,128)S(1)} %bitcast.4), channel_id=1, replica_groups=mesh['gx'=16,'gy'=16] {'gx'}, dimensions={0} | all-to-all | bytes 1048576 | tf_op jit(solution)/shard_map/all_to_all | solution.py:684
  73.6 4.7 %shard_map.43 = f32[16,16,128]{2,1,0:T(8,128)} custom-call(f32[1024,128]{1,0:T(8,128)S(1)} %bitcast.5, f32[16,16,128]{2,1,0:T(8,128)S(1)} %get-tuple-element.48.u0, f32[22,24,128]{2,1,0:T(8,128)S(1)} %get-tuple-element.49.fx0, f32[22,24,128]{2,1,0:T(8,128)S(1)} %get-tuple-element.50.fy0, f32[22,24,128]{2,1,0:T(8,128)S(1)} %get-tuple-element.51.fz0, ...), custom_call_target="tpu_custom_call" | custom-call | flops 10000000 | bytes 3792896 | tf_op jit(solution)/shard_map/pallas_call | solution.py:127
  (7 shorter events, 0.1 us)
Async XLA Ops:
  0.0 1.0 %copy-start.1 = (f32[16,16,128]{2,1,0:T(8,128)S(1)}, f32[16,16,128]{2,1,0:T(8,128)}, u32[]{:S(2)}) copy-start(f32[16,16,128]{2,1,0:T(8,128)} %src.3) | copy-start | bytes 393220
  0.0 1.0 %copy-start.2 = (f32[16,16,128]{2,1,0:T(8,128)S(1)}, f32[16,16,128]{2,1,0:T(8,128)}, u32[]{:S(2)}) copy-start(f32[16,16,128]{2,1,0:T(8,128)} %scr.3) | copy-start | bytes 393220
  1.1 9.3 %collective-permute-start = (f32[28,16,128]{2,1,0:T(8,128)S(1)}, f32[28,16,128]{2,1,0:T(8,128)S(1)}, u32[]{:S(2)}, u32[]{:S(2)}) collective-permute-start(f32[28,16,128]{2,1,0:T(8,128)S(1)} %pad_maximum_fusion), channel_id=1, source_target_pairs={{16,32},{32,16},{48,64},{64,48},{80,96},{96,80},{112,128},{128,112... | collective-permute-start | bytes 688136 | tf_op jit(solution)/shard_map/ppermute | solution.py:641
  1.8 4.5 %copy-start = (f32[16,16,128]{2,1,0:T(8,128)S(1)}, f32[16,16,128]{2,1,0:T(8,128)}, u32[]{:S(2)}) copy-start(f32[16,16,128]{2,1,0:T(8,128)} %eps.3) | copy-start | bytes 393220
  1.8 9.8 %collective-permute-start.1 = (f32[28,16,128]{2,1,0:T(8,128)S(1)}, f32[28,16,128]{2,1,0:T(8,128)S(1)}, u32[]{:S(2)}, u32[]{:S(2)}) collective-permute-start(f32[28,16,128]{2,1,0:T(8,128)S(1)} %pad_maximum_fusion.1), channel_id=1, source_target_pairs={{0,16},{16,0},{32,48},{48,32},{64,80},{80,64},{96,112},{112,96},{1... | collective-permute-start | bytes 688136 | tf_op jit(solution)/shard_map/ppermute | solution.py:641
  6.4 9.3 %collective-permute-start.2 = (f32[60,8,128]{2,1,0:T(8,128)S(1)}, f32[60,8,128]{2,1,0:T(8,128)S(1)}, u32[]{:S(2)}, u32[]{:S(2)}) collective-permute-start(f32[60,8,128]{2,1,0:T(8,128)S(1)} %get-tuple-element.34), channel_id=1, source_target_pairs={{1,2},{2,1},{3,4},{4,3},{5,6},{6,5},{7,8},{8,7},{9,10},{10,9},{11,... | collective-permute-start | bytes 737288 | tf_op jit(solution)/shard_map/ppermute | solution.py:641
  8.3 7.4 %collective-permute-start.3 = (f32[60,8,128]{2,1,0:T(8,128)S(1)}, f32[60,8,128]{2,1,0:T(8,128)S(1)}, u32[]{:S(2)}, u32[]{:S(2)}) collective-permute-start(f32[60,8,128]{2,1,0:T(8,128)S(1)} %get-tuple-element.35), channel_id=1, source_target_pairs={{0,1},{1,0},{2,3},{3,2},{4,5},{5,4},{6,7},{7,6},{8,9},{9,8},{10,11... | collective-permute-start | bytes 737288 | tf_op jit(solution)/shard_map/ppermute | solution.py:641
  11.6 6.3 %collective-permute-start.4 = (f32[33,8,128]{2,1,0:T(8,128)S(1)}, f32[33,8,128]{2,1,0:T(8,128)S(1)}, u32[]{:S(2)}, u32[]{:S(2)}) collective-permute-start(f32[33,8,128]{2,1,0:T(8,128)S(1)} %get-tuple-element.36), channel_id=1, source_target_pairs={{1,2},{2,1},{3,4},{4,3},{5,6},{6,5},{7,8},{8,7},{9,10},{10,9},{11,... | collective-permute-start | bytes 405512 | tf_op jit(solution)/shard_map/ppermute | solution.py:641
  13.6 4.4 %collective-permute-start.5 = (f32[33,8,128]{2,1,0:T(8,128)S(1)}, f32[33,8,128]{2,1,0:T(8,128)S(1)}, u32[]{:S(2)}, u32[]{:S(2)}) collective-permute-start(f32[33,8,128]{2,1,0:T(8,128)S(1)} %get-tuple-element.37), channel_id=1, source_target_pairs={{0,1},{1,0},{2,3},{3,2},{4,5},{5,4},{6,7},{7,6},{8,9},{9,8},{10,11... | collective-permute-start | bytes 405512 | tf_op jit(solution)/shard_map/ppermute | solution.py:641
  21.2 5.5 %collective-permute-start.6 = (f32[13,8,128]{2,1,0:T(8,128)S(1)}, f32[13,8,128]{2,1,0:T(8,128)S(1)}, u32[]{:S(2)}, u32[]{:S(2)}) collective-permute-start(f32[13,8,128]{2,1,0:T(8,128)S(1)} %get-tuple-element.41), channel_id=1, source_target_pairs={{1,2},{2,1},{3,4},{4,3},{5,6},{6,5},{7,8},{8,7},{9,10},{10,9},{11,... | collective-permute-start | bytes 159752 | tf_op jit(solution)/shard_map/ppermute | solution.py:641
  23.1 3.5 %collective-permute-start.7 = (f32[13,8,128]{2,1,0:T(8,128)S(1)}, f32[13,8,128]{2,1,0:T(8,128)S(1)}, u32[]{:S(2)}, u32[]{:S(2)}) collective-permute-start(f32[13,8,128]{2,1,0:T(8,128)S(1)} %get-tuple-element.42), channel_id=1, source_target_pairs={{0,1},{1,0},{2,3},{3,2},{4,5},{5,4},{6,7},{7,6},{8,9},{9,8},{10,11... | collective-permute-start | bytes 159752 | tf_op jit(solution)/shard_map/ppermute | solution.py:641
  26.7 4.4 %collective-permute-start.8 = (f32[22,8,128]{2,1,0:T(8,128)S(1)}, f32[22,8,128]{2,1,0:T(8,128)S(1)}, u32[]{:S(2)}, u32[]{:S(2)}) collective-permute-start(f32[22,8,128]{2,1,0:T(8,128)S(1)} %get-tuple-element.45), channel_id=1, source_target_pairs={{16,32},{32,16},{48,64},{64,48},{80,96},{96,80},{112,128},{128,112... | collective-permute-start | bytes 270344 | tf_op jit(solution)/shard_map/ppermute | solution.py:641
  27.3 6.6 %collective-permute-start.9 = (f32[22,8,128]{2,1,0:T(8,128)S(1)}, f32[22,8,128]{2,1,0:T(8,128)S(1)}, u32[]{:S(2)}, u32[]{:S(2)}) collective-permute-start(f32[22,8,128]{2,1,0:T(8,128)S(1)} %get-tuple-element.46), channel_id=1, source_target_pairs={{0,16},{16,0},{32,48},{48,32},{64,80},{80,64},{96,112},{112,96},{1... | collective-permute-start | bytes 270344 | tf_op jit(solution)/shard_map/ppermute | solution.py:641
